TPU v7x, 32 devices: a whole 2x2x4 slice. The times are simulated.
32 devices in a mesh: member: 2 (over y), lon: 8 (over z, x), lat: 2 (over core).
Axes of the slice: x: 2, y: 2, z: 4, core: 2. Of those that a mesh axis runs over, the one named last changes fastest.
Arguments:
- state: float32 [8, 32, 128, 256], P(('member', 'lat'), 'lon'), parts along dimension 0, may hold values from -4 to 4
- weights: bfloat16 [4, 4, 32, 6, 128, 128], P(None, 'lat', 'lon'), may hold values from -0.21875 to 0.21875
- positions: float32 [3, 4, 32, 128], P(None, 'lat', 'lon'), may hold values from -1 to 1
- stencil_codes: int32 [4, 32, 6], P('lat', 'lon'), may hold values from 0 to 8, as said below
- ovl_owner: int32 [512, 2, 1], P(('lon', 'lat')), may hold values from 0 to 15, as said below
- ovl_local: int32 [512, 2], P(('lon', 'lat')), may hold values from 0 to 7
- interp: bfloat16 [512, 2, 128, 128], P(('lon', 'lat')), may hold values from -0.375 to 0.375
Outputs:
- next_state: float32 [8, 32, 128, 256], P(('member', 'lat'), 'lon'), parts along dimension 0
- ocean: bfloat16 [1024, 128, 256], P(('member', 'lon', 'lat')), parts along dimension 0
There are 2 independent parts, one for each index of `member`. A program takes and returns all parts, laid end to end along the dimension named above; an argument that names none is the same for every part. Nothing has to cross between parts.
Inputs may be any that keep to these rules, and one draw needn't show every extreme that they name: `stencil_codes`: each row tile's codes are distinct, include 4 (the tile itself), and never point outside the latitude range. `ovl_owner`: the owners named in the rows of the device with longitude index l lie in sector (l + 4) mod 8 or the two beside it, in any latitude band; among the rows of one device no owner is named more than 16 times, and the owner in the device's own band and that centre sector exactly 16 times.
All inputs are finite; a program needn't handle non-finite values.
Results may differ from a plain program's by a relative error of at most 0.0051.
Values may be sent and summed in bfloat16 or wider, within the bound.
No kernel may reach another device: no remote copies, remote signals or barrier semaphores. Data moves between devices by JAX's collectives and lax.ppermute only.
A program may use at most 64 MiB of HBM per device.

v0:
```python
import jax
import jax.numpy as jnp
from jax import lax
from jax.sharding import PartitionSpec as P

GRAVITY = 1.0
CORIOLIS = 2.0
STEP_SIZE = 0.2


def extended_2(block, sides, width, periodic):
    for axis, dim in sides:
        count = lax.axis_size(axis)
        forward = [(i, i + 1) for i in range(count - 1)]
        if periodic:
            forward.append((count - 1, 0))
        backward = [(target, source) for source, target in forward]
        low = lax.ppermute(
            lax.slice_in_dim(block, block.shape[dim] - width, None, axis=dim), axis, forward
        )
        high = lax.ppermute(lax.slice_in_dim(block, 0, width, axis=dim), axis, backward)
        block = jnp.concatenate([low, block, high], axis=dim)
    return block


def shifted(value, axis, steps):
    count = lax.axis_size(axis)
    pairs = [(source, (source + steps) % count) for source in range(count)]
    return lax.ppermute(value, axis, pairs)


def tendency_from(current, derivs, positions):
    split_shape = current.shape[:-1] + (4, current.shape[-1] // 4)
    fields = current.reshape(split_shape)
    grads = derivs.reshape((4,) + split_shape)
    coords = [positions[component][..., None] for component in range(3)]
    velocity = [fields[..., component, :] for component in range(3)]
    height = fields[..., 3, :]
    rotation = CORIOLIS * coords[2]
    cross = [
        coords[1] * velocity[2] - coords[2] * velocity[1],
        coords[2] * velocity[0] - coords[0] * velocity[2],
        coords[0] * velocity[1] - coords[1] * velocity[0],
    ]
    forcing = []
    for component in range(3):
        advect = (
            velocity[0] * grads[0][..., component, :]
            + velocity[1] * grads[1][..., component, :]
            + velocity[2] * grads[2][..., component, :]
        )
        forcing.append(
            -advect
            - rotation * cross[component]
            - GRAVITY * grads[component][..., 3, :]
            + grads[3][..., component, :]
        )
    radial = coords[0] * forcing[0] + coords[1] * forcing[1] + coords[2] * forcing[2]
    moment = [forcing[component] - coords[component] * radial for component in range(3)]
    diverge = grads[0][..., 0, :] + grads[1][..., 1, :] + grads[2][..., 2, :]
    height_rate = (
        -(
            velocity[0] * grads[0][..., 3, :]
            + velocity[1] * grads[1][..., 3, :]
            + velocity[2] * grads[2][..., 3, :]
        )
        - height * diverge
        + grads[3][..., 3, :]
    )
    return jnp.stack(moment + [height_rate], axis=-2).reshape(current.shape)


def extend(field):
    widened = extended_2(field, (("lon", 1),), 1, True)
    return extended_2(widened, (("lat", 0),), 1, False)


def widen_sector(tiles, lon_tiles):
    return extended_2(tiles, (("lon", 1),), lon_tiles, True)


def local(state, weights, positions, stencil_codes, ovl_owner, ovl_local, interp):
    lat_tiles, lon_tiles, tile_nodes, features = state.shape
    tile_row = lax.broadcasted_iota(jnp.int32, stencil_codes.shape, 0)
    tile_col = lax.broadcasted_iota(jnp.int32, stencil_codes.shape, 1)
    ext_index = (tile_row + stencil_codes // 3) * (lon_tiles + 2) + tile_col + stencil_codes % 3

    def rate(current):
        rounded = current.astype(jnp.bfloat16)
        extended = extend(rounded).reshape(-1, tile_nodes, features)
        nearby = extended[ext_index]
        derivs = jnp.einsum(
            "qabkij,abkjf->qabif", weights, nearby, preferred_element_type=jnp.float32
        )
        return tendency_from(current, derivs, positions)

    first = rate(state)
    second = rate(state + 0.5 * STEP_SIZE * first)
    third = rate(state + 0.5 * STEP_SIZE * second)
    fourth = rate(state + STEP_SIZE * third)
    next_state = state + STEP_SIZE / 6.0 * (first + 2.0 * second + 2.0 * third + fourth)
    final_tiles = next_state.astype(jnp.bfloat16)
    ocean_dev, intersections = ovl_local.shape
    lon_count = lax.axis_size("lon")
    lat_count = lax.axis_size("lat")
    band_pair = lax.all_gather(final_tiles, "lat", axis=0, tiled=True)
    window = widen_sector(band_pair, lon_tiles)
    source = shifted(window, "lon", lon_count // 2)
    my_lon = lax.axis_index("lon")
    center = (my_lon + lon_count // 2) % lon_count
    owners = ovl_owner.reshape(-1)
    local_ids = ovl_local.reshape(-1)
    owner_lon = owners // lat_count
    owner_lat = owners % lat_count
    relative = (owner_lon - center + 1 + lon_count) % lon_count
    row_index = owner_lat * lat_tiles + local_ids // lon_tiles
    col_index = relative * lon_tiles + local_ids % lon_tiles
    fetched = source[row_index, col_index].reshape(ocean_dev, intersections, tile_nodes, features)
    ocean = jnp.einsum("ojst,ojsf->otf", interp, fetched, preferred_element_type=jnp.float32)
    return (next_state, ocean.astype(jnp.bfloat16))


def solution(mesh):
    placed = (
        P(("member", "lat"), "lon", None, None),
        P(None, "lat", "lon", None, None, None),
        P(None, "lat", "lon", None),
        P("lat", "lon", None),
        P(("lon", "lat"), None, None),
        P(("lon", "lat"), None),
        P(("lon", "lat"), None, None, None),
    )
    return jax.shard_map(
        local,
        mesh=mesh,
        in_specs=placed,
        out_specs=(
            P(("member", "lat"), "lon", None, None),
            P(("member", "lon", "lat"), None, None),
        ),
        check_vma=False,
    )
```

profile of v0, /device:TPU:0, one launch (start us, length us, event | category | flops | bytes accessed | tf_op | source)
XLA Modules:
  0.0 351.5 jit_solution(15057899053271192058)
XLA Ops:
  9.3 2.9 collective-permute-start
  12.3 3.0 collective-permute-start.1
  27.6 3.9 %gather_fusion = bf16[48,128,256]{2,1,0:T(8,128)(2,1)} fusion(bf16[24,128,256]{2,1,0:T(8,128)(2,1)} %bitcast.107, s32[1024]{0:T(1024)S(1)} %pad_clamp_fusion), kind=kCustom, calls=%fused_computation | custom fusion | bytes 6291648 | tf_op jit(solution)/shard_map/gather | solution.py:91
  31.5 5.1 %fusion.8 = f32[4,2,4,128,256]{3,4,0,2,1:T(8,128)S(1)} fusion(bf16[2,4,6,128,256,1]{4,3,2,5,1,0:T(8,128)(2,1)} %bitcast.110, bf16[4,2,4,6,128,128]{5,4,3,2,1,0:T(8,128)(2,1)} %param.8), kind=kOutput, calls=%fused_computation.15 | convolution fusion | flops 1610612736 | bytes 13631488 | tf_op jit(solution)/shard_map/qabkij,abkjf->qabif/dot_general | solution.py:92
  39.8 4.2 %collective-permute-start.5 = (bf16[2,1,128,256]{2,3,1,0:T(8,128)(2,1)S(1)}, bf16[2,1,128,256]{2,3,1,0:T(8,128)(2,1)S(1)}, u32[]{:S(2)}, u32[]{:S(2)}) collective-permute-start(bf16[2,1,128,256]{2,3,1,0:T(8,128)(2,1)S(1)} %get-tuple-element.69), channel_id=1, source_target_pairs={{2,0},{4,2},{6,4},{8,6},{10,8},{12,10},{14,12},{0,14},{3,1},{5,3},... | collective-permute-start | bytes 393224 | tf_op jit(solution)/shard_map/ppermute | solution.py:21
  44.1 3.6 %collective-permute-done.4 = bf16[2,1,128,256]{2,3,1,0:T(8,128)(2,1)S(1)} collective-permute-done((bf16[2,1,128,256]{2,3,1,0:T(8,128)(2,1)S(1)}, bf16[2,1,128,256]{2,3,1,0:T(8,128)(2,1)S(1)}, u32[]{:S(2)}, u32[]{:S(2)}) %collective-permute-start.4) | collective-permute-done | bytes 131104 | tf_op jit(solution)/shard_map/ppermute | solution.py:18
  55.7 4.1 %gather_fusion.1 = bf16[48,128,256]{1,2,0:T(8,128)(2,1)} fusion(bf16[24,128,256]{1,2,0:T(8,128)(2,1)} %bitcast.108, s32[1024]{0:T(1024)S(1)} %pad_clamp_fusion), kind=kCustom, calls=%fused_computation.1 | custom fusion | bytes 6291648 | tf_op jit(solution)/shard_map/gather | solution.py:91
  59.8 4.9 %fusion.11 = f32[4,2,4,128,256]{3,4,0,2,1:T(8,128)S(1)} fusion(bf16[2,4,6,128,256,1]{3,4,2,5,1,0:T(8,128)(2,1)} %bitcast.150, bf16[4,2,4,6,128,128]{5,4,3,2,1,0:T(8,128)(2,1)} %param.8), kind=kOutput, calls=%fused_computation.16 | convolution fusion | flops 1610612736 | bytes 13631488 | tf_op jit(solution)/shard_map/qabkij,abkjf->qabif/dot_general | solution.py:92
  69.2 4.7 %collective-permute-start.9 = (bf16[2,1,128,256]{2,3,1,0:T(8,128)(2,1)S(1)}, bf16[2,1,128,256]{2,3,1,0:T(8,128)(2,1)S(1)}, u32[]{:S(2)}, u32[]{:S(2)}) collective-permute-start(bf16[2,1,128,256]{2,3,1,0:T(8,128)(2,1)S(1)} %get-tuple-element.67), channel_id=1, source_target_pairs={{2,0},{4,2},{6,4},{8,6},{10,8},{12,10},{14,12},{0,14},{3,1},{5,3},... | collective-permute-start | bytes 393224 | tf_op jit(solution)/shard_map/ppermute | solution.py:21
  73.9 3.6 %collective-permute-done.8 = bf16[2,1,128,256]{2,3,1,0:T(8,128)(2,1)S(1)} collective-permute-done((bf16[2,1,128,256]{2,3,1,0:T(8,128)(2,1)S(1)}, bf16[2,1,128,256]{2,3,1,0:T(8,128)(2,1)S(1)}, u32[]{:S(2)}, u32[]{:S(2)}) %collective-permute-start.8) | collective-permute-done | bytes 131104 | tf_op jit(solution)/shard_map/ppermute | solution.py:18
  85.5 4.1 %gather_fusion.2 = bf16[48,128,256]{1,2,0:T(8,128)(2,1)} fusion(bf16[24,128,256]{1,2,0:T(8,128)(2,1)} %bitcast.109, s32[1024]{0:T(1024)S(1)} %pad_clamp_fusion), kind=kCustom, calls=%fused_computation.2 | custom fusion | bytes 6291648 | tf_op jit(solution)/shard_map/gather | solution.py:91
  89.6 4.9 %fusion.14 = f32[4,2,4,128,256]{3,4,0,2,1:T(8,128)S(1)} fusion(bf16[2,4,6,128,256,1]{3,4,2,5,1,0:T(8,128)(2,1)} %bitcast.151, bf16[4,2,4,6,128,128]{5,4,3,2,1,0:T(8,128)(2,1)} %param.8), kind=kOutput, calls=%fused_computation.17 | convolution fusion | flops 1610612736 | bytes 13631488 | tf_op jit(solution)/shard_map/qabkij,abkjf->qabif/dot_general | solution.py:92
  99.0 4.7 %collective-permute-start.13 = (bf16[2,1,128,256]{2,3,1,0:T(8,128)(2,1)S(1)}, bf16[2,1,128,256]{2,3,1,0:T(8,128)(2,1)S(1)}, u32[]{:S(2)}, u32[]{:S(2)}) collective-permute-start(bf16[2,1,128,256]{2,3,1,0:T(8,128)(2,1)S(1)} %get-tuple-element.65), channel_id=1, source_target_pairs={{2,0},{4,2},{6,4},{8,6},{10,8},{12,10},{14,12},{0,14},{3,1},{5,3},... | collective-permute-start | bytes 393224 | tf_op jit(solution)/shard_map/ppermute | solution.py:21
  103.7 3.6 %collective-permute-done.12 = bf16[2,1,128,256]{2,3,1,0:T(8,128)(2,1)S(1)} collective-permute-done((bf16[2,1,128,256]{2,3,1,0:T(8,128)(2,1)S(1)}, bf16[2,1,128,256]{2,3,1,0:T(8,128)(2,1)S(1)}, u32[]{:S(2)}, u32[]{:S(2)}) %collective-permute-start.12) | collective-permute-done | bytes 131104 | tf_op jit(solution)/shard_map/ppermute | solution.py:18
  115.3 4.1 %gather_fusion.3 = bf16[48,128,256]{1,2,0:T(8,128)(2,1)} fusion(bf16[24,128,256]{1,2,0:T(8,128)(2,1)} %bitcast.106, s32[1024]{0:T(1024)S(1)} %pad_clamp_fusion), kind=kCustom, calls=%fused_computation.3 | custom fusion | bytes 6291648 | tf_op jit(solution)/shard_map/gather | solution.py:91
  119.4 4.9 %fusion.17 = f32[4,2,4,128,256]{3,4,0,2,1:T(8,128)S(1)} fusion(bf16[2,4,6,128,256,1]{3,4,2,5,1,0:T(8,128)(2,1)} %bitcast.149, bf16[4,2,4,6,128,128]{5,4,3,2,1,0:T(8,128)(2,1)} %param.8), kind=kOutput, calls=%fused_computation.18 | convolution fusion | flops 1610612736 | bytes 13631488 | tf_op jit(solution)/shard_map/qabkij,abkjf->qabif/dot_general | solution.py:92
  131.9 8.7 %all-gather.2.cloned.1.call-done = bf16[4,4,128,256]{3,2,1,0:T(8,128)(2,1)} async-done(((bf16[2,4,128,256]{3,2,1,0:T(8,128)(2,1)}), bf16[4,4,128,256]{3,2,1,0:T(8,128)(2,1)}) %all-gather.2.cloned.1.call-update) | async-done | bytes 1048592 | tf_op jit(solution)/shard_map/all_gather | solution.py:106
  142.3 3.0 collective-permute-start.17
  145.3 42.7 %collective-permute-done.16 = bf16[4,4,128,256]{3,2,1,0:T(8,128)(2,1)S(1)} collective-permute-done((bf16[4,4,128,256]{3,2,1,0:T(8,128)(2,1)}, bf16[4,4,128,256]{3,2,1,0:T(8,128)(2,1)S(1)}, u32[]{:S(2)}, u32[]{:S(2)}) %collective-permute-start.16) | collective-permute-done | bytes 1048608 | tf_op jit(solution)/shard_map/ppermute | solution.py:18
  190.1 2.8 pad_maximum_fusion
  196.8 134.3 %collective-permute-done.18 = bf16[4,12,128,256]{3,2,1,0:T(8,128)(2,1)} collective-permute-done((bf16[4,12,128,256]{3,2,1,0:T(8,128)(2,1)}, bf16[4,12,128,256]{3,2,1,0:T(8,128)(2,1)}, u32[]{:S(2)}, u32[]{:S(2)}) %collective-permute-start.18) | collective-permute-done | bytes 3145760 | tf_op jit(solution)/shard_map/ppermute | solution.py:29
  331.0 4.7 %gather_fusion.4 = bf16[64,128,256]{2,1,0:T(8,128)(2,1)} fusion(bf16[4,12,128,256]{3,2,1,0:T(8,128)(2,1)} %collective-permute-done.18, s32[64]{0:T(128)S(1)} %fusion.102), kind=kCustom, calls=%fused_computation.4 | custom fusion | bytes 8389120 | tf_op jit(solution)/shard_map/gather | solution.py:118
  335.7 4.9 %fusion.20 = bf16[32,128,256]{1,2,0:T(8,128)(2,1)} fusion(bf16[32,2,128,256]{3,2,1,0:T(8,128)(2,1)} %bitcast.105, bf16[32,2,128,128]{3,2,1,0:T(8,128)(2,1)S(1)} %copy-done), kind=kOutput, calls=%fused_computation.19 | convolution fusion | flops 537919488 | bytes 8388608 | tf_op jit(solution)/shard_map/ojst,ojsf->otf/dot_general | solution.py:119
  340.6 4.1 %copy.70 = bf16[32,128,256]{2,1,0:T(8,128)(2,1)} copy(bf16[32,128,256]{1,2,0:T(8,128)(2,1)} %fusion.20) | data formatting | bytes 4194304
  (146 shorter events, 65.3 us)
Async XLA Ops:
  7.2 328.6 %copy-start = (bf16[32,2,128,128]{3,2,1,0:T(8,128)(2,1)S(1)}, bf16[32,2,128,128]{3,2,1,0:T(8,128)(2,1)}, u32[]{:S(2)}) copy-start(bf16[32,2,128,128]{3,2,1,0:T(8,128)(2,1)} %param.13) | copy-start | bytes 6291460
  7.2 133.4 %all-gather.2.cloned.1.call-start = ((), (), s32[]{:S(2)}) async-start(), calls=%async_computation | async-start | bytes 1572864 | tf_op jit(solution)/shard_map/all_gather | solution.py:106
  9.3 9.8 %collective-permute-start = (bf16[2,1,128,256]{3,2,1,0:T(8,128)(2,1)}, bf16[2,1,128,256]{3,2,1,0:T(8,128)(2,1)S(1)}, u32[]{:S(2)}, u32[]{:S(2)}) collective-permute-start(bf16[2,1,128,256]{3,2,1,0:T(8,128)(2,1)} %get-tuple-element.70), channel_id=1, source_target_pairs={{0,2},{2,4},{4,6},{6,8},{8,10},{10,12},{12,14},{14,0},{1,3},{3,5},... | collective-permute-start | bytes 393224 | tf_op jit(solution)/shard_map/ppermute | solution.py:18
  12.3 7.8 %collective-permute-start.1 = (bf16[2,1,128,256]{3,2,1,0:T(8,128)(2,1)S(1)}, bf16[2,1,128,256]{3,2,1,0:T(8,128)(2,1)S(1)}, u32[]{:S(2)}, u32[]{:S(2)}) collective-permute-start(bf16[2,1,128,256]{3,2,1,0:T(8,128)(2,1)S(1)} %get-tuple-element.71), channel_id=1, source_target_pairs={{2,0},{4,2},{6,4},{8,6},{10,8},{12,10},{14,12},{0,14},{3,1},{5,3},... | collective-permute-start | bytes 393224 | tf_op jit(solution)/shard_map/ppermute | solution.py:21
  21.3 2.7 collective-permute-start.2
  22.6 3.6 %collective-permute-start.3 = (bf16[1,6,128,256]{3,2,1,0:T(8,128)(2,1)S(1)}, bf16[1,6,128,256]{3,2,1,0:T(8,128)(2,1)S(1)}, u32[]{:S(2)}, u32[]{:S(2)}) collective-permute-start(bf16[1,6,128,256]{3,2,1,0:T(8,128)(2,1)S(1)} %get-tuple-element.63), channel_id=1, source_target_pairs={{1,0},{3,2},{5,4},{7,6},{9,8},{11,10},{13,12},{15,14},{17,16},{19,... | collective-permute-start | bytes 1179656 | tf_op jit(solution)/shard_map/ppermute | solution.py:21
  39.3 8.4 %collective-permute-start.4 = (bf16[2,1,128,256]{2,3,1,0:T(8,128)(2,1)S(1)}, bf16[2,1,128,256]{2,3,1,0:T(8,128)(2,1)S(1)}, u32[]{:S(2)}, u32[]{:S(2)}) collective-permute-start(bf16[2,1,128,256]{2,3,1,0:T(8,128)(2,1)S(1)} %get-tuple-element.68), channel_id=1, source_target_pairs={{0,2},{2,4},{4,6},{6,8},{8,10},{10,12},{12,14},{14,0},{1,3},{3,5},... | collective-permute-start | bytes 393224 | tf_op jit(solution)/shard_map/ppermute | solution.py:18
  39.8 9.4 %collective-permute-start.5 = (bf16[2,1,128,256]{2,3,1,0:T(8,128)(2,1)S(1)}, bf16[2,1,128,256]{2,3,1,0:T(8,128)(2,1)S(1)}, u32[]{:S(2)}, u32[]{:S(2)}) collective-permute-start(bf16[2,1,128,256]{2,3,1,0:T(8,128)(2,1)S(1)} %get-tuple-element.69), channel_id=1, source_target_pairs={{2,0},{4,2},{6,4},{8,6},{10,8},{12,10},{14,12},{0,14},{3,1},{5,3},... | collective-permute-start | bytes 393224 | tf_op jit(solution)/shard_map/ppermute | solution.py:21
  49.4 2.6 collective-permute-start.6
  50.7 3.6 %collective-permute-start.7 = (bf16[1,6,128,256]{2,3,1,0:T(8,128)(2,1)S(1)}, bf16[1,6,128,256]{2,3,1,0:T(8,128)(2,1)S(1)}, u32[]{:S(2)}, u32[]{:S(2)}) collective-permute-start(bf16[1,6,128,256]{2,3,1,0:T(8,128)(2,1)S(1)} %get-tuple-element.61), channel_id=1, source_target_pairs={{1,0},{3,2},{5,4},{7,6},{9,8},{11,10},{13,12},{15,14},{17,16},{19,... | collective-permute-start | bytes 1179656 | tf_op jit(solution)/shard_map/ppermute | solution.py:21
  69.1 8.4 %collective-permute-start.8 = (bf16[2,1,128,256]{2,3,1,0:T(8,128)(2,1)S(1)}, bf16[2,1,128,256]{2,3,1,0:T(8,128)(2,1)S(1)}, u32[]{:S(2)}, u32[]{:S(2)}) collective-permute-start(bf16[2,1,128,256]{2,3,1,0:T(8,128)(2,1)S(1)} %get-tuple-element.66), channel_id=1, source_target_pairs={{0,2},{2,4},{4,6},{6,8},{8,10},{10,12},{12,14},{14,0},{1,3},{3,5},... | collective-permute-start | bytes 393224 | tf_op jit(solution)/shard_map/ppermute | solution.py:18
  69.2 9.9 %collective-permute-start.9 = (bf16[2,1,128,256]{2,3,1,0:T(8,128)(2,1)S(1)}, bf16[2,1,128,256]{2,3,1,0:T(8,128)(2,1)S(1)}, u32[]{:S(2)}, u32[]{:S(2)}) collective-permute-start(bf16[2,1,128,256]{2,3,1,0:T(8,128)(2,1)S(1)} %get-tuple-element.67), channel_id=1, source_target_pairs={{2,0},{4,2},{6,4},{8,6},{10,8},{12,10},{14,12},{0,14},{3,1},{5,3},... | collective-permute-start | bytes 393224 | tf_op jit(solution)/shard_map/ppermute | solution.py:21
  79.2 2.8 collective-permute-start.10
  80.5 3.6 %collective-permute-start.11 = (bf16[1,6,128,256]{2,3,1,0:T(8,128)(2,1)S(1)}, bf16[1,6,128,256]{2,3,1,0:T(8,128)(2,1)S(1)}, u32[]{:S(2)}, u32[]{:S(2)}) collective-permute-start(bf16[1,6,128,256]{2,3,1,0:T(8,128)(2,1)S(1)} %get-tuple-element.59), channel_id=1, source_target_pairs={{1,0},{3,2},{5,4},{7,6},{9,8},{11,10},{13,12},{15,14},{17,16},{19,... | collective-permute-start | bytes 1179656 | tf_op jit(solution)/shard_map/ppermute | solution.py:21
  98.9 8.4 %collective-permute-start.12 = (bf16[2,1,128,256]{2,3,1,0:T(8,128)(2,1)S(1)}, bf16[2,1,128,256]{2,3,1,0:T(8,128)(2,1)S(1)}, u32[]{:S(2)}, u32[]{:S(2)}) collective-permute-start(bf16[2,1,128,256]{2,3,1,0:T(8,128)(2,1)S(1)} %get-tuple-element.64), channel_id=1, source_target_pairs={{0,2},{2,4},{4,6},{6,8},{8,10},{10,12},{12,14},{14,0},{1,3},{3,5},... | collective-permute-start | bytes 393224 | tf_op jit(solution)/shard_map/ppermute | solution.py:18
  99.0 9.9 %collective-permute-start.13 = (bf16[2,1,128,256]{2,3,1,0:T(8,128)(2,1)S(1)}, bf16[2,1,128,256]{2,3,1,0:T(8,128)(2,1)S(1)}, u32[]{:S(2)}, u32[]{:S(2)}) collective-permute-start(bf16[2,1,128,256]{2,3,1,0:T(8,128)(2,1)S(1)} %get-tuple-element.65), channel_id=1, source_target_pairs={{2,0},{4,2},{6,4},{8,6},{10,8},{12,10},{14,12},{0,14},{3,1},{5,3},... | collective-permute-start | bytes 393224 | tf_op jit(solution)/shard_map/ppermute | solution.py:21
  109.0 2.6 collective-permute-start.14
  110.3 3.6 %collective-permute-start.15 = (bf16[1,6,128,256]{2,3,1,0:T(8,128)(2,1)S(1)}, bf16[1,6,128,256]{2,3,1,0:T(8,128)(2,1)S(1)}, u32[]{:S(2)}, u32[]{:S(2)}) collective-permute-start(bf16[1,6,128,256]{2,3,1,0:T(8,128)(2,1)S(1)} %get-tuple-element.57), channel_id=1, source_target_pairs={{1,0},{3,2},{5,4},{7,6},{9,8},{11,10},{13,12},{15,14},{17,16},{19,... | collective-permute-start | bytes 1179656 | tf_op jit(solution)/shard_map/ppermute | solution.py:21
  131.9 63.2 %copy-start.30 = (s32[32,2,1]{0,2,1:T(1,128)S(1)}, s32[32,2,1]{0,2,1:T(1,128)}, u32[]{:S(2)}) copy-start(s32[32,2,1]{0,2,1:T(1,128)} %param.11) | copy-start | bytes 772
  131.9 63.3 %copy-start.31 = (s32[32,2]{0,1:T(2,128)S(1)}, s32[32,2]{0,1:T(2,128)}, u32[]{:S(2)}) copy-start(s32[32,2]{0,1:T(2,128)} %param.12) | copy-start | bytes 772
  131.9 63.6 %copy-start.6 = (f32[2,4,128,256]{2,3,1,0:T(8,128)S(1)}, f32[2,4,128,256]{2,3,1,0:T(8,128)}, u32[]{:S(2)}) copy-start(f32[2,4,128,256]{2,3,1,0:T(8,128)} %get-tuple-element.9) | copy-start | bytes 3145732
  140.6 47.4 %collective-permute-start.16 = (bf16[4,4,128,256]{3,2,1,0:T(8,128)(2,1)}, bf16[4,4,128,256]{3,2,1,0:T(8,128)(2,1)S(1)}, u32[]{:S(2)}, u32[]{:S(2)}) collective-permute-start(bf16[4,4,128,256]{3,2,1,0:T(8,128)(2,1)} %all-gather.2.cloned.1.call-done), channel_id=1, source_target_pairs={{0,2},{2,4},{4,6},{6,8},{8,10},{10,12},{12,14},{14,0},{1,3},{3,5},... | collective-permute-start | bytes 3145736 | tf_op jit(solution)/shard_map/ppermute | solution.py:18
  142.3 47.8 %collective-permute-start.17 = (bf16[4,4,128,256]{3,2,1,0:T(8,128)(2,1)}, bf16[4,4,128,256]{3,2,1,0:T(8,128)(2,1)S(1)}, u32[]{:S(2)}, u32[]{:S(2)}) collective-permute-start(bf16[4,4,128,256]{3,2,1,0:T(8,128)(2,1)} %all-gather.2.cloned.1.call-done), channel_id=1, source_target_pairs={{2,0},{4,2},{6,4},{8,6},{10,8},{12,10},{14,12},{0,14},{3,1},{5,3},... | collective-permute-start | bytes 3145736 | tf_op jit(solution)/shard_map/ppermute | solution.py:21
  192.9 138.1 %collective-permute-start.18 = (bf16[4,12,128,256]{3,2,1,0:T(8,128)(2,1)}, bf16[4,12,128,256]{3,2,1,0:T(8,128)(2,1)}, u32[]{:S(2)}, u32[]{:S(2)}) collective-permute-start(bf16[4,12,128,256]{3,2,1,0:T(8,128)(2,1)} %pad_maximum_fusion), channel_id=1, source_target_pairs={{0,8},{2,10},{4,12},{6,14},{8,0},{10,2},{12,4},{14,6},{1,9},{3,11}... | collective-permute-start | bytes 9437192 | tf_op jit(solution)/shard_map/ppermute | solution.py:29
  (28 other events, 59.2 us)
Sparse Core Ops, SparseCore 0:
  132.0 8.5 all-gather.1
where the time goes:
time: 352 us
  waiting for transfers between devices  213 us (61%)
  local copies, waits for them, and re-layouts  38.8 us (11%)
  starting transfers between devices  37.8 us (11%)
  matrix products  24.7 us (7%)
  other arithmetic  22.3 us (6%)
  between operations  14.7 us (4%)
    ppermute x1, waiting for transfers between devices, shifted(): return lax.ppermute(value, axis, pairs)  134 us
    ppermute x9, waiting for transfers between devices, extended_2(): lax.ppermute(lax.slice_in_dim(block, block.shape[dim] - width, None, axis...  53.7 us
    ppermute x9, starting transfers between devices, extended_2(): lax.ppermute(lax.slice_in_dim(block, 0, width, axis=dim), axis, backward)  25 us
    dot_general x4, matrix products, rate(): jnp.einsum('qabkij,abkjf->qabif', weights, nearby, preferred_element_type...  19.8 us
    ppermute x9, waiting for transfers between devices, extended_2(): lax.ppermute(lax.slice_in_dim(block, 0, width, axis=dim), axis, backward)  16.7 us
    gather x4, local copies, waits for them, and re-layouts, rate(): nearby = extended[ext_index]  16.2 us
    unnamed x69, local copies, waits for them, and re-layouts  12.9 us
    ppermute x9, starting transfers between devices, extended_2(): lax.ppermute(lax.slice_in_dim(block, block.shape[dim] - width, None, axis...  10.6 us
  transfers between devices with their start and end apart: 20, of which 16 were waited for; matrix products, arithmetic and copies ran while one was open for 2% of the time, Pallas kernels for 0%

commit v1 on v0

v1 whole, which is shorter than its diff:
```python
import functools

import jax
import jax.numpy as jnp
from jax import lax
from jax.experimental import pallas as pl
from jax.experimental.pallas import tpu as pltpu
from jax.sharding import PartitionSpec as P

CORIOLIS = 2.0
STEP_SIZE = 0.2
BF16 = jnp.bfloat16
F32 = jnp.float32
ANY = pl.BlockSpec(memory_space=pl.ANY)
VMEM = pl.BlockSpec(memory_space=pltpu.VMEM)
SMEM = pl.BlockSpec(memory_space=pltpu.SMEM)
LIMIT = 48 * 1024 * 1024


def in_vmem(value):
    return pltpu.with_memory_space_constraint(value, pltpu.VMEM)


def prep_kernel(send_ref, state_ref, pos_ref, own_ref, west_ref, east_ref, row_ref, coef_ref):
    rows, cols = state_ref.shape[:2]
    for a in range(rows):
        for b in range(cols):
            tile = state_ref[a, b].astype(BF16)
            own_ref[a, b] = tile
            if b == 0:
                west_ref[a, 0] = tile
            if b == cols - 1:
                east_ref[a, 0] = tile

            @pl.when(send_ref[0] == a)
            def _():
                row_ref[0, b] = tile

    nodes = pos_ref.shape[-1]
    low = lax.broadcasted_iota(jnp.int32, (nodes, nodes), 1) < nodes // 2
    for a in range(rows):
        for b in range(cols):
            x0, x1, x2 = (
                jnp.broadcast_to(pos_ref[c, a, b][None, :], (nodes, nodes)).T for c in range(3)
            )
            spin = CORIOLIS * x2
            coef_ref[a, b, 0] = jnp.where(low, x0, x1)
            coef_ref[a, b, 1] = jnp.where(low, x2, 0.0)
            coef_ref[a, b, 2] = spin * jnp.where(low, x1, -x0)
            coef_ref[a, b, 3] = spin * jnp.where(low, -x2, x2)
            coef_ref[a, b, 4] = jnp.where(low, spin * x0, 0.0)
            coef_ref[a, b, 5] = jnp.where(low, spin * x1, 0.0)


def turned(value):
    return pltpu.roll(value, value.shape[-1] // 2, axis=1)


def tendency(tile, grads, coef, low):
    half = tile.shape[-1] // 2
    sa, sb = tile[:, :half], tile[:, half:]
    ra, rb = turned(sa), turned(sb)
    v0 = jnp.where(low, sa, ra)
    v1 = jnp.where(low, ra, sa)
    v2 = jnp.where(low, sb, rb)
    ga = [g[:, :half] for g in grads]
    gb = [g[:, half:] for g in grads]
    t0a, t0b, t2b = turned(ga[0]), turned(gb[0]), turned(gb[2])
    fa = (
        ga[3]
        - (v0 * ga[0] + v1 * ga[1] + v2 * ga[2])
        - (coef[2] * v2 + coef[3] * ra)
        - jnp.where(low, t0b, gb[1])
    )
    spread = sb * (t0a + ga[1] + t2b)
    fb = (
        gb[3]
        - (v0 * gb[0] + v1 * gb[1] + v2 * gb[2])
        - (coef[4] * v1 - coef[5] * v0)
        - jnp.where(low, t2b, spread)
    )
    part = coef[0] * fa + coef[1] * fb
    radial = part + turned(part)
    return fa - coef[0] * radial, fb - coef[1] * radial


def stage_kernel(last, scale, index_ref, send_ref, w_ref, coef_ref, *refs):
    if last:
        (state_ref, second_ref, third_ref, now_ref, own_ref, west_ref, east_ref, other_ref,
         cwest_ref, ceast_ref, next_ref, bown_ref, ext, sems) = refs
    else:
        (state_ref, now_ref, own_ref, west_ref, east_ref, other_ref,
         cwest_ref, ceast_ref, next_ref, bown_ref, bwest_ref, beast_ref, brow_ref, ext, sems) = refs
    rows, cols, nodes, feats = state_ref.shape
    mine = 1 - send_ref[0]
    copies = [
        pltpu.make_async_copy(own_ref, ext.at[0:rows, 1 : cols + 1], sems.at[0]),
        pltpu.make_async_copy(west_ref, ext.at[0:rows, 0:1], sems.at[1]),
        pltpu.make_async_copy(east_ref, ext.at[0:rows, cols + 1 : cols + 2], sems.at[2]),
        pltpu.make_async_copy(other_ref, ext.at[rows : rows + 1, 1 : cols + 1], sems.at[3]),
        pltpu.make_async_copy(
            cwest_ref.at[pl.ds(mine, 1)], ext.at[rows : rows + 1, 0:1], sems.at[4]
        ),
        pltpu.make_async_copy(
            ceast_ref.at[pl.ds(mine, 1)], ext.at[rows : rows + 1, cols + 1 : cols + 2], sems.at[5]
        ),
    ]
    for copy in copies:
        copy.start()
    for copy in copies:
        copy.wait()
    low = lax.broadcasted_iota(jnp.int32, (nodes, feats // 2), 1) < feats // 4
    half = feats // 2
    taps = w_ref.shape[3]
    for a in range(rows):
        for b in range(cols):
            where = [index_ref[a, b, k] for k in range(taps)]
            near = jnp.concatenate(
                [ext[w // (cols + 2), w % (cols + 2)] for w in where], axis=0
            )
            weights = jnp.concatenate(
                [
                    jnp.concatenate([w_ref[q, a, b, k] for k in range(taps)], axis=1)
                    for q in range(4)
                ],
                axis=0,
            )
            derivs = jnp.dot(weights, near, preferred_element_type=F32)
            grads = [derivs[q * nodes : (q + 1) * nodes] for q in range(4)]
            coef = [coef_ref[a, b, i] for i in range(6)]
            ka, kb = tendency(now_ref[a, b], grads, coef, low)
            rate = jnp.concatenate([ka, kb], axis=1)
            if last:
                third = 1.0 / 3.0
                out = (
                    third * (second_ref[a, b] + 2.0 * third_ref[a, b] + now_ref[a, b] - state_ref[a, b])
                    + scale * rate
                )
            else:
                out = state_ref[a, b] + scale * rate
            next_ref[a, b] = out
            rounded = out.astype(BF16)
            bown_ref[a, b] = rounded
            if not last:
                if b == 0:
                    bwest_ref[a, 0] = rounded
                if b == cols - 1:
                    beast_ref[a, 0] = rounded

                @pl.when(send_ref[0] == a)
                def _():
                    brow_ref[0, b] = rounded


def turn_kernel(interp_ref, out_ref):
    tiles, taps, nodes, points = interp_ref.shape
    for o in range(tiles):
        out_ref[o] = interp_ref[o].reshape(taps * nodes, points).T


def ocean_kernel(slot_ref, ends_ref, interp_ref, *refs):
    *sources, nat_ref, other_nat_ref, out_ref, tiles, sems = refs
    count = sources[0].shape[0]

    def copy(source, place):
        return pltpu.make_async_copy(source, tiles.at[place], sems.at[place])

    plain = (ends_ref[0] == 0, None, ends_ref[1] == 0)

    @pl.when(pl.program_id(0) == 0)
    def _():
        for place in range(6):
            use = plain[place // 2]
            if use is None:
                copy(sources[place], place).start()
            else:
                nat = (nat_ref, other_nat_ref)[place % 2]

                @pl.when(use)
                def _():
                    copy(sources[place], place).start()

                @pl.when(jnp.logical_not(use))
                def _():
                    copy(nat, place).start()

        for place in range(6):
            copy(sources[place], place).wait()

    block, taps = interp_ref.shape[0], slot_ref.shape[1]
    base = pl.program_id(0) * block
    for o in range(block):
        where = [slot_ref[base + o, j] for j in range(taps)]
        near = jnp.concatenate([tiles[w // count, w % count] for w in where], axis=0)
        out_ref[o] = jnp.dot(interp_ref[o], near, preferred_element_type=F32).astype(BF16)


def local(state, weights, positions, stencil_codes, ovl_owner, ovl_local, interp):
    rows, cols, nodes, feats = state.shape
    taps = stencil_codes.shape[-1]
    lon_count = lax.axis_size("lon")
    lat_count = lax.axis_size("lat")
    my_lon = lax.axis_index("lon")
    my_lat = lax.axis_index("lat")
    forward = [(i, (i + 1) % lon_count) for i in range(lon_count)]
    backward = [(target, source) for source, target in forward]
    swap = [(i, lat_count - 1 - i) for i in range(lat_count)]
    params = pltpu.CompilerParams(vmem_limit_bytes=LIMIT)

    tile_row = lax.broadcasted_iota(jnp.int32, stencil_codes.shape, 0)
    tile_col = lax.broadcasted_iota(jnp.int32, stencil_codes.shape, 1)
    ext_row = tile_row + stencil_codes // 3 - 1
    ext_row = jnp.where(ext_row < 0, rows, ext_row)
    index = ext_row * (cols + 2) + tile_col + stencil_codes % 3
    send = (1 - my_lat).astype(jnp.int32).reshape(1)

    col_shape = (rows, 1, nodes, feats)
    row_shape = (1, cols, nodes, feats)
    bf_shapes = [
        jax.ShapeDtypeStruct((rows, cols, nodes, feats), BF16),
        jax.ShapeDtypeStruct(col_shape, BF16),
        jax.ShapeDtypeStruct(col_shape, BF16),
        jax.ShapeDtypeStruct(row_shape, BF16),
    ]
    own, west, east, row, coef = pl.pallas_call(
        prep_kernel,
        out_shape=bf_shapes + [jax.ShapeDtypeStruct((rows, cols, 6, nodes, nodes), F32)],
        in_specs=[SMEM, VMEM, VMEM],
        out_specs=[VMEM] * 5,
        compiler_params=params,
        name="prep",
    )(send, state, positions)

    def halo(west, east, row):
        from_west = lax.ppermute(east, "lon", forward)
        from_east = lax.ppermute(west, "lon", backward)
        other = lax.ppermute(row, "lat", swap)
        corner_west = lax.ppermute(from_west, "lat", swap)
        corner_east = lax.ppermute(from_east, "lat", swap)
        return from_west, from_east, other, corner_west, corner_east

    flops = 2 * 4 * rows * cols * taps * nodes * nodes * feats

    def stage(scale, fields, own, edges, last=False):
        outs = [pltpu.VMEM((rows, cols, nodes, feats), F32)] if False else [
            jax.ShapeDtypeStruct((rows, cols, nodes, feats), F32)
        ]
        outs = outs + (bf_shapes[:1] if last else bf_shapes)
        return pl.pallas_call(
            functools.partial(stage_kernel, last, scale),
            out_shape=outs,
            in_specs=[SMEM, SMEM, VMEM, VMEM] + [VMEM] * len(fields) + [ANY] * 6,
            out_specs=[VMEM] * len(outs),
            scratch_shapes=[
                pltpu.VMEM((rows + 1, cols + 2, nodes, feats), BF16),
                pltpu.SemaphoreType.DMA((6,)),
            ],
            compiler_params=params,
            cost_estimate=pl.CostEstimate(flops=flops, bytes_accessed=8 << 20, transcendentals=0),
            name="last_stage" if last else "stage",
        )(index, send, weights, coef, *fields, own, *edges)

    second, own, west2, east2, row2 = stage(
        0.5 * STEP_SIZE, [state, state], own, halo(west, east, row)
    )
    third, own, west3, east3, row3 = stage(
        0.5 * STEP_SIZE, [state, second], own, halo(west2, east2, row2)
    )
    fourth, own, west4, east4, row4 = stage(
        STEP_SIZE, [state, third], own, halo(west3, east3, row3)
    )
    next_state, final = stage(
        STEP_SIZE / 6.0, [state, second, third, fourth], own, halo(west4, east4, row4), last=True
    )

    ocean_dev, intersections = ovl_local.shape
    turned_interp = pl.pallas_call(
        turn_kernel,
        out_shape=jax.ShapeDtypeStruct((ocean_dev, nodes, intersections * nodes), BF16),
        in_specs=[VMEM],
        out_specs=VMEM,
        compiler_params=params,
        name="turn_interp",
    )(interp)

    final = final.reshape(rows * cols, nodes, feats)
    half = lon_count // 2
    opposite = [(i, (i + half) % lon_count) for i in range(lon_count)]
    seam = (half - 1, lon_count - 1)
    ends = [(0, half - 1), (half - 1, 0), (half, lon_count - 1), (lon_count - 1, half)]
    up = [pair for pair in forward if pair[0] not in seam]
    down = [pair for pair in backward if pair[1] not in seam]
    native = lax.ppermute(final, "lon", ends)
    center = lax.ppermute(final, "lon", opposite)
    below = lax.ppermute(center, "lon", up)
    above = lax.ppermute(center, "lon", down)
    sources = []
    for piece in (below, center, above):
        sources += [piece, lax.ppermute(piece, "lat", swap)]
    other_native = lax.ppermute(native, "lat", swap)

    middle = (my_lon + half) % lon_count
    owners = ovl_owner.reshape(ocean_dev, intersections)
    relative = (owners // lat_count - middle + 1 + lon_count) % lon_count
    away = (owners % lat_count != my_lat).astype(jnp.int32)
    slot = (relative * 2 + away) * (rows * cols) + ovl_local
    in_half = my_lon % half
    ends_at = jnp.stack([in_half == 0, in_half == half - 1]).astype(jnp.int32)
    block = 8
    ocean = pl.pallas_call(
        ocean_kernel,
        grid=(ocean_dev // block,),
        out_shape=jax.ShapeDtypeStruct((ocean_dev, nodes, feats), BF16),
        in_specs=[SMEM, SMEM, pl.BlockSpec((block, nodes, intersections * nodes), lambda g: (g, 0, 0))]
        + [ANY] * 8,
        out_specs=pl.BlockSpec((block, nodes, feats), lambda g: (g, 0, 0)),
        scratch_shapes=[
            pltpu.VMEM((6, rows * cols, nodes, feats), BF16),
            pltpu.SemaphoreType.DMA((6,)),
        ],
        compiler_params=params,
        name="ocean",
    )(slot, ends_at, turned_interp, *sources, native, other_native)
    return next_state, ocean


def solution(mesh):
    placed = (
        P(("member", "lat"), "lon", None, None),
        P(None, "lat", "lon", None, None, None),
        P(None, "lat", "lon", None),
        P("lat", "lon", None),
        P(("lon", "lat"), None, None),
        P(("lon", "lat"), None),
        P(("lon", "lat"), None, None, None),
    )
    return jax.shard_map(
        local,
        mesh=mesh,
        in_specs=placed,
        out_specs=(
            P(("member", "lat"), "lon", None, None),
            P(("member", "lon", "lat"), None, None),
        ),
        check_vma=False,
    )
```

time: 352 us -> 148 us (0.42)
  waiting for transfers between devices: 213 us -> 62.6 us
  Pallas kernels: 0 us -> 44.1 us
  local copies, waits for them, and re-layouts: 38.8 us -> 5.08 us
  matrix products: 24.7 us -> 0 us
  other arithmetic: 22.3 us -> 0.82 us
  between operations: 14.7 us -> 0.98 us
  starting transfers between devices: 37.8 us -> 31.9 us
    ppermute x19 -> x28, waiting for transfers between devices: 205 us -> 62.6 us  [the longest x1 19.6 us: local(): center = lax.ppermute(final, 'lon', opposite)]
    pallas_call x0 -> x7, Pallas kernels: none -> 44.1 us  [the longest x4 37 us: stage(): pl.pallas_call(functools.partial(stage_kernel, last, scale), out_shape=ou...]
    dot_general x5 -> x0, matrix products: 24.7 us -> none  [the longest x4 19.8 us: rate(): jnp.einsum('qabkij,abkjf->qabif', weights, nearby, preferred_element_type...]
    gather x5 -> x0, local copies, waits for them, and re-layouts: 20.9 us -> none  [the longest x4 16.2 us: rate(): nearby = extended[ext_index]]
    concatenate x10 -> x0, other arithmetic: 9.75 us -> none  [the longest x9 9.72 us: extended_2(): block = jnp.concatenate([low, block, high], axis=dim)]
    all_gather x1 -> x0, waiting for transfers between devices: 8.66 us -> none  [local(): band_pair = lax.all_gather(final_tiles, 'lat', axis=0, tiled=True)]
    unnamed x69 -> x15, local copies, waits for them, and re-layouts: 12.9 us -> 5 us
    convert_element_type x5 -> x1, other arithmetic: 6.41 us -> 0.07 us  [local(): ends_at = jnp.stack([in_half == 0, in_half == half - 1]).astype(jnp.int32)]
  transfers between devices with their start and end apart: 20 -> 28, of which waited for: 16 -> 17; matrix products, arithmetic and copies ran while one was open for 2% -> 1% of each run, Pallas kernels for 0% -> 0%
where the time goes in v1:
time: 148 us; the launch traced here: 146 us
  waiting for transfers between devices  62.6 us (42%)
  Pallas kernels  44.1 us (30%)
  starting transfers between devices  31.9 us (22%)
  local copies, waits for them, and re-layouts  5.08 us (3%)
    pallas_call x4, Pallas kernels, stage(): pl.pallas_call(functools.partial(stage_kernel, last, scale), out_shape=ou...  37 us
    ppermute x1, waiting for transfers between devices, local(): center = lax.ppermute(final, 'lon', opposite)  19.6 us
    ppermute x1, waiting for transfers between devices, local(): below = lax.ppermute(center, 'lon', up)  19.4 us
    ppermute x4, starting transfers between devices, halo(): from_east = lax.ppermute(west, 'lon', backward)  16.3 us
    ppermute x4, waiting for transfers between devices, halo(): from_west = lax.ppermute(east, 'lon', forward)  14.5 us
    pallas_call x1, Pallas kernels, local(): pl.pallas_call(ocean_kernel, grid=(ocean_dev // block,), out_shape=jax.Sh...  6 us
    unnamed x15, local copies, waits for them, and re-layouts  5 us
    ppermute x1, starting transfers between devices, local(): native = lax.ppermute(final, 'lon', ends)  4.71 us
  transfers between devices with their start and end apart: 28, of which 17 were waited for; matrix products, arithmetic and copies ran while one was open for 1% of the time, Pallas kernels for 0%

profile of v1, /device:TPU:0, one launch (start us, length us, event | category | flops | bytes accessed | tf_op | source)
XLA Modules:
  0.0 145.5 jit_solution(13335905437601065418)
XLA Ops:
  3.1 1.6 %copy-done = f32[2,4,6,128,128]{4,3,2,1,0:T(8,128)} copy-done((f32[2,4,6,128,128]{4,3,2,1,0:T(8,128)}, f32[2,4,6,128,128]{4,3,2,1,0:T(8,128)S(1)}, u32[]{:S(2)}) %copy-start) | copy-done | bytes 3145752
  4.8 2.9 %collective-permute-start = (bf16[2,1,128,256]{3,2,1,0:T(8,128)(2,1)S(1)}, bf16[2,1,128,256]{3,2,1,0:T(8,128)(2,1)S(1)}, u32[]{:S(2)}, u32[]{:S(2)}) collective-permute-start(bf16[2,1,128,256]{3,2,1,0:T(8,128)(2,1)S(1)} %get-tuple-element.26), channel_id=1, source_target_pairs={{0,2},{2,4},{4,6},{6,8},{8,10},{10,12},{12,14},{14,0},{1,3},{3,5},... | collective-permute-start | bytes 393224 | tf_op jit(solution)/shard_map/ppermute | solution.py:235
  7.7 3.0 %collective-permute-start.1 = (bf16[2,1,128,256]{3,2,1,0:T(8,128)(2,1)S(1)}, bf16[2,1,128,256]{3,2,1,0:T(8,128)(2,1)S(1)}, u32[]{:S(2)}, u32[]{:S(2)}) collective-permute-start(bf16[2,1,128,256]{3,2,1,0:T(8,128)(2,1)S(1)} %get-tuple-element.27), channel_id=1, source_target_pairs={{2,0},{4,2},{6,4},{8,6},{10,8},{12,10},{14,12},{0,14},{3,1},{5,3},... | collective-permute-start | bytes 393224 | tf_op jit(solution)/shard_map/ppermute | solution.py:236
  10.7 3.6 %collective-permute-done.refs_3_ = bf16[2,1,128,256]{3,2,1,0:T(8,128)(2,1)S(1)} collective-permute-done((bf16[2,1,128,256]{3,2,1,0:T(8,128)(2,1)S(1)}, bf16[2,1,128,256]{3,2,1,0:T(8,128)(2,1)S(1)}, u32[]{:S(2)}, u32[]{:S(2)}) %collective-permute-start) | collective-permute-done | bytes 131104 | tf_op jit(solution)/shard_map/ppermute | solution.py:235
  16.8 9.6 %stage.3 = (f32[2,4,128,256]{3,2,1,0:T(8,128)S(1)}, bf16[2,4,128,256]{3,2,1,0:T(8,128)(2,1)S(1)}, bf16[2,1,128,256]{3,2,1,0:T(8,128)(2,1)S(1)}, bf16[2,1,128,256...) custom-call(s32[2,4,6]{2,1,0:T(4,128)S(1)} %fusion.10.index_ref, s32[1]{0:T(128)} %bitcast.send_ref, ...), custom_call_target="tpu_custom_call" | custom-call | flops 1610612736 | bytes 8388608 | tf_op jit(solution)/shard_map/stage/pallas_call | solution.py:249
  27.0 4.2 %collective-permute-start.6 = (bf16[2,1,128,256]{3,2,1,0:T(8,128)(2,1)S(1)}, bf16[2,1,128,256]{3,2,1,0:T(8,128)(2,1)S(1)}, u32[]{:S(2)}, u32[]{:S(2)}) collective-permute-start(bf16[2,1,128,256]{3,2,1,0:T(8,128)(2,1)S(1)} %get-tuple-element.32), channel_id=1, source_target_pairs={{2,0},{4,2},{6,4},{8,6},{10,8},{12,10},{14,12},{0,14},{3,1},{5,3},... | collective-permute-start | bytes 393224 | tf_op jit(solution)/shard_map/ppermute | solution.py:236
  31.2 3.6 %collective-permute-done.5.refs_3_ = bf16[2,1,128,256]{3,2,1,0:T(8,128)(2,1)S(1)} collective-permute-done((bf16[2,1,128,256]{3,2,1,0:T(8,128)(2,1)S(1)}, bf16[2,1,128,256]{3,2,1,0:T(8,128)(2,1)S(1)}, u32[]{:S(2)}, u32[]{:S(2)}) %collective-permute-start.5) | collective-permute-done | bytes 131104 | tf_op jit(solution)/shard_map/ppermute | solution.py:235
  34.9 1.3 collective-permute-done.6.refs_4_
  36.2 1.3 collective-permute-done.9.refs_7_
  37.6 9.6 %stage.4 = (f32[2,4,128,256]{3,2,1,0:T(8,128)S(1)}, bf16[2,4,128,256]{3,2,1,0:T(8,128)(2,1)S(1)}, bf16[2,1,128,256]{3,2,1,0:T(8,128)(2,1)S(1)}, bf16[2,1,128,256...) custom-call(s32[2,4,6]{2,1,0:T(4,128)S(1)} %fusion.10.index_ref, s32[1]{0:T(128)} %bitcast.send_ref, ...), custom_call_target="tpu_custom_call" | custom-call | flops 1610612736 | bytes 8388608 | tf_op jit(solution)/shard_map/stage/pallas_call | solution.py:249
  47.5 4.5 %collective-permute-start.11 = (bf16[2,1,128,256]{3,2,1,0:T(8,128)(2,1)S(1)}, bf16[2,1,128,256]{3,2,1,0:T(8,128)(2,1)S(1)}, u32[]{:S(2)}, u32[]{:S(2)}) collective-permute-start(bf16[2,1,128,256]{3,2,1,0:T(8,128)(2,1)S(1)} %get-tuple-element.37), channel_id=1, source_target_pairs={{2,0},{4,2},{6,4},{8,6},{10,8},{12,10},{14,12},{0,14},{3,1},{5,3},... | collective-permute-start | bytes 393224 | tf_op jit(solution)/shard_map/ppermute | solution.py:236
  52.0 3.6 %collective-permute-done.10.refs_3_ = bf16[2,1,128,256]{3,2,1,0:T(8,128)(2,1)S(1)} collective-permute-done((bf16[2,1,128,256]{3,2,1,0:T(8,128)(2,1)S(1)}, bf16[2,1,128,256]{3,2,1,0:T(8,128)(2,1)S(1)}, u32[]{:S(2)}, u32[]{:S(2)}) %collective-permute-start.10) | collective-permute-done | bytes 131104 | tf_op jit(solution)/shard_map/ppermute | solution.py:235
  57.9 9.8 %stage.5 = (f32[2,4,128,256]{3,2,1,0:T(8,128)S(1)}, bf16[2,4,128,256]{3,2,1,0:T(8,128)(2,1)S(1)}, bf16[2,1,128,256]{3,2,1,0:T(8,128)(2,1)S(1)}, bf16[2,1,128,256...) custom-call(s32[2,4,6]{2,1,0:T(4,128)S(1)} %fusion.10.index_ref, s32[1]{0:T(128)} %bitcast.send_ref, ...), custom_call_target="tpu_custom_call" | custom-call | flops 1610612736 | bytes 8388608 | tf_op jit(solution)/shard_map/stage/pallas_call | solution.py:249
  68.0 4.5 %collective-permute-start.16 = (bf16[2,1,128,256]{3,2,1,0:T(8,128)(2,1)S(1)}, bf16[2,1,128,256]{3,2,1,0:T(8,128)(2,1)S(1)}, u32[]{:S(2)}, u32[]{:S(2)}) collective-permute-start(bf16[2,1,128,256]{3,2,1,0:T(8,128)(2,1)S(1)} %get-tuple-element.42), channel_id=1, source_target_pairs={{2,0},{4,2},{6,4},{8,6},{10,8},{12,10},{14,12},{0,14},{3,1},{5,3},... | collective-permute-start | bytes 393224 | tf_op jit(solution)/shard_map/ppermute | solution.py:236
  72.5 3.6 %collective-permute-done.15.refs_5_ = bf16[2,1,128,256]{3,2,1,0:T(8,128)(2,1)S(1)} collective-permute-done((bf16[2,1,128,256]{3,2,1,0:T(8,128)(2,1)S(1)}, bf16[2,1,128,256]{3,2,1,0:T(8,128)(2,1)S(1)}, u32[]{:S(2)}, u32[]{:S(2)}) %collective-permute-start.15) | collective-permute-done | bytes 131104 | tf_op jit(solution)/shard_map/ppermute | solution.py:235
  78.3 7.9 %last_stage.1 = (f32[2,4,128,256]{3,2,1,0:T(8,128)}, bf16[2,4,128,256]{3,2,1,0:T(8,128)(2,1)S(1)}) custom-call(s32[2,4,6]{2,1,0:T(4,128)S(1)} %fusion.10.index_ref, s32[1]{0:T(128)} %bitcast.send_ref, bf16[4,2,4,6,128,128]{5,4,3,2,1,0:T(8,128)(2,1)} %w_ref.7, f32[2,4,6,128,128]{4,3,2,1,0:T(8,128)} %copy-done, f32[2,4,128,256]{3,2,1,0:T(8,128)S(1)} %copy-done.1, ...), custom_call_target="tpu_custom_call" | custom-call | flops 1610612736 | bytes 8388608 | tf_op jit(solution)/shard_map/last_stage/pallas_call | solution.py:249
  86.3 1.9 %collective-permute-start.20 = (bf16[8,128,256]{2,1,0:T(8,128)(2,1)S(1)}, bf16[8,128,256]{2,1,0:T(8,128)(2,1)S(1)}, u32[]{:S(2)}, u32[]{:S(2)}) collective-permute-start(bf16[8,128,256]{2,1,0:T(8,128)(2,1)S(1)} %bitcast.5), channel_id=1, source_target_pairs={{0,8},{2,10},{4,12},{6,14},{8,0},{10,2},{12,4},{14,6},{1,9},{3,11}... | collective-permute-start | bytes 1572872 | tf_op jit(solution)/shard_map/ppermute | solution.py:294
  88.2 4.7 %collective-permute-start.26 = (bf16[8,128,256]{2,1,0:T(8,128)(2,1)S(1)}, bf16[8,128,256]{2,1,0:T(8,128)(2,1)S(1)}, u32[]{:S(2)}, u32[]{:S(2)}) collective-permute-start(bf16[8,128,256]{2,1,0:T(8,128)(2,1)S(1)} %bitcast.6), channel_id=1, source_target_pairs={{0,6},{6,0},{8,14},{14,8},{1,7},{7,1},{9,15},{15,9},{16,22},{22,16... | collective-permute-start | bytes 1572872 | tf_op jit(solution)/shard_map/ppermute | solution.py:293
  92.9 19.6 %collective-permute-done.20.refs_2_ = bf16[8,128,256]{2,1,0:T(8,128)(2,1)S(1)} collective-permute-done((bf16[8,128,256]{2,1,0:T(8,128)(2,1)S(1)}, bf16[8,128,256]{2,1,0:T(8,128)(2,1)S(1)}, u32[]{:S(2)}, u32[]{:S(2)}) %collective-permute-start.20) | collective-permute-done | bytes 524320 | tf_op jit(solution)/shard_map/ppermute | solution.py:294
  112.5 2.6 %collective-permute-start.21 = (bf16[8,128,256]{2,1,0:T(8,128)(2,1)S(1)}, bf16[8,128,256]{2,1,0:T(8,128)(2,1)}, u32[]{:S(2)}, u32[]{:S(2)}) collective-permute-start(bf16[8,128,256]{2,1,0:T(8,128)(2,1)S(1)} %collective-permute-done.20.refs_2_), channel_id=1, source_target_pairs={{0,2},{2,4},{4,6},{8,10},{10,12},{12,14},{1,3},{3,5},{5,7},{9,11},... | collective-permute-start | bytes 1572872 | tf_op jit(solution)/shard_map/ppermute | solution.py:295
  115.1 1.3 collective-permute-start.24
  117.0 19.4 %collective-permute-done.21.refs_0_ = bf16[8,128,256]{2,1,0:T(8,128)(2,1)} collective-permute-done((bf16[8,128,256]{2,1,0:T(8,128)(2,1)S(1)}, bf16[8,128,256]{2,1,0:T(8,128)(2,1)}, u32[]{:S(2)}, u32[]{:S(2)}) %collective-permute-start.21) | collective-permute-done | bytes 524320 | tf_op jit(solution)/shard_map/ppermute | solution.py:295
  137.7 1.4 copy-done.2
  139.4 6.0 %ocean.1 = bf16[32,128,256]{2,1,0:T(8,128)(2,1)} custom-call(s32[32,2]{1,0:T(8,128)S(1)} %fusion.6.slot_ref, s32[2]{0:T(128)S(1)} %add_convert_fusion.ends_ref, bf16[32,128,256]{2,1,0:T(8,128)(2,1)} %copy-done.2, bf16[8,128,256]{2,1,0:T(8,128)(2,1)} %collective-permute-done.21.refs_0_, bf16[8,128,256]{2,1,0:T(8,128)(2,1)} %collective-permute-done.22.refs_1_, ...), custom_call_target="tpu_custom_call" | custom-call | tf_op jit(solution)/shard_map/ocean/pallas_call | solution.py:310
  (58 shorter events, 12.7 us)
Async XLA Ops:
  4.8 9.6 %collective-permute-start = (bf16[2,1,128,256]{3,2,1,0:T(8,128)(2,1)S(1)}, bf16[2,1,128,256]{3,2,1,0:T(8,128)(2,1)S(1)}, u32[]{:S(2)}, u32[]{:S(2)}) collective-permute-start(bf16[2,1,128,256]{3,2,1,0:T(8,128)(2,1)S(1)} %get-tuple-element.26), channel_id=1, source_target_pairs={{0,2},{2,4},{4,6},{6,8},{8,10},{10,12},{12,14},{14,0},{1,3},{3,5},... | collective-permute-start | bytes 393224 | tf_op jit(solution)/shard_map/ppermute | solution.py:235
  7.7 7.8 %collective-permute-start.1 = (bf16[2,1,128,256]{3,2,1,0:T(8,128)(2,1)S(1)}, bf16[2,1,128,256]{3,2,1,0:T(8,128)(2,1)S(1)}, u32[]{:S(2)}, u32[]{:S(2)}) collective-permute-start(bf16[2,1,128,256]{3,2,1,0:T(8,128)(2,1)S(1)} %get-tuple-element.27), channel_id=1, source_target_pairs={{2,0},{4,2},{6,4},{8,6},{10,8},{12,10},{14,12},{0,14},{3,1},{5,3},... | collective-permute-start | bytes 393224 | tf_op jit(solution)/shard_map/ppermute | solution.py:236
  10.7 5.4 %collective-permute-start.2 = (bf16[1,4,128,256]{3,2,1,0:T(8,128)(2,1)S(1)}, bf16[1,4,128,256]{3,2,1,0:T(8,128)(2,1)S(1)}, u32[]{:S(2)}, u32[]{:S(2)}) collective-permute-start(bf16[1,4,128,256]{3,2,1,0:T(8,128)(2,1)S(1)} %get-tuple-element.28), channel_id=1, source_target_pairs={{0,1},{1,0},{2,3},{3,2},{4,5},{5,4},{6,7},{7,6},{8,9},{9,8},{10,11... | collective-permute-start | bytes 786440 | tf_op jit(solution)/shard_map/ppermute | solution.py:237
  14.3 1.9 %collective-permute-start.3 = (bf16[2,1,128,256]{3,2,1,0:T(8,128)(2,1)S(1)}, bf16[2,1,128,256]{3,2,1,0:T(8,128)(2,1)S(1)}, u32[]{:S(2)}, u32[]{:S(2)}) collective-permute-start(bf16[2,1,128,256]{3,2,1,0:T(8,128)(2,1)S(1)} %collective-permute-done.refs_3_), channel_id=1, source_target_pairs={{0,1},{1,0},{2,3},{3,2},{4,5},{5,4},{6,7},{7,6},{8,9},{9,8},{10,11... | collective-permute-start | bytes 393224 | tf_op jit(solution)/shard_map/ppermute | solution.py:238
  15.5 1.3 collective-permute-start.4
  26.5 8.4 %collective-permute-start.5 = (bf16[2,1,128,256]{3,2,1,0:T(8,128)(2,1)S(1)}, bf16[2,1,128,256]{3,2,1,0:T(8,128)(2,1)S(1)}, u32[]{:S(2)}, u32[]{:S(2)}) collective-permute-start(bf16[2,1,128,256]{3,2,1,0:T(8,128)(2,1)S(1)} %get-tuple-element.31), channel_id=1, source_target_pairs={{0,2},{2,4},{4,6},{6,8},{8,10},{10,12},{12,14},{14,0},{1,3},{3,5},... | collective-permute-start | bytes 393224 | tf_op jit(solution)/shard_map/ppermute | solution.py:235
  27.0 9.2 %collective-permute-start.7 = (bf16[1,4,128,256]{3,2,1,0:T(8,128)(2,1)S(1)}, bf16[1,4,128,256]{3,2,1,0:T(8,128)(2,1)S(1)}, u32[]{:S(2)}, u32[]{:S(2)}) collective-permute-start(bf16[1,4,128,256]{3,2,1,0:T(8,128)(2,1)S(1)} %get-tuple-element.33), channel_id=1, source_target_pairs={{0,1},{1,0},{2,3},{3,2},{4,5},{5,4},{6,7},{7,6},{8,9},{9,8},{10,11... | collective-permute-start | bytes 786440 | tf_op jit(solution)/shard_map/ppermute | solution.py:237
  27.0 9.2 %collective-permute-start.6 = (bf16[2,1,128,256]{3,2,1,0:T(8,128)(2,1)S(1)}, bf16[2,1,128,256]{3,2,1,0:T(8,128)(2,1)S(1)}, u32[]{:S(2)}, u32[]{:S(2)}) collective-permute-start(bf16[2,1,128,256]{3,2,1,0:T(8,128)(2,1)S(1)} %get-tuple-element.32), channel_id=1, source_target_pairs={{2,0},{4,2},{6,4},{8,6},{10,8},{12,10},{14,12},{0,14},{3,1},{5,3},... | collective-permute-start | bytes 393224 | tf_op jit(solution)/shard_map/ppermute | solution.py:236
  34.9 1.4 collective-permute-start.8
  36.2 1.3 collective-permute-start.9
  47.2 8.4 %collective-permute-start.10 = (bf16[2,1,128,256]{3,2,1,0:T(8,128)(2,1)S(1)}, bf16[2,1,128,256]{3,2,1,0:T(8,128)(2,1)S(1)}, u32[]{:S(2)}, u32[]{:S(2)}) collective-permute-start(bf16[2,1,128,256]{3,2,1,0:T(8,128)(2,1)S(1)} %get-tuple-element.36), channel_id=1, source_target_pairs={{0,2},{2,4},{4,6},{6,8},{8,10},{10,12},{12,14},{14,0},{1,3},{3,5},... | collective-permute-start | bytes 393224 | tf_op jit(solution)/shard_map/ppermute | solution.py:235
  47.3 9.3 %collective-permute-start.12 = (bf16[1,4,128,256]{3,2,1,0:T(8,128)(2,1)S(1)}, bf16[1,4,128,256]{3,2,1,0:T(8,128)(2,1)S(1)}, u32[]{:S(2)}, u32[]{:S(2)}) collective-permute-start(bf16[1,4,128,256]{3,2,1,0:T(8,128)(2,1)S(1)} %get-tuple-element.38), channel_id=1, source_target_pairs={{0,1},{1,0},{2,3},{3,2},{4,5},{5,4},{6,7},{7,6},{8,9},{9,8},{10,11... | collective-permute-start | bytes 786440 | tf_op jit(solution)/shard_map/ppermute | solution.py:237
  47.5 9.0 %collective-permute-start.11 = (bf16[2,1,128,256]{3,2,1,0:T(8,128)(2,1)S(1)}, bf16[2,1,128,256]{3,2,1,0:T(8,128)(2,1)S(1)}, u32[]{:S(2)}, u32[]{:S(2)}) collective-permute-start(bf16[2,1,128,256]{3,2,1,0:T(8,128)(2,1)S(1)} %get-tuple-element.37), channel_id=1, source_target_pairs={{2,0},{4,2},{6,4},{8,6},{10,8},{12,10},{14,12},{0,14},{3,1},{5,3},... | collective-permute-start | bytes 393224 | tf_op jit(solution)/shard_map/ppermute | solution.py:236
  67.7 8.4 %collective-permute-start.15 = (bf16[2,1,128,256]{3,2,1,0:T(8,128)(2,1)S(1)}, bf16[2,1,128,256]{3,2,1,0:T(8,128)(2,1)S(1)}, u32[]{:S(2)}, u32[]{:S(2)}) collective-permute-start(bf16[2,1,128,256]{3,2,1,0:T(8,128)(2,1)S(1)} %get-tuple-element.41), channel_id=1, source_target_pairs={{0,2},{2,4},{4,6},{6,8},{8,10},{10,12},{12,14},{14,0},{1,3},{3,5},... | collective-permute-start | bytes 393224 | tf_op jit(solution)/shard_map/ppermute | solution.py:235
  67.7 9.2 %collective-permute-start.17 = (bf16[1,4,128,256]{3,2,1,0:T(8,128)(2,1)S(1)}, bf16[1,4,128,256]{3,2,1,0:T(8,128)(2,1)S(1)}, u32[]{:S(2)}, u32[]{:S(2)}) collective-permute-start(bf16[1,4,128,256]{3,2,1,0:T(8,128)(2,1)S(1)} %get-tuple-element.43), channel_id=1, source_target_pairs={{0,1},{1,0},{2,3},{3,2},{4,5},{5,4},{6,7},{7,6},{8,9},{9,8},{10,11... | collective-permute-start | bytes 786440 | tf_op jit(solution)/shard_map/ppermute | solution.py:237
  68.0 9.0 %collective-permute-start.16 = (bf16[2,1,128,256]{3,2,1,0:T(8,128)(2,1)S(1)}, bf16[2,1,128,256]{3,2,1,0:T(8,128)(2,1)S(1)}, u32[]{:S(2)}, u32[]{:S(2)}) collective-permute-start(bf16[2,1,128,256]{3,2,1,0:T(8,128)(2,1)S(1)} %get-tuple-element.42), channel_id=1, source_target_pairs={{2,0},{4,2},{6,4},{8,6},{10,8},{12,10},{14,12},{0,14},{3,1},{5,3},... | collective-permute-start | bytes 393224 | tf_op jit(solution)/shard_map/ppermute | solution.py:236
  86.3 26.2 %collective-permute-start.20 = (bf16[8,128,256]{2,1,0:T(8,128)(2,1)S(1)}, bf16[8,128,256]{2,1,0:T(8,128)(2,1)S(1)}, u32[]{:S(2)}, u32[]{:S(2)}) collective-permute-start(bf16[8,128,256]{2,1,0:T(8,128)(2,1)S(1)} %bitcast.5), channel_id=1, source_target_pairs={{0,8},{2,10},{4,12},{6,14},{8,0},{10,2},{12,4},{14,6},{1,9},{3,11}... | collective-permute-start | bytes 1572872 | tf_op jit(solution)/shard_map/ppermute | solution.py:294
  88.2 28.3 %collective-permute-start.26 = (bf16[8,128,256]{2,1,0:T(8,128)(2,1)S(1)}, bf16[8,128,256]{2,1,0:T(8,128)(2,1)S(1)}, u32[]{:S(2)}, u32[]{:S(2)}) collective-permute-start(bf16[8,128,256]{2,1,0:T(8,128)(2,1)S(1)} %bitcast.6), channel_id=1, source_target_pairs={{0,6},{6,0},{8,14},{14,8},{1,7},{7,1},{9,15},{15,9},{16,22},{22,16... | collective-permute-start | bytes 1572872 | tf_op jit(solution)/shard_map/ppermute | solution.py:293
  112.5 23.9 %collective-permute-start.21 = (bf16[8,128,256]{2,1,0:T(8,128)(2,1)S(1)}, bf16[8,128,256]{2,1,0:T(8,128)(2,1)}, u32[]{:S(2)}, u32[]{:S(2)}) collective-permute-start(bf16[8,128,256]{2,1,0:T(8,128)(2,1)S(1)} %collective-permute-done.20.refs_2_), channel_id=1, source_target_pairs={{0,2},{2,4},{4,6},{8,10},{10,12},{12,14},{1,3},{3,5},{5,7},{9,11},... | collective-permute-start | bytes 1572872 | tf_op jit(solution)/shard_map/ppermute | solution.py:295
  115.1 21.3 %collective-permute-start.24 = (bf16[8,128,256]{2,1,0:T(8,128)(2,1)S(1)}, bf16[8,128,256]{2,1,0:T(8,128)(2,1)}, u32[]{:S(2)}, u32[]{:S(2)}) collective-permute-start(bf16[8,128,256]{2,1,0:T(8,128)(2,1)S(1)} %collective-permute-done.20.refs_2_), channel_id=1, source_target_pairs={{2,0},{4,2},{6,4},{10,8},{12,10},{14,12},{3,1},{5,3},{7,5},{11,9},... | collective-permute-start | bytes 1572872 | tf_op jit(solution)/shard_map/ppermute | solution.py:296
  116.4 22.7 %collective-permute-start.23 = (bf16[8,128,256]{2,1,0:T(8,128)(2,1)S(1)}, bf16[8,128,256]{2,1,0:T(8,128)(2,1)}, u32[]{:S(2)}, u32[]{:S(2)}) collective-permute-start(bf16[8,128,256]{2,1,0:T(8,128)(2,1)S(1)} %collective-permute-done.20.refs_2_), channel_id=1, source_target_pairs={{0,1},{1,0},{2,3},{3,2},{4,5},{5,4},{6,7},{7,6},{8,9},{9,8},{10,11... | collective-permute-start | bytes 1572872 | tf_op jit(solution)/shard_map/ppermute | solution.py:299
  116.5 22.7 %collective-permute-start.27 = (bf16[8,128,256]{2,1,0:T(8,128)(2,1)S(1)}, bf16[8,128,256]{2,1,0:T(8,128)(2,1)}, u32[]{:S(2)}, u32[]{:S(2)}) collective-permute-start(bf16[8,128,256]{2,1,0:T(8,128)(2,1)S(1)} %collective-permute-done.26.refs_6_), channel_id=1, source_target_pairs={{0,1},{1,0},{2,3},{3,2},{4,5},{5,4},{6,7},{7,6},{8,9},{9,8},{10,11... | collective-permute-start | bytes 1572872 | tf_op jit(solution)/shard_map/ppermute | solution.py:300
  136.4 2.8 %collective-permute-start.22 = (bf16[8,128,256]{2,1,0:T(8,128)(2,1)}, bf16[8,128,256]{2,1,0:T(8,128)(2,1)}, u32[]{:S(2)}, u32[]{:S(2)}) collective-permute-start(bf16[8,128,256]{2,1,0:T(8,128)(2,1)} %collective-permute-done.21.refs_0_), channel_id=1, source_target_pairs={{0,1},{1,0},{2,3},{3,2},{4,5},{5,4},{6,7},{7,6},{8,9},{9,8},{10,11... | collective-permute-start | bytes 1572872 | tf_op jit(solution)/shard_map/ppermute | solution.py:299
  136.4 3.0 %collective-permute-start.25 = (bf16[8,128,256]{2,1,0:T(8,128)(2,1)}, bf16[8,128,256]{2,1,0:T(8,128)(2,1)}, u32[]{:S(2)}, u32[]{:S(2)}) collective-permute-start(bf16[8,128,256]{2,1,0:T(8,128)(2,1)} %collective-permute-done.24.refs_4_), channel_id=1, source_target_pairs={{0,1},{1,0},{2,3},{3,2},{4,5},{5,4},{6,7},{7,6},{8,9},{9,8},{10,11... | collective-permute-start | bytes 1572872 | tf_op jit(solution)/shard_map/ppermute | solution.py:299
  (11 other events, 186.2 us)

commit v2 on v1

v2 whole, which is shorter than its diff:
```python
import functools

import jax
import jax.numpy as jnp
from jax import lax
from jax.experimental import pallas as pl
from jax.experimental.pallas import tpu as pltpu
from jax.sharding import PartitionSpec as P

CORIOLIS = 2.0
STEP_SIZE = 0.2
BF16 = jnp.bfloat16
F32 = jnp.float32
VMEM = pl.BlockSpec(memory_space=pltpu.VMEM)
SMEM = pl.BlockSpec(memory_space=pltpu.SMEM)
MIB = 1024 * 1024


def in_vmem(value):
    return pltpu.with_memory_space_constraint(value, pltpu.VMEM)


def vmem_call(kernel, name, outs, scalars, arrays, scratch=(), limit=8, flops=0):
    return pl.pallas_call(
        kernel,
        out_shape=[pltpu.VMEM(shape, dtype) for shape, dtype in outs],
        in_specs=[SMEM] * len(scalars) + [VMEM] * len(arrays),
        out_specs=[VMEM] * len(outs),
        scratch_shapes=list(scratch),
        compiler_params=pltpu.CompilerParams(vmem_limit_bytes=limit * MIB),
        cost_estimate=pl.CostEstimate(flops=flops, bytes_accessed=1 * MIB, transcendentals=0),
        name=name,
    )(*scalars, *[in_vmem(array) for array in arrays])


def prep_kernel(scalar_ref, state_ref, inner_ref, west_ref, east_ref, erow_ref, irow_ref):
    rows, cols = state_ref.shape[:2]
    for a in range(rows):
        west_ref[a, 0] = state_ref[a, 0].astype(BF16)
        east_ref[a, 0] = state_ref[a, cols - 1].astype(BF16)
        for b in range(1, cols - 1):
            inner_ref[a, b - 1] = state_ref[a, b].astype(BF16)
    send = scalar_ref[0]
    erow_ref[0, 0] = west_ref[send, 0]
    erow_ref[0, 1] = east_ref[send, 0]
    irow_ref[0] = inner_ref[send]


def coef_kernel(pos_ref, coef_ref):
    rows, cols, nodes = pos_ref.shape[1:]
    low = lax.broadcasted_iota(jnp.int32, (nodes, nodes), 1) < nodes // 2
    for a in range(rows):
        for b in range(cols):
            x0, x1, x2 = (
                jnp.broadcast_to(pos_ref[c, a, b][None, :], (nodes, nodes)).T for c in range(3)
            )
            spin = CORIOLIS * x2
            coef_ref[a, b, 0] = jnp.where(low, x0, x1)
            coef_ref[a, b, 1] = jnp.where(low, x2, 0.0)
            coef_ref[a, b, 2] = spin * jnp.where(low, x1, -x0)
            coef_ref[a, b, 3] = spin * jnp.where(low, -x2, x2)
            coef_ref[a, b, 4] = jnp.where(low, spin * x0, 0.0)
            coef_ref[a, b, 5] = jnp.where(low, spin * x1, 0.0)


def turned(value):
    return pltpu.roll(value, value.shape[-1] // 2, axis=1)


def tendency(tile, grads, coef, low):
    half = tile.shape[-1] // 2
    sa, sb = tile[:, :half], tile[:, half:]
    ra, rb = turned(sa), turned(sb)
    v0 = jnp.where(low, sa, ra)
    v1 = jnp.where(low, ra, sa)
    v2 = jnp.where(low, sb, rb)
    ga = [g[:, :half] for g in grads]
    gb = [g[:, half:] for g in grads]
    t0a, t0b, t2b = turned(ga[0]), turned(gb[0]), turned(gb[2])
    fa = (
        ga[3]
        - (v0 * ga[0] + v1 * ga[1] + v2 * ga[2])
        - (coef[2] * v2 + coef[3] * ra)
        - jnp.where(low, t0b, gb[1])
    )
    spread = sb * (t0a + ga[1] + t2b)
    fb = (
        gb[3]
        - (v0 * gb[0] + v1 * gb[1] + v2 * gb[2])
        - (coef[4] * v1 - coef[5] * v0)
        - jnp.where(low, t2b, spread)
    )
    part = coef[0] * fa + coef[1] * fb
    radial = part + turned(part)
    return fa - coef[0] * radial, fb - coef[1] * radial


def stage_kernel(edge, first, last, scale, scalar_ref, w_ref, coef_ref, state_ref, *refs):
    refs = list(refs)
    ext = refs.pop()
    rows, cols, nodes, feats = state_ref.shape
    taps = w_ref.shape[3]
    columns = (0, cols - 1) if edge else tuple(range(1, cols - 1))

    def take(count):
        taken, refs[:count] = refs[:count], []
        return taken

    older = take(2) if last else []
    now_ref = None if first else take(1)[0]
    inner_ref, west_ref, east_ref, erow_ref, irow_ref = take(5)
    for a in range(rows):
        ext[a, 1] = west_ref[a, 0]
        ext[a, cols] = east_ref[a, 0]
        for b in range(cols - 2):
            ext[a, b + 2] = inner_ref[a, b]
    ext[rows, 1] = erow_ref[0, 0]
    ext[rows, cols] = erow_ref[0, 1]
    for b in range(cols - 2):
        ext[rows, b + 2] = irow_ref[0, b]
    send = scalar_ref[0]
    if edge:
        fwest_ref, feast_ref, cwest_ref, ceast_ref = take(4)
        for a in range(rows):
            ext[a, 0] = fwest_ref[a, 0]
            ext[a, cols + 1] = feast_ref[a, 0]
        ext[rows, 0] = cwest_ref[1 - send, 0]
        ext[rows, cols + 1] = ceast_ref[1 - send, 0]

    next_ref, *outs = refs
    low = lax.broadcasted_iota(jnp.int32, (nodes, feats // 2), 1) < feats // 4
    for a in range(rows):
        for place, b in enumerate(columns):
            base = 1 + (a * cols + b) * taps
            where = [scalar_ref[base + k] for k in range(taps)]
            near = jnp.concatenate([ext[w // (cols + 2), w % (cols + 2)] for w in where], axis=0)
            weights = jnp.concatenate(
                [
                    jnp.concatenate([w_ref[q, a, b, k] for k in range(taps)], axis=1)
                    for q in range(4)
                ],
                axis=0,
            )
            derivs = jnp.dot(weights, near, preferred_element_type=F32)
            grads = [derivs[q * nodes : (q + 1) * nodes] for q in range(4)]
            coef = [coef_ref[a, b, i] for i in range(6)]
            now = state_ref[a, b] if first else now_ref[a, place]
            rate = jnp.concatenate(tendency(now, grads, coef, low), axis=1)
            if last:
                out = (1.0 / 3.0) * (
                    older[0][a, place] + 2.0 * older[1][a, place] + now - state_ref[a, b]
                ) + scale * rate
            else:
                out = state_ref[a, b] + scale * rate
            next_ref[a, place] = out
            rounded = out.astype(BF16)
            if last or not edge:
                outs[0][a, place] = rounded
            else:
                outs[place][a, 0] = rounded
    if not last:
        if edge:
            outs[2][0, 0] = outs[0][send, 0]
            outs[2][0, 1] = outs[1][send, 0]
        else:
            outs[1][0] = outs[0][send]


def turn_kernel(interp_ref, out_ref):
    tiles, taps, nodes, points = interp_ref.shape
    for o in range(tiles):
        out_ref[o] = interp_ref[o].reshape(taps * nodes, points).T


def ocean_kernel(chunks, scalar_ref, interp_ref, *refs):
    *sources, out_ref, tiles = refs
    size = sources[0].shape[0] * sources[0].shape[1]
    flat = [source.reshape(size, *source.shape[2:]) for source in sources]
    per = 2 * chunks

    @pl.when(pl.program_id(0) == 0)
    def _():
        for side, flag in ((0, scalar_ref[0]), (1, None), (2, scalar_ref[1])):
            for part in range(per):
                place = (side * per + part) * size
                if flag is None:
                    tiles[pl.ds(place, size)] = flat[side * per + part][...]
                else:

                    @pl.when(flag == 0)
                    def _():
                        tiles[pl.ds(place, size)] = flat[side * per + part][...]

                    @pl.when(flag == 1)
                    def _():
                        tiles[pl.ds(place, size)] = flat[3 * per + part][...]

    block = interp_ref.shape[0]
    taps = 2
    base = 2 + pl.program_id(0) * (block * taps)
    for o in range(block):
        near = jnp.concatenate(
            [tiles[scalar_ref[base + o * taps + j]] for j in range(taps)], axis=0
        )
        out_ref[o] = jnp.dot(interp_ref[o], near, preferred_element_type=F32).astype(BF16)


def local(state, weights, positions, stencil_codes, ovl_owner, ovl_local, interp):
    rows, cols, nodes, feats = state.shape
    taps = stencil_codes.shape[-1]
    lon_count = lax.axis_size("lon")
    lat_count = lax.axis_size("lat")
    my_lon = lax.axis_index("lon")
    my_lat = lax.axis_index("lat")
    forward = [(i, (i + 1) % lon_count) for i in range(lon_count)]
    backward = [(target, source) for source, target in forward]
    swap = [(i, lat_count - 1 - i) for i in range(lat_count)]

    tile_row = lax.broadcasted_iota(jnp.int32, stencil_codes.shape, 0)
    tile_col = lax.broadcasted_iota(jnp.int32, stencil_codes.shape, 1)
    ext_row = tile_row + stencil_codes // 3 - 1
    ext_row = jnp.where(ext_row < 0, rows, ext_row)
    index = ext_row * (cols + 2) + tile_col + stencil_codes % 3
    send = (1 - my_lat).astype(jnp.int32).reshape(1)
    scalars = jnp.concatenate([send, index.reshape(-1)])

    inner_cols = cols - 2
    tile = (nodes, feats)
    west_s = ((rows, 1) + tile, BF16)
    inner_s = ((rows, inner_cols) + tile, BF16)
    erow_s = ((1, 2) + tile, BF16)
    irow_s = ((1, inner_cols) + tile, BF16)

    inner, west, east, erow, irow = vmem_call(
        prep_kernel, "prep", [inner_s, west_s, west_s, erow_s, irow_s], [send], [state]
    )
    (coef,) = vmem_call(
        coef_kernel, "coef", [((rows, cols, 6, nodes, nodes), F32)], [], [positions]
    )

    def flip(value):
        return lax.ppermute(value, "lat", swap)

    flops = 2 * 4 * rows * taps * nodes * nodes * feats

    def stage(scale, fields_i, fields_e, own, first=False, last=False):
        inner, west, east, erow, irow = own
        from_west = lax.ppermute(east, "lon", forward)
        from_east = lax.ppermute(west, "lon", backward)
        near = [inner, west, east, flip(erow), flip(irow)]
        far = [from_west, from_east, flip(from_west), flip(from_east)]
        results = []
        for edge in (False, True):
            width = 2 if edge else inner_cols
            outs = [((rows, width) + tile, F32)]
            if last:
                outs += [((rows, width) + tile, BF16)]
            else:
                outs += [west_s, west_s, erow_s] if edge else [inner_s, irow_s]
            results.append(
                vmem_call(
                    functools.partial(stage_kernel, edge, first, last, scale),
                    ("edge" if edge else "inner") + ("_last" if last else ""),
                    outs,
                    [scalars],
                    [weights, coef, state]
                    + (fields_e if edge else fields_i)
                    + near
                    + (far if edge else []),
                    [pltpu.VMEM((rows + 1, cols + 2) + tile, BF16)],
                    flops=flops * width,
                )
            )
        return results

    own = (inner, west, east, erow, irow)
    half_step = 0.5 * STEP_SIZE
    (i2, inner, irow), (e2, west, east, erow) = stage(half_step, [], [], own, first=True)
    own = (inner, west, east, erow, irow)
    (i3, inner, irow), (e3, west, east, erow) = stage(half_step, [i2], [e2], own)
    own = (inner, west, east, erow, irow)
    (i4, inner, irow), (e4, west, east, erow) = stage(STEP_SIZE, [i3], [e3], own)
    own = (inner, west, east, erow, irow)
    (next_i, final_i), (next_e, final_e) = stage(
        STEP_SIZE / 6.0, [i2, i3, i4], [e2, e3, e4], own, last=True
    )
    next_state = jnp.concatenate([next_e[:, :1], next_i, next_e[:, 1:]], axis=1)

    ocean_dev, intersections = ovl_local.shape
    (turned_interp,) = vmem_call(
        turn_kernel,
        "turn_interp",
        [((ocean_dev, nodes, intersections * nodes), BF16)],
        [],
        [interp],
    )

    half = lon_count // 2
    opposite = [(i, (i + half) % lon_count) for i in range(lon_count)]
    seam = (half - 1, lon_count - 1)
    ends = [(0, half - 1), (half - 1, 0), (half, lon_count - 1), (lon_count - 1, half)]
    up = [pair for pair in forward if pair[0] not in seam]
    down = [pair for pair in backward if pair[1] not in seam]
    below, center, above, native = [], [], [], []
    chunks = [final_i, final_e]
    for final in chunks:
        native.append(lax.ppermute(final, "lon", ends))
        center.append(lax.ppermute(final, "lon", opposite))
        below.append(lax.ppermute(center[-1], "lon", up))
        above.append(lax.ppermute(center[-1], "lon", down))
    sources = []
    for pieces in (below, center, above, native):
        sources += pieces + [flip(piece) for piece in pieces]

    middle = (my_lon + half) % lon_count
    owners = ovl_owner.reshape(ocean_dev, intersections)
    relative = (owners // lat_count - middle + 1 + lon_count) % lon_count
    away = (owners % lat_count != my_lat).astype(jnp.int32)
    tile_row, tile_col = ovl_local // cols, ovl_local % cols
    is_edge = (tile_col == 0) | (tile_col == cols - 1)
    chunk = is_edge.astype(jnp.int32)
    within = jnp.where(
        is_edge, tile_row * 2 + (tile_col == cols - 1), tile_row * inner_cols + tile_col - 1
    )
    per_chunk = rows * inner_cols
    slot = ((relative * 2 + away) * 2 + chunk) * per_chunk + within
    in_half = my_lon % half
    at_ends = jnp.stack([in_half == 0, in_half == half - 1]).astype(jnp.int32)
    ocean_scalars = jnp.concatenate([at_ends, slot.reshape(-1).astype(jnp.int32)])
    block = 8
    ocean = pl.pallas_call(
        functools.partial(ocean_kernel, len(chunks)),
        grid=(ocean_dev // block,),
        out_shape=jax.ShapeDtypeStruct((ocean_dev, nodes, feats), BF16),
        in_specs=[SMEM, pl.BlockSpec((block, nodes, intersections * nodes), lambda g: (g, 0, 0))]
        + [VMEM] * len(sources),
        out_specs=pl.BlockSpec((block, nodes, feats), lambda g: (g, 0, 0)),
        scratch_shapes=[pltpu.VMEM((6 * rows * cols, nodes, feats), BF16)],
        compiler_params=pltpu.CompilerParams(vmem_limit_bytes=16 * MIB),
        name="ocean",
    )(ocean_scalars, turned_interp, *[in_vmem(source) for source in sources])
    return next_state, ocean


def solution(mesh):
    placed = (
        P(("member", "lat"), "lon", None, None),
        P(None, "lat", "lon", None, None, None),
        P(None, "lat", "lon", None),
        P("lat", "lon", None),
        P(("lon", "lat"), None, None),
        P(("lon", "lat"), None),
        P(("lon", "lat"), None, None, None),
    )
    return jax.shard_map(
        local,
        mesh=mesh,
        in_specs=placed,
        out_specs=(
            P(("member", "lat"), "lon", None, None),
            P(("member", "lon", "lat"), None, None),
        ),
        check_vma=False,
    )
```

time: 148 us -> 107 us (0.72); the launches traced: 146 us -> 106 us
  waiting for transfers between devices: 62.6 us -> 30.5 us
  Pallas kernels: 44.1 us -> 24.2 us
  starting transfers between devices: 31.9 us -> 39.5 us
  local copies, waits for them, and re-layouts: 5.08 us -> 9.2 us
    ppermute x28 -> x40, waiting for transfers between devices: 62.6 us -> 30.5 us  [the longest x2 8.16 us: local(): center.append(lax.ppermute(final, 'lon', opposite))]
    pallas_call x7 -> x12, Pallas kernels: 44.1 us -> 24.2 us  [the longest x11 20.4 us: vmem_call(): pl.pallas_call(kernel, out_shape=[pltpu.VMEM(shape, dtype) for shape, dty...]
    ppermute x28 -> x40, starting transfers between devices: 31.9 us -> 39.5 us  [the longest x4 16.9 us: stage(): from_east = lax.ppermute(west, 'lon', backward)]
    unnamed x15 -> x30, local copies, waits for them, and re-layouts: 5 us -> 8.88 us
  transfers between devices with their start and end apart: 28 -> 40, of which waited for: 17 -> 16; matrix products, arithmetic and copies ran while one was open for 1% -> 2% of each run, Pallas kernels for 0% -> 14%
where the time goes in v2:
time: 107 us; the launch traced here: 106 us
  starting transfers between devices  39.5 us (37%)
  waiting for transfers between devices  30.5 us (29%)
  Pallas kernels  24.2 us (23%)
  local copies, waits for them, and re-layouts  9.2 us (9%)
  other arithmetic  2.02 us (2%)
    pallas_call x11, Pallas kernels, vmem_call(): pl.pallas_call(kernel, out_shape=[pltpu.VMEM(shape, dtype) for shape, dty...  20.4 us
    ppermute x4, starting transfers between devices, stage(): from_east = lax.ppermute(west, 'lon', backward)  16.9 us
    unnamed x30, local copies, waits for them, and re-layouts  8.88 us
    ppermute x2, waiting for transfers between devices, local(): center.append(lax.ppermute(final, 'lon', opposite))  8.16 us
    ppermute x2, starting transfers between devices, local(): native.append(lax.ppermute(final, 'lon', ends))  6.28 us
    ppermute x2, waiting for transfers between devices, local(): above.append(lax.ppermute(center[-1], 'lon', down))  5.83 us
    ppermute x4, waiting for transfers between devices, stage(): from_west = lax.ppermute(east, 'lon', forward)  4.78 us
    ppermute x24, starting transfers between devices, flip(): return lax.ppermute(value, 'lat', swap)  3.98 us
  transfers between devices with their start and end apart: 40, of which 16 were waited for; matrix products, arithmetic and copies ran while one was open for 2% of the time, Pallas kernels for 14%

profile of v2, /device:TPU:0, one launch (start us, length us, event | category | flops | bytes accessed | tf_op | source)
XLA Modules:
  0.0 106.4 jit_solution(17586254054605712217)
XLA Ops:
  2.6 2.9 %collective-permute-start.2 = (bf16[2,1,128,256]{3,2,1,0:T(8,128)(2,1)S(1)}, bf16[2,1,128,256]{3,2,1,0:T(8,128)(2,1)}, u32[]{:S(2)}, u32[]{:S(2)}) collective-permute-start(bf16[2,1,128,256]{3,2,1,0:T(8,128)(2,1)S(1)} %get-tuple-element.34.refs_2_), channel_id=1, source_target_pairs={{0,2},{2,4},{4,6},{6,8},{8,10},{10,12},{12,14},{14,0},{1,3},{3,5},... | collective-permute-start | bytes 393224 | tf_op jit(solution)/shard_map/ppermute | solution.py:248
  6.2 3.0 %collective-permute-start.3 = (bf16[2,1,128,256]{3,2,1,0:T(8,128)(2,1)S(1)}, bf16[2,1,128,256]{3,2,1,0:T(8,128)(2,1)}, u32[]{:S(2)}, u32[]{:S(2)}) collective-permute-start(bf16[2,1,128,256]{3,2,1,0:T(8,128)(2,1)S(1)} %get-tuple-element.33.refs_1_), channel_id=1, source_target_pairs={{2,0},{4,2},{6,4},{8,6},{10,8},{12,10},{14,12},{0,14},{3,1},{5,3},... | collective-permute-start | bytes 393224 | tf_op jit(solution)/shard_map/ppermute | solution.py:249
  9.8 2.5 %collective-permute-done.2.refs_5_ = bf16[2,1,128,256]{3,2,1,0:T(8,128)(2,1)} collective-permute-done((bf16[2,1,128,256]{3,2,1,0:T(8,128)(2,1)S(1)}, bf16[2,1,128,256]{3,2,1,0:T(8,128)(2,1)}, u32[]{:S(2)}, u32[]{:S(2)}) %collective-permute-start.2) | collective-permute-done | bytes 131104 | tf_op jit(solution)/shard_map/ppermute | solution.py:248
  16.5 2.8 %copy-done = bf16[4,2,4,6,128,128]{5,4,3,2,1,0:T(8,128)(2,1)S(1)} copy-done((bf16[4,2,4,6,128,128]{5,4,3,2,1,0:T(8,128)(2,1)S(1)}, bf16[4,2,4,6,128,128]{5,4,3,2,1,0:T(8,128)(2,1)}, u32[]{:S(2)}) %copy-start) | copy-done | bytes 6291480
  19.3 2.8 %edge.3 = (f32[2,2,128,256]{3,2,1,0:T(8,128)S(1)}, bf16[2,1,128,256]{3,2,1,0:T(8,128)(2,1)S(1)}, bf16[2,1,128,256]{3,2,1,0:T(8,128)(2,1)S(1)}, bf16[1,2,128,256]{3,2,1,0:T(8,128)(2,1)S(1)}) custom-call(s32[49]{0:T(128)S(1)} %pad_add_fusion.scalar_ref, bf16[4,2,4,6,128,128]{5,4,3,2,1,0:T(8,128)(2,1)S(1)} %copy-done, f32[2,4,6,128,128]{4,3,2,1,0:T(8,128)S(1)} %coef.1.coef_ref, ...), custom_call_target="tpu_custom_call" | custom-call | flops 805306368 | bytes 1048576 | tf_op jit(solution)/shard_map/edge/pallas_call | solution.py:24
  22.2 4.7 %collective-permute-start.9 = (bf16[2,1,128,256]{3,2,1,0:T(8,128)(2,1)S(1)}, bf16[2,1,128,256]{3,2,1,0:T(8,128)(2,1)S(1)}, u32[]{:S(2)}, u32[]{:S(2)}) collective-permute-start(bf16[2,1,128,256]{3,2,1,0:T(8,128)(2,1)S(1)} %get-tuple-element.39.refs_2_), channel_id=1, source_target_pairs={{2,0},{4,2},{6,4},{8,6},{10,8},{12,10},{14,12},{0,14},{3,1},{5,3},... | collective-permute-start | bytes 393224 | tf_op jit(solution)/shard_map/ppermute | solution.py:249
  26.9 2.4 %inner.3 = (f32[2,2,128,256]{3,2,1,0:T(8,128)S(1)}, bf16[2,2,128,256]{3,2,1,0:T(8,128)(2,1)S(1)}, bf16[1,2,128,256]{3,2,1,0:T(8,128)(2,1)S(1)}) custom-call(s32[49]{0:T(128)S(1)} %pad_add_fusion.scalar_ref, bf16[4,2,4,6,128,128]{5,4,3,2,1,0:T(8,128)(2,1)S(1)} %copy-done, f32[2,4,6,128,128]{4,3,2,1,0:T(8,128)S(1)} %coef.1.coef_ref, ...), custom_call_target="tpu_custom_call" | custom-call | flops 805306368 | bytes 1048576 | tf_op jit(solution)/shard_map/inner/pallas_call | solution.py:24
  32.4 2.0 %edge.4 = (f32[2,2,128,256]{3,2,1,0:T(8,128)S(1)}, bf16[2,1,128,256]{3,2,1,0:T(8,128)(2,1)S(1)}, bf16[2,1,128,256]{3,2,1,0:T(8,128)(2,1)S(1)}, bf16[1,2,128,256]{3,2,1,0:T(8,128)(2,1)S(1)}) custom-call(s32[49]{0:T(128)S(1)} %pad_add_fusion.scalar_ref, bf16[4,2,4,6,128,128]{5,4,3,2,1,0:T(8,128)(2,1)S(1)} %bitcast.5, f32[2,4,6,128,128]{4,3,2,1,0:T(8,128)S(1)} %coef.1.coef_ref, ...), custom_call_target="tpu_custom_call" | custom-call | flops 805306368 | bytes 1048576 | tf_op jit(solution)/shard_map/edge/pallas_call | solution.py:24
  34.8 4.4 %collective-permute-start.15 = (bf16[2,1,128,256]{3,2,1,0:T(8,128)(2,1)S(1)}, bf16[2,1,128,256]{3,2,1,0:T(8,128)(2,1)S(1)}, u32[]{:S(2)}, u32[]{:S(2)}) collective-permute-start(bf16[2,1,128,256]{3,2,1,0:T(8,128)(2,1)S(1)} %get-tuple-element.46.refs_2_), channel_id=1, source_target_pairs={{2,0},{4,2},{6,4},{8,6},{10,8},{12,10},{14,12},{0,14},{3,1},{5,3},... | collective-permute-start | bytes 393224 | tf_op jit(solution)/shard_map/ppermute | solution.py:249
  39.2 2.0 %inner.4 = (f32[2,2,128,256]{3,2,1,0:T(8,128)S(1)}, bf16[2,2,128,256]{3,2,1,0:T(8,128)(2,1)S(1)}, bf16[1,2,128,256]{3,2,1,0:T(8,128)(2,1)S(1)}) custom-call(s32[49]{0:T(128)S(1)} %pad_add_fusion.scalar_ref, bf16[4,2,4,6,128,128]{5,4,3,2,1,0:T(8,128)(2,1)S(1)} %bitcast.5, f32[2,4,6,128,128]{4,3,2,1,0:T(8,128)S(1)} %coef.1.coef_ref, ...), custom_call_target="tpu_custom_call" | custom-call | flops 805306368 | bytes 1048576 | tf_op jit(solution)/shard_map/inner/pallas_call | solution.py:24
  43.6 2.0 %inner.5 = (f32[2,2,128,256]{3,2,1,0:T(8,128)S(1)}, bf16[2,2,128,256]{3,2,1,0:T(8,128)(2,1)S(1)}, bf16[1,2,128,256]{3,2,1,0:T(8,128)(2,1)S(1)}) custom-call(s32[49]{0:T(128)S(1)} %pad_add_fusion.scalar_ref, bf16[4,2,4,6,128,128]{5,4,3,2,1,0:T(8,128)(2,1)S(1)} %bitcast.5, f32[2,4,6,128,128]{4,3,2,1,0:T(8,128)S(1)} %coef.1.coef_ref, ...), custom_call_target="tpu_custom_call" | custom-call | flops 805306368 | bytes 1048576 | tf_op jit(solution)/shard_map/inner/pallas_call | solution.py:24
  46.1 2.0 %edge.5 = (f32[2,2,128,256]{3,2,1,0:T(8,128)S(1)}, bf16[2,1,128,256]{3,2,1,0:T(8,128)(2,1)S(1)}, bf16[2,1,128,256]{3,2,1,0:T(8,128)(2,1)S(1)}, bf16[1,2,128,256]{3,2,1,0:T(8,128)(2,1)S(1)}) custom-call(s32[49]{0:T(128)S(1)} %pad_add_fusion.scalar_ref, bf16[4,2,4,6,128,128]{5,4,3,2,1,0:T(8,128)(2,1)S(1)} %bitcast.5, f32[2,4,6,128,128]{4,3,2,1,0:T(8,128)S(1)} %coef.1.coef_ref, ...), custom_call_target="tpu_custom_call" | custom-call | flops 805306368 | bytes 1048576 | tf_op jit(solution)/shard_map/edge/pallas_call | solution.py:24
  48.3 4.7 %collective-permute-start.21 = (bf16[2,1,128,256]{3,2,1,0:T(8,128)(2,1)S(1)}, bf16[2,1,128,256]{3,2,1,0:T(8,128)(2,1)S(1)}, u32[]{:S(2)}, u32[]{:S(2)}) collective-permute-start(bf16[2,1,128,256]{3,2,1,0:T(8,128)(2,1)S(1)} %get-tuple-element.53.refs_4_), channel_id=1, source_target_pairs={{2,0},{4,2},{6,4},{8,6},{10,8},{12,10},{14,12},{0,14},{3,1},{5,3},... | collective-permute-start | bytes 393224 | tf_op jit(solution)/shard_map/ppermute | solution.py:249
  53.0 2.8 %inner_last.1 = (f32[2,2,128,256]{3,2,1,0:T(8,128)S(1)}, bf16[2,2,128,256]{3,2,1,0:T(8,128)(2,1)}) custom-call(s32[49]{0:T(128)S(1)} %pad_add_fusion.scalar_ref, bf16[4,2,4,6,128,128]{5,4,3,2,1,0:T(8,128)(2,1)S(1)} %bitcast.5, f32[2,4,6,128,128]{4,3,2,1,0:T(8,128)S(1)} %coef.1.coef_ref, f32[2,4,128,256]{3,2,1,0:T(8,128)S(1)} %copy-done.2, ...), custom_call_target="tpu_custom_call" | custom-call | flops 805306368 | bytes 1048576 | tf_op jit(solution)/shard_map/inner_last/pallas_call | solution.py:24
  57.8 2.9 %collective-permute-start.36 = (bf16[2,2,128,256]{3,2,1,0:T(8,128)(2,1)}, bf16[2,2,128,256]{3,2,1,0:T(8,128)(2,1)}, u32[]{:S(2)}, u32[]{:S(2)}) collective-permute-start(bf16[2,2,128,256]{3,2,1,0:T(8,128)(2,1)} %get-tuple-element.60), channel_id=1, source_target_pairs={{0,6},{6,0},{8,14},{14,8},{1,7},{7,1},{9,15},{15,9},{16,22},{22,16... | collective-permute-start | bytes 786440 | tf_op jit(solution)/shard_map/ppermute | solution.py:307
  60.8 2.7 %edge_last.1 = (f32[2,2,128,256]{3,2,1,0:T(8,128)S(1)}, bf16[2,2,128,256]{3,2,1,0:T(8,128)(2,1)}) custom-call(s32[49]{0:T(128)S(1)} %pad_add_fusion.scalar_ref, bf16[4,2,4,6,128,128]{5,4,3,2,1,0:T(8,128)(2,1)S(1)} %bitcast.5, f32[2,4,6,128,128]{4,3,2,1,0:T(8,128)S(1)} %coef.1.coef_ref, f32[2,4,128,256]{3,2,1,0:T(8,128)S(1)} %copy-done.2, ...), custom_call_target="tpu_custom_call" | custom-call | flops 805306368 | bytes 1048576 | tf_op jit(solution)/shard_map/edge_last/pallas_call | solution.py:24
  64.3 3.1 %collective-permute-start.26 = (bf16[2,2,128,256]{3,2,1,0:T(8,128)(2,1)}, bf16[2,2,128,256]{3,2,1,0:T(8,128)(2,1)S(1)}, u32[]{:S(2)}, u32[]{:S(2)}) collective-permute-start(bf16[2,2,128,256]{3,2,1,0:T(8,128)(2,1)} %get-tuple-element.61), channel_id=1, source_target_pairs={{0,8},{2,10},{4,12},{6,14},{8,0},{10,2},{12,4},{14,6},{1,9},{3,11}... | collective-permute-start | bytes 786440 | tf_op jit(solution)/shard_map/ppermute | solution.py:308
  67.5 3.4 %collective-permute-start.37 = (bf16[2,2,128,256]{3,2,1,0:T(8,128)(2,1)}, bf16[2,2,128,256]{3,2,1,0:T(8,128)(2,1)S(1)}, u32[]{:S(2)}, u32[]{:S(2)}) collective-permute-start(bf16[2,2,128,256]{3,2,1,0:T(8,128)(2,1)} %get-tuple-element.61), channel_id=1, source_target_pairs={{0,6},{6,0},{8,14},{14,8},{1,7},{7,1},{9,15},{15,9},{16,22},{22,16... | collective-permute-start | bytes 786440 | tf_op jit(solution)/shard_map/ppermute | solution.py:307
  70.8 5.3 %collective-permute-done.24.refs_4_ = bf16[2,2,128,256]{3,2,1,0:T(8,128)(2,1)S(1)} collective-permute-done((bf16[2,2,128,256]{3,2,1,0:T(8,128)(2,1)}, bf16[2,2,128,256]{3,2,1,0:T(8,128)(2,1)S(1)}, u32[]{:S(2)}, u32[]{:S(2)}) %collective-permute-start.24) | collective-permute-done | bytes 262176 | tf_op jit(solution)/shard_map/ppermute | solution.py:308
  78.9 2.8 %collective-permute-done.26.refs_5_ = bf16[2,2,128,256]{3,2,1,0:T(8,128)(2,1)S(1)} collective-permute-done((bf16[2,2,128,256]{3,2,1,0:T(8,128)(2,1)}, bf16[2,2,128,256]{3,2,1,0:T(8,128)(2,1)S(1)}, u32[]{:S(2)}, u32[]{:S(2)}) %collective-permute-start.26) | collective-permute-done | bytes 262176 | tf_op jit(solution)/shard_map/ppermute | solution.py:308
  81.7 3.7 %collective-permute-done.37.refs_13_ = bf16[2,2,128,256]{3,2,1,0:T(8,128)(2,1)S(1)} collective-permute-done((bf16[2,2,128,256]{3,2,1,0:T(8,128)(2,1)}, bf16[2,2,128,256]{3,2,1,0:T(8,128)(2,1)S(1)}, u32[]{:S(2)}, u32[]{:S(2)}) %collective-permute-start.37) | collective-permute-done | bytes 262176 | tf_op jit(solution)/shard_map/ppermute | solution.py:307
  86.7 3.0 %collective-permute-done.25.refs_0_ = bf16[2,2,128,256]{3,2,1,0:T(8,128)(2,1)S(1)} collective-permute-done((bf16[2,2,128,256]{3,2,1,0:T(8,128)(2,1)S(1)}, bf16[2,2,128,256]{3,2,1,0:T(8,128)(2,1)S(1)}, u32[]{:S(2)}, u32[]{:S(2)}) %collective-permute-start.25) | collective-permute-done | bytes 262176 | tf_op jit(solution)/shard_map/ppermute | solution.py:309
  95.2 5.8 %collective-permute-done.33.refs_9_ = bf16[2,2,128,256]{3,2,1,0:T(8,128)(2,1)S(1)} collective-permute-done((bf16[2,2,128,256]{3,2,1,0:T(8,128)(2,1)S(1)}, bf16[2,2,128,256]{3,2,1,0:T(8,128)(2,1)S(1)}, u32[]{:S(2)}, u32[]{:S(2)}) %collective-permute-start.33) | collective-permute-done | bytes 262176 | tf_op jit(solution)/shard_map/ppermute | solution.py:310
  102.6 3.8 %ocean.1 = bf16[32,128,256]{2,1,0:T(8,128)(2,1)} custom-call(s32[66]{0:T(128)S(1)} %pad_add_fusion.1.scalar_ref, bf16[32,128,256]{2,1,0:T(8,128)(2,1)S(1)} %turn_interp.1.interp_ref, bf16[2,2,128,256]{3,2,1,0:T(8,128)(2,1)S(1)} %collective-permute-done.25.refs_0_, bf16[2,2,128,256]{3,2,1,0:T(8,128)(2,1)S(1)} %collective-permute-done.27.refs_1_, ...), custom_call_target="tpu_custom_call" | custom-call | tf_op jit(solution)/shard_map/ocean/pallas_call | solution.py:331
  (109 shorter events, 27.8 us)
Async XLA Ops:
  2.6 9.7 %collective-permute-start.2 = (bf16[2,1,128,256]{3,2,1,0:T(8,128)(2,1)S(1)}, bf16[2,1,128,256]{3,2,1,0:T(8,128)(2,1)}, u32[]{:S(2)}, u32[]{:S(2)}) collective-permute-start(bf16[2,1,128,256]{3,2,1,0:T(8,128)(2,1)S(1)} %get-tuple-element.34.refs_2_), channel_id=1, source_target_pairs={{0,2},{2,4},{4,6},{6,8},{8,10},{10,12},{12,14},{14,0},{1,3},{3,5},... | collective-permute-start | bytes 393224 | tf_op jit(solution)/shard_map/ppermute | solution.py:248
  6.2 7.9 %collective-permute-start.3 = (bf16[2,1,128,256]{3,2,1,0:T(8,128)(2,1)S(1)}, bf16[2,1,128,256]{3,2,1,0:T(8,128)(2,1)}, u32[]{:S(2)}, u32[]{:S(2)}) collective-permute-start(bf16[2,1,128,256]{3,2,1,0:T(8,128)(2,1)S(1)} %get-tuple-element.33.refs_1_), channel_id=1, source_target_pairs={{2,0},{4,2},{6,4},{8,6},{10,8},{12,10},{14,12},{0,14},{3,1},{5,3},... | collective-permute-start | bytes 393224 | tf_op jit(solution)/shard_map/ppermute | solution.py:249
  9.3 6.9 %collective-permute-start = (bf16[1,2,128,256]{3,2,1,0:T(8,128)(2,1)}, bf16[1,2,128,256]{3,2,1,0:T(8,128)(2,1)}, u32[]{:S(2)}, u32[]{:S(2)}) collective-permute-start(bf16[1,2,128,256]{3,2,1,0:T(8,128)(2,1)} %get-tuple-element.35), channel_id=1, source_target_pairs={{0,1},{1,0},{2,3},{3,2},{4,5},{5,4},{6,7},{7,6},{8,9},{9,8},{10,11... | collective-permute-start | bytes 393224 | tf_op jit(solution)/shard_map/ppermute | solution.py:242
  22.1 8.8 %collective-permute-start.8 = (bf16[2,1,128,256]{3,2,1,0:T(8,128)(2,1)S(1)}, bf16[2,1,128,256]{3,2,1,0:T(8,128)(2,1)S(1)}, u32[]{:S(2)}, u32[]{:S(2)}) collective-permute-start(bf16[2,1,128,256]{3,2,1,0:T(8,128)(2,1)S(1)} %get-tuple-element.40.refs_3_), channel_id=1, source_target_pairs={{0,2},{2,4},{4,6},{6,8},{8,10},{10,12},{12,14},{14,0},{1,3},{3,5},... | collective-permute-start | bytes 393224 | tf_op jit(solution)/shard_map/ppermute | solution.py:248
  22.2 8.8 %collective-permute-start.9 = (bf16[2,1,128,256]{3,2,1,0:T(8,128)(2,1)S(1)}, bf16[2,1,128,256]{3,2,1,0:T(8,128)(2,1)S(1)}, u32[]{:S(2)}, u32[]{:S(2)}) collective-permute-start(bf16[2,1,128,256]{3,2,1,0:T(8,128)(2,1)S(1)} %get-tuple-element.39.refs_2_), channel_id=1, source_target_pairs={{2,0},{4,2},{6,4},{8,6},{10,8},{12,10},{14,12},{0,14},{3,1},{5,3},... | collective-permute-start | bytes 393224 | tf_op jit(solution)/shard_map/ppermute | solution.py:249
  34.4 8.6 %collective-permute-start.14 = (bf16[2,1,128,256]{3,2,1,0:T(8,128)(2,1)S(1)}, bf16[2,1,128,256]{3,2,1,0:T(8,128)(2,1)S(1)}, u32[]{:S(2)}, u32[]{:S(2)}) collective-permute-start(bf16[2,1,128,256]{3,2,1,0:T(8,128)(2,1)S(1)} %get-tuple-element.47.refs_3_), channel_id=1, source_target_pairs={{0,2},{2,4},{4,6},{6,8},{8,10},{10,12},{12,14},{14,0},{1,3},{3,5},... | collective-permute-start | bytes 393224 | tf_op jit(solution)/shard_map/ppermute | solution.py:248
  34.8 8.8 %collective-permute-start.15 = (bf16[2,1,128,256]{3,2,1,0:T(8,128)(2,1)S(1)}, bf16[2,1,128,256]{3,2,1,0:T(8,128)(2,1)S(1)}, u32[]{:S(2)}, u32[]{:S(2)}) collective-permute-start(bf16[2,1,128,256]{3,2,1,0:T(8,128)(2,1)S(1)} %get-tuple-element.46.refs_2_), channel_id=1, source_target_pairs={{2,0},{4,2},{6,4},{8,6},{10,8},{12,10},{14,12},{0,14},{3,1},{5,3},... | collective-permute-start | bytes 393224 | tf_op jit(solution)/shard_map/ppermute | solution.py:249
  45.6 7.4 %collective-permute-start.19 = (bf16[1,2,128,256]{3,2,1,0:T(8,128)(2,1)S(1)}, bf16[1,2,128,256]{3,2,1,0:T(8,128)(2,1)S(1)}, u32[]{:S(2)}, u32[]{:S(2)}) collective-permute-start(bf16[1,2,128,256]{3,2,1,0:T(8,128)(2,1)S(1)} %get-tuple-element.56), channel_id=1, source_target_pairs={{0,1},{1,0},{2,3},{3,2},{4,5},{5,4},{6,7},{7,6},{8,9},{9,8},{10,11... | collective-permute-start | bytes 393224 | tf_op jit(solution)/shard_map/ppermute | solution.py:242
  48.2 9.0 %collective-permute-start.20 = (bf16[2,1,128,256]{3,2,1,0:T(8,128)(2,1)S(1)}, bf16[2,1,128,256]{3,2,1,0:T(8,128)(2,1)S(1)}, u32[]{:S(2)}, u32[]{:S(2)}) collective-permute-start(bf16[2,1,128,256]{3,2,1,0:T(8,128)(2,1)S(1)} %get-tuple-element.54.refs_5_), channel_id=1, source_target_pairs={{0,2},{2,4},{4,6},{6,8},{8,10},{10,12},{12,14},{14,0},{1,3},{3,5},... | collective-permute-start | bytes 393224 | tf_op jit(solution)/shard_map/ppermute | solution.py:248
  48.3 9.5 %collective-permute-start.21 = (bf16[2,1,128,256]{3,2,1,0:T(8,128)(2,1)S(1)}, bf16[2,1,128,256]{3,2,1,0:T(8,128)(2,1)S(1)}, u32[]{:S(2)}, u32[]{:S(2)}) collective-permute-start(bf16[2,1,128,256]{3,2,1,0:T(8,128)(2,1)S(1)} %get-tuple-element.53.refs_4_), channel_id=1, source_target_pairs={{2,0},{4,2},{6,4},{8,6},{10,8},{12,10},{14,12},{0,14},{3,1},{5,3},... | collective-permute-start | bytes 393224 | tf_op jit(solution)/shard_map/ppermute | solution.py:249
  56.5 19.6 %collective-permute-start.24 = (bf16[2,2,128,256]{3,2,1,0:T(8,128)(2,1)}, bf16[2,2,128,256]{3,2,1,0:T(8,128)(2,1)S(1)}, u32[]{:S(2)}, u32[]{:S(2)}) collective-permute-start(bf16[2,2,128,256]{3,2,1,0:T(8,128)(2,1)} %get-tuple-element.60), channel_id=1, source_target_pairs={{0,8},{2,10},{4,12},{6,14},{8,0},{10,2},{12,4},{14,6},{1,9},{3,11}... | collective-permute-start | bytes 786440 | tf_op jit(solution)/shard_map/ppermute | solution.py:308
  57.8 19.7 %collective-permute-start.36 = (bf16[2,2,128,256]{3,2,1,0:T(8,128)(2,1)}, bf16[2,2,128,256]{3,2,1,0:T(8,128)(2,1)}, u32[]{:S(2)}, u32[]{:S(2)}) collective-permute-start(bf16[2,2,128,256]{3,2,1,0:T(8,128)(2,1)} %get-tuple-element.60), channel_id=1, source_target_pairs={{0,6},{6,0},{8,14},{14,8},{1,7},{7,1},{9,15},{15,9},{16,22},{22,16... | collective-permute-start | bytes 786440 | tf_op jit(solution)/shard_map/ppermute | solution.py:307
  64.3 17.4 %collective-permute-start.26 = (bf16[2,2,128,256]{3,2,1,0:T(8,128)(2,1)}, bf16[2,2,128,256]{3,2,1,0:T(8,128)(2,1)S(1)}, u32[]{:S(2)}, u32[]{:S(2)}) collective-permute-start(bf16[2,2,128,256]{3,2,1,0:T(8,128)(2,1)} %get-tuple-element.61), channel_id=1, source_target_pairs={{0,8},{2,10},{4,12},{6,14},{8,0},{10,2},{12,4},{14,6},{1,9},{3,11}... | collective-permute-start | bytes 786440 | tf_op jit(solution)/shard_map/ppermute | solution.py:308
  67.5 17.9 %collective-permute-start.37 = (bf16[2,2,128,256]{3,2,1,0:T(8,128)(2,1)}, bf16[2,2,128,256]{3,2,1,0:T(8,128)(2,1)S(1)}, u32[]{:S(2)}, u32[]{:S(2)}) collective-permute-start(bf16[2,2,128,256]{3,2,1,0:T(8,128)(2,1)} %get-tuple-element.61), channel_id=1, source_target_pairs={{0,6},{6,0},{8,14},{14,8},{1,7},{7,1},{9,15},{15,9},{16,22},{22,16... | collective-permute-start | bytes 786440 | tf_op jit(solution)/shard_map/ppermute | solution.py:307
  76.2 13.5 %collective-permute-start.25 = (bf16[2,2,128,256]{3,2,1,0:T(8,128)(2,1)S(1)}, bf16[2,2,128,256]{3,2,1,0:T(8,128)(2,1)S(1)}, u32[]{:S(2)}, u32[]{:S(2)}) collective-permute-start(bf16[2,2,128,256]{3,2,1,0:T(8,128)(2,1)S(1)} %collective-permute-done.24.refs_4_), channel_id=1, source_target_pairs={{0,2},{2,4},{4,6},{8,10},{10,12},{12,14},{1,3},{3,5},{5,7},{9,11},... | collective-permute-start | bytes 786440 | tf_op jit(solution)/shard_map/ppermute | solution.py:309
  77.5 12.2 %collective-permute-start.30 = (bf16[2,2,128,256]{3,2,1,0:T(8,128)(2,1)S(1)}, bf16[2,2,128,256]{3,2,1,0:T(8,128)(2,1)S(1)}, u32[]{:S(2)}, u32[]{:S(2)}) collective-permute-start(bf16[2,2,128,256]{3,2,1,0:T(8,128)(2,1)S(1)} %collective-permute-done.24.refs_4_), channel_id=1, source_target_pairs={{0,1},{1,0},{2,3},{3,2},{4,5},{5,4},{6,7},{7,6},{8,9},{9,8},{10,11... | collective-permute-start | bytes 786440 | tf_op jit(solution)/shard_map/ppermute | solution.py:242
  77.6 16.0 %collective-permute-start.32 = (bf16[2,2,128,256]{3,2,1,0:T(8,128)(2,1)S(1)}, bf16[2,2,128,256]{3,2,1,0:T(8,128)(2,1)S(1)}, u32[]{:S(2)}, u32[]{:S(2)}) collective-permute-start(bf16[2,2,128,256]{3,2,1,0:T(8,128)(2,1)S(1)} %collective-permute-done.24.refs_4_), channel_id=1, source_target_pairs={{2,0},{4,2},{6,4},{10,8},{12,10},{14,12},{3,1},{5,3},{7,5},{11,9},... | collective-permute-start | bytes 786440 | tf_op jit(solution)/shard_map/ppermute | solution.py:310
  81.7 12.4 %collective-permute-start.38 = (bf16[2,2,128,256]{3,2,1,0:T(8,128)(2,1)}, bf16[2,2,128,256]{3,2,1,0:T(8,128)(2,1)S(1)}, u32[]{:S(2)}, u32[]{:S(2)}) collective-permute-start(bf16[2,2,128,256]{3,2,1,0:T(8,128)(2,1)} %collective-permute-done.36.refs_12_), channel_id=1, source_target_pairs={{0,1},{1,0},{2,3},{3,2},{4,5},{5,4},{6,7},{7,6},{8,9},{9,8},{10,11... | collective-permute-start | bytes 786440 | tf_op jit(solution)/shard_map/ppermute | solution.py:242
  85.4 9.3 %collective-permute-start.27 = (bf16[2,2,128,256]{3,2,1,0:T(8,128)(2,1)S(1)}, bf16[2,2,128,256]{3,2,1,0:T(8,128)(2,1)S(1)}, u32[]{:S(2)}, u32[]{:S(2)}) collective-permute-start(bf16[2,2,128,256]{3,2,1,0:T(8,128)(2,1)S(1)} %collective-permute-done.26.refs_5_), channel_id=1, source_target_pairs={{0,2},{2,4},{4,6},{8,10},{10,12},{12,14},{1,3},{3,5},{5,7},{9,11},... | collective-permute-start | bytes 786440 | tf_op jit(solution)/shard_map/ppermute | solution.py:309
  89.7 11.3 %collective-permute-start.33 = (bf16[2,2,128,256]{3,2,1,0:T(8,128)(2,1)S(1)}, bf16[2,2,128,256]{3,2,1,0:T(8,128)(2,1)S(1)}, u32[]{:S(2)}, u32[]{:S(2)}) collective-permute-start(bf16[2,2,128,256]{3,2,1,0:T(8,128)(2,1)S(1)} %collective-permute-done.26.refs_5_), channel_id=1, source_target_pairs={{2,0},{4,2},{6,4},{10,8},{12,10},{14,12},{3,1},{5,3},{7,5},{11,9},... | collective-permute-start | bytes 786440 | tf_op jit(solution)/shard_map/ppermute | solution.py:310
  93.6 8.6 %collective-permute-start.39 = (bf16[2,2,128,256]{3,2,1,0:T(8,128)(2,1)S(1)}, bf16[2,2,128,256]{3,2,1,0:T(8,128)(2,1)S(1)}, u32[]{:S(2)}, u32[]{:S(2)}) collective-permute-start(bf16[2,2,128,256]{3,2,1,0:T(8,128)(2,1)S(1)} %collective-permute-done.37.refs_13_), channel_id=1, source_target_pairs={{0,1},{1,0},{2,3},{3,2},{4,5},{5,4},{6,7},{7,6},{8,9},{9,8},{10,11... | collective-permute-start | bytes 786440 | tf_op jit(solution)/shard_map/ppermute | solution.py:242
  94.1 8.0 %collective-permute-start.28 = (bf16[2,2,128,256]{3,2,1,0:T(8,128)(2,1)S(1)}, bf16[2,2,128,256]{3,2,1,0:T(8,128)(2,1)S(1)}, u32[]{:S(2)}, u32[]{:S(2)}) collective-permute-start(bf16[2,2,128,256]{3,2,1,0:T(8,128)(2,1)S(1)} %collective-permute-done.25.refs_0_), channel_id=1, source_target_pairs={{0,1},{1,0},{2,3},{3,2},{4,5},{5,4},{6,7},{7,6},{8,9},{9,8},{10,11... | collective-permute-start | bytes 786440 | tf_op jit(solution)/shard_map/ppermute | solution.py:242
  94.7 7.5 %collective-permute-start.34 = (bf16[2,2,128,256]{3,2,1,0:T(8,128)(2,1)S(1)}, bf16[2,2,128,256]{3,2,1,0:T(8,128)(2,1)S(1)}, u32[]{:S(2)}, u32[]{:S(2)}) collective-permute-start(bf16[2,2,128,256]{3,2,1,0:T(8,128)(2,1)S(1)} %collective-permute-done.32.refs_8_), channel_id=1, source_target_pairs={{0,1},{1,0},{2,3},{3,2},{4,5},{5,4},{6,7},{7,6},{8,9},{9,8},{10,11... | collective-permute-start | bytes 786440 | tf_op jit(solution)/shard_map/ppermute | solution.py:242
  94.7 7.5 %collective-permute-start.29 = (bf16[2,2,128,256]{3,2,1,0:T(8,128)(2,1)S(1)}, bf16[2,2,128,256]{3,2,1,0:T(8,128)(2,1)S(1)}, u32[]{:S(2)}, u32[]{:S(2)}) collective-permute-start(bf16[2,2,128,256]{3,2,1,0:T(8,128)(2,1)S(1)} %collective-permute-done.27.refs_1_), channel_id=1, source_target_pairs={{0,1},{1,0},{2,3},{3,2},{4,5},{5,4},{6,7},{7,6},{8,9},{9,8},{10,11... | collective-permute-start | bytes 786440 | tf_op jit(solution)/shard_map/ppermute | solution.py:242
  (31 other events, 192.5 us)

commit v3 on v0

v3 whole, which is shorter than its diff:
```python
import functools

import jax
import jax.numpy as jnp
from jax import lax
from jax.experimental import pallas as pl
from jax.experimental.pallas import tpu as pltpu
from jax.sharding import PartitionSpec as P

CORIOLIS = 2.0
STEP_SIZE = 0.2
BF16 = jnp.bfloat16
F32 = jnp.float32
VMEM = pl.BlockSpec(memory_space=pltpu.VMEM)
HBM = pl.BlockSpec(memory_space=pltpu.HBM)
MIB = 1024 * 1024


def in_vmem(value):
    return pltpu.with_memory_space_constraint(value, pltpu.VMEM)


def in_hbm(value):
    return pltpu.with_memory_space_constraint(value, pltpu.HBM)


def vmem_call(kernel, name, outs, arrays, scratch=(), limit=4, aliases=None):
    return pl.pallas_call(
        kernel,
        out_shape=[pltpu.VMEM(shape, dtype) for shape, dtype in outs],
        in_specs=[VMEM] * len(arrays),
        out_specs=[VMEM] * len(outs),
        scratch_shapes=list(scratch),
        compiler_params=pltpu.CompilerParams(vmem_limit_bytes=limit * MIB),
        cost_estimate=pl.CostEstimate(flops=1000, bytes_accessed=1000, transcendentals=0),
        input_output_aliases=aliases or {},
        name=name,
    )(*[in_vmem(array) for array in arrays])


def after(value, *others):
    return lax.optimization_barrier((value,) + others)[0]


def prep_kernel(scalar_ref, state_ref, inner_ref, irow_ref, edge_a_ref, edge_b_ref, erow_ref):
    rows, cols = state_ref.shape[:2]
    for a in range(rows):
        edge_a_ref[a, 0] = state_ref[a, scalar_ref[0, 1]].astype(BF16)
        edge_b_ref[a, 0] = state_ref[a, scalar_ref[0, cols]].astype(BF16)
        for c in range(1, cols - 1):
            inner_ref[a, c - 1] = state_ref[a, scalar_ref[0, 1 + c]].astype(BF16)
    send = scalar_ref[0, 0]
    irow_ref[0] = inner_ref[send]
    erow_ref[0, 0] = edge_a_ref[send, 0]
    erow_ref[0, 1] = edge_b_ref[send, 0]


def setup_kernel(scalar_ref, pos_ref, w_ref, coef_ref, inner_ref, edge_ref, sems):
    copies = []
    for c in range(pos_ref.shape[2]):
        on_edge = c in (0, pos_ref.shape[2] - 1)
        target, place = (edge_ref, min(c, 1)) if on_edge else (inner_ref, c - 1)
        copies.append(
            pltpu.make_async_copy(
                w_ref.at[:, :, pl.ds(scalar_ref[0, 1 + c], 1)],
                target.at[:, :, pl.ds(place, 1)],
                sems.at[c],
            )
        )
    for copy in copies:
        copy.start()
    rows, cols, nodes = pos_ref.shape[1:]
    low = lax.broadcasted_iota(jnp.int32, (nodes, nodes), 1) < nodes // 2
    for a in range(rows):
        for b in range(cols):
            x0, x1, x2 = (
                jnp.broadcast_to(pos_ref[c, a, b][None, :], (nodes, nodes)).T for c in range(3)
            )
            coef_ref[a, b, 0] = jnp.where(low, x0, x1)
            coef_ref[a, b, 1] = x2
    for copy in copies:
        copy.wait()


def turn_kernel(interp_ref, turned_ref, interp, sem):
    copy = pltpu.make_async_copy(interp_ref, interp, sem)
    copy.start()
    copy.wait()
    tiles, taps, nodes, points = interp.shape
    for o in range(tiles):
        turned_ref[o] = interp[o].reshape(taps * nodes, points).T


def turned(value):
    return pltpu.roll(value, value.shape[-1] // 2, axis=1)


def tendency(tile, grads, x01, x2, low):
    half = tile.shape[-1] // 2
    sa, sb = tile[:, :half], tile[:, half:]
    ra, rb = turned(sa), turned(sb)
    v0 = jnp.where(low, sa, ra)
    v1 = jnp.where(low, ra, sa)
    v2 = jnp.where(low, sb, rb)
    ga = [g[:, :half] for g in grads]
    gb = [g[:, half:] for g in grads]
    t0a, t0b, t2b = turned(ga[0]), turned(gb[0]), turned(gb[2])
    x10 = turned(x01)
    spin = CORIOLIS * x2
    cross = spin * (x10 * v2 - x2 * ra)
    fa = (
        ga[3]
        - (v0 * ga[0] + v1 * ga[1] + v2 * ga[2])
        - jnp.where(low, cross + t0b, gb[1] - cross)
    )
    spread = sb * (t0a + ga[1] + t2b)
    fb = (
        gb[3]
        - (v0 * gb[0] + v1 * gb[1] + v2 * gb[2])
        - jnp.where(low, spin * (x01 * v1 - x10 * v0) + t2b, spread)
    )
    x2_low = jnp.where(low, x2, 0.0)
    part = x01 * fa + x2_low * fb
    radial = part + turned(part)
    return fa - x01 * radial, fb - x2_low * radial


def stage_kernel(edge, number, stages, scale, scalar_ref, w_ref, coef_ref, *refs):
    refs = list(refs)
    ext = refs.pop()
    rows, cols = coef_ref.shape[:2]
    nodes, feats = ext.shape[1:]
    taps = w_ref.shape[3]
    wide = cols + 2
    last = number == stages - 1
    blend = number == stages - 2
    state_ref = None if last else refs.pop(0)
    sum_ref = refs.pop(0) if last or blend else None
    now_ref = refs.pop(0) if number else None
    inner_ref, irow_ref, edge_a_ref, edge_b_ref, erow_ref = refs[:5]
    refs = refs[5:]
    send = scalar_ref[0, 0]
    for a in range(rows):
        ext[a * wide + 1] = edge_a_ref[a, 0]
        ext[a * wide + cols] = edge_b_ref[a, 0]
        ext[pl.ds(a * wide + 2, cols - 2)] = inner_ref[a]
    ext[rows * wide + 1] = erow_ref[0, 0]
    ext[rows * wide + cols] = erow_ref[0, 1]
    ext[pl.ds(rows * wide + 2, cols - 2)] = irow_ref[0]
    if edge:
        halo_a_ref, halo_b_ref, corner_a_ref, corner_b_ref = refs[:4]
        refs = refs[4:]
        for a in range(rows):
            ext[a * wide] = halo_a_ref[a, 0]
            ext[a * wide + cols + 1] = halo_b_ref[a, 0]
        ext[rows * wide] = corner_a_ref[1 - send, 0]
        ext[rows * wide + cols + 1] = corner_b_ref[1 - send, 0]
    blend_ref = refs.pop(0) if blend else None
    next_ref, *outs = refs
    columns = (0, cols - 1) if edge else tuple(range(1, cols - 1))
    low = lax.broadcasted_iota(jnp.int32, (nodes, feats // 2), 1) < feats // 4
    for a in range(rows):
        for place, c in enumerate(columns):
            b = scalar_ref[0, 1 + c]
            base = 1 + cols + (a * cols + c) * taps
            near = jnp.concatenate([ext[scalar_ref[0, base + k]] for k in range(taps)], axis=0)
            weights = jnp.concatenate(
                [
                    jnp.concatenate([w_ref[q, a, place, k] for k in range(taps)], axis=1)
                    for q in range(4)
                ],
                axis=0,
            )
            derivs = jnp.dot(weights, near, preferred_element_type=F32)
            grads = [derivs[q * nodes : (q + 1) * nodes] for q in range(4)]
            now = now_ref[a, place] if number else state_ref[a, b]
            x01, x2 = coef_ref[a, b, 0], coef_ref[a, b, 1]
            rate = jnp.concatenate(tendency(now, grads, x01, x2, low), axis=1)
            out = (sum_ref[a, place] if last else state_ref[a, b]) + scale * rate
            if blend:
                blend_ref[a, place] = (1.0 / 3.0) * (
                    sum_ref[a, place] + 2.0 * now + out - state_ref[a, b]
                )
            next_ref[a, place] = out
            rounded = out.astype(BF16)
            if edge and not last:
                outs[place][a, 0] = rounded
            else:
                outs[0][a, place] = rounded
    if not last:
        if edge:
            outs[2][0, 0] = outs[0][send, 0]
            outs[2][0, 1] = outs[1][send, 0]
        else:
            outs[1][0] = outs[0][send]


def join_kernel(scalar_ref, inner_ref, edge_ref, out_ref):
    rows, cols = out_ref.shape[:2]
    for a in range(rows):
        for c in range(cols):
            source = edge_ref[a, c // (cols - 1)] if c in (0, cols - 1) else inner_ref[a, c - 1]
            out_ref[a, scalar_ref[0, 1 + c]] = source


def pick_kernel(flag, scalar_ref, first_ref, *refs):
    count = len(refs) // 2
    for i in range(count):
        refs[count + i][...] = jnp.where(
            scalar_ref[0, flag + i] == 1, first_ref[...], refs[i][...]
        )


def collect_kernel(places, *refs):
    pieces, out_ref = refs[-1 - len(places) : -1], refs[-1]
    for place, piece in zip(places, pieces):
        flat = piece.reshape(piece.shape[0] * piece.shape[1], *piece.shape[2:])
        out_ref[pl.ds(place, flat.shape[0])] = flat[...]


def ocean_kernel(scalar_ref, interp_ref, tiles_ref, out_ref):
    block = out_ref.shape[0]
    taps = scalar_ref.shape[1]
    first = pl.program_id(0) * block
    for o in range(block):
        near = jnp.concatenate(
            [tiles_ref[scalar_ref[first + o, j]] for j in range(taps)], axis=0
        )
        out_ref[o] = jnp.dot(interp_ref[first + o], near, preferred_element_type=F32).astype(BF16)


def local(state, weights, positions, stencil_codes, ovl_owner, ovl_local, interp):
    rows, cols, nodes, feats = state.shape
    taps = stencil_codes.shape[-1]
    lon_count = lax.axis_size("lon")
    lat_count = lax.axis_size("lat")
    my_lon = lax.axis_index("lon")
    my_lat = lax.axis_index("lat")
    to_a = [(i, i ^ 1) for i in range(lon_count)]
    to_b = [(i, (i + 1 if i % 2 else i - 1) % lon_count) for i in range(lon_count)]
    swap = [(i, lat_count - 1 - i) for i in range(lat_count)]

    def flip(value):
        return lax.ppermute(value, "lat", swap)

    a_is_east = my_lon % 2 == 0
    tile_row = lax.broadcasted_iota(jnp.int32, stencil_codes.shape, 0)
    tile_col = lax.broadcasted_iota(jnp.int32, stencil_codes.shape, 1)
    near_col = tile_col + stencil_codes % 3 - 1
    ext_row = tile_row + stencil_codes // 3 - 1
    ext_row = jnp.where(ext_row < 0, rows, ext_row)
    ext_col = jnp.where(a_is_east, cols - 1 - near_col, near_col)
    index = ext_row * (cols + 2) + ext_col + 1
    index = jnp.where(a_is_east, index[:, ::-1], index)
    order = jnp.arange(cols, dtype=jnp.int32)
    order = jnp.where(a_is_east, cols - 1 - order, order)
    send = (1 - my_lat).astype(jnp.int32).reshape(1)

    def as_row(parts):
        flat = jnp.concatenate([part.reshape(-1).astype(jnp.int32) for part in parts])
        return jnp.pad(flat, (0, -flat.size % 128)).reshape(1, -1)

    middle = lon_count // 2
    in_half = my_lon % middle
    ocean_dev, intersections = ovl_local.shape
    target = (my_lon + middle) % lon_count
    owners = ovl_owner.reshape(ocean_dev, intersections)
    owner_lon = owners // lat_count
    relative = (owner_lon - target + 1 + lon_count) % lon_count
    kind = jnp.where(relative == 1, 0, jnp.where((relative == 2) == a_is_east, 1, 2))
    away = (owners % lat_count != my_lat).astype(jnp.int32)
    owner_row, owner_col = ovl_local // cols, ovl_local % cols
    owner_col = jnp.where(owner_lon % 2 == 0, cols - 1 - owner_col, owner_col)
    inner_count = rows * (cols - 2)
    inner_slot = (kind * 2 + away) * inner_count + owner_row * (cols - 2) + owner_col - 1
    edge_slot = 6 * inner_count + (relative * 2 + away) * (2 * rows)
    edge_slot += 2 * owner_row + (owner_col != 0)
    slot = jnp.where((owner_col == 0) | (owner_col == cols - 1), edge_slot, inner_slot)

    turns = (in_half == middle - 2) | (in_half == 1)
    scalars = as_row([send, order, index, turns, in_half == middle - 1, in_half == 0])
    flags = 1 + cols + index.size

    tile = (nodes, feats)
    inner_s = ((rows, cols - 2) + tile, BF16)
    irow_s = ((1, cols - 2) + tile, BF16)
    edge_s = ((rows, 1) + tile, BF16)
    erow_s = ((1, 2) + tile, BF16)

    own = vmem_call(
        prep_kernel,
        "prep",
        [inner_s, irow_s, edge_s, edge_s, erow_s],
        [as_row([send, order]), state],
    )

    quarter = weights.shape[:2]
    coef, w_inner, w_edge = pl.pallas_call(
        setup_kernel,
        out_shape=[
            pltpu.VMEM((rows, cols, 2, nodes, nodes), F32),
            pltpu.VMEM(quarter + (cols - 2,) + weights.shape[3:], BF16),
            pltpu.VMEM(quarter + (2,) + weights.shape[3:], BF16),
        ],
        in_specs=[VMEM, VMEM, HBM],
        out_specs=[VMEM] * 3,
        scratch_shapes=[pltpu.SemaphoreType.DMA((cols,))],
        compiler_params=pltpu.CompilerParams(vmem_limit_bytes=4 * MIB),
        name="setup",
    )(in_vmem(scalars), in_vmem(after(positions, slot)), in_hbm(weights))
    scales = (0.5 * STEP_SIZE, 0.5 * STEP_SIZE, STEP_SIZE, STEP_SIZE / 6.0)
    stages = len(scales)

    fields = {False: [], True: []}
    for number, scale in enumerate(scales):
        last = number == stages - 1
        blend = number == stages - 2
        inner, irow, edge_a, edge_b, erow = own
        halo_a = lax.ppermute(edge_a, "lon", to_a)
        halo_b = lax.ppermute(edge_b, "lon", to_b)
        if number == 0:
            halo_a = after(halo_a, w_edge)
        near = [inner, flip(irow), edge_a, edge_b, flip(erow)]
        far = [halo_a, halo_b, flip(halo_a), flip(halo_b)]
        own = []
        for edge in (False, True):
            field_s = ((rows, 2 if edge else cols - 2) + tile, F32)
            outs = [edge_s, edge_s, erow_s] if edge else [inner_s, irow_s]
            if last:
                outs = [((rows, 2 if edge else cols - 2) + tile, BF16)]
            outs = ([field_s] if blend else []) + [field_s] + outs
            results = vmem_call(
                functools.partial(stage_kernel, edge, number, stages, scale),
                ("edge" if edge else "inner") + ("_last" if last else ""),
                outs,
                [scalars, w_edge if edge else w_inner, coef]
                + ([] if last else [state])
                + fields[edge]
                + near
                + (far if edge else []),
                [pltpu.VMEM(((rows + 1) * (cols + 2),) + tile, BF16)],
            )
            if blend:
                fields[edge], results = list(results[:2]), results[2:]
            else:
                fields[edge], results = (fields[edge] + [results[0]])[-2:], results[1:]
            own += results
    next_i, next_e = fields[False][-1], fields[True][-1]
    final_i, final_e = own

    (next_state,) = pl.pallas_call(
        join_kernel,
        out_shape=[jax.ShapeDtypeStruct(state.shape, F32)],
        in_specs=[VMEM] * 3,
        out_specs=[VMEM],
        compiler_params=pltpu.CompilerParams(vmem_limit_bytes=4 * MIB),
        name="join",
    )(scalars, next_i, next_e)
    turned_interp = pl.pallas_call(
        turn_kernel,
        out_shape=pltpu.VMEM((ocean_dev, nodes, intersections * nodes), BF16),
        in_specs=[HBM],
        out_specs=VMEM,
        scratch_shapes=[pltpu.VMEM(interp.shape, BF16), pltpu.SemaphoreType.DMA(())],
        compiler_params=pltpu.CompilerParams(vmem_limit_bytes=4 * MIB),
        name="turn_interp",
    )(in_hbm(after(interp, next_e)))

    opposite = [(i, (i + middle) % lon_count) for i in range(lon_count)]

    def within_half(step):
        return [(i, i - i % middle + (i + step(i)) % middle) for i in range(lon_count)]

    up, down = within_half(lambda i: 1), within_half(lambda i: -1)
    onward = within_half(lambda i: -2 if i % 2 else 2)

    def pick(flag, *pieces):
        return vmem_call(
            functools.partial(pick_kernel, flag),
            "pick",
            [(pieces[0].shape, BF16)] * (len(pieces) - 1),
            [scalars, *pieces],
        )

    def collect(tiles, place, pieces):
        size = pieces[0].shape[0] * pieces[0].shape[1]
        return vmem_call(
            functools.partial(collect_kernel, [place + i * size for i in range(len(pieces))]),
            "collect",
            [((6 * rows * cols,) + tile, BF16)],
            ([] if tiles is None else [tiles]) + pieces,
            aliases=None if tiles is None else {0: 0},
        )[0]

    final_i = after(final_i, halo_a, halo_b)
    center_i = lax.ppermute(final_i, "lon", opposite)
    native = lax.ppermute(final_i, "lon", to_a)
    center_e = lax.ppermute(after(final_e, center_i, next_state, turned_interp), "lon", opposite)
    paired = lax.ppermute(after(center_i, native, next_state, turned_interp), "lon", to_a)
    passed = lax.ppermute(pick(flags, native, paired)[0], "lon", onward)
    tiles = collect(
        None, 0, [center_i, flip(center_i), paired, flip(paired), passed, flip(passed)]
    )
    going_up, going_down = pick(flags + 1, final_e, center_e, center_e)
    below = lax.ppermute(going_up, "lon", up)
    above = lax.ppermute(going_down, "lon", down)
    tiles = collect(
        tiles,
        6 * inner_count,
        [below, flip(below), center_e, flip(center_e), above, flip(above)],
    )
    block = 8
    ocean = pl.pallas_call(
        ocean_kernel,
        grid=(ocean_dev // block,),
        out_shape=jax.ShapeDtypeStruct((ocean_dev, nodes, feats), BF16),
        in_specs=[VMEM] * 3,
        out_specs=pl.BlockSpec((block, nodes, feats), lambda g: (g, 0, 0)),
        compiler_params=pltpu.CompilerParams(vmem_limit_bytes=4 * MIB),
        name="ocean",
    )(in_vmem(slot), in_vmem(turned_interp), in_vmem(tiles))
    return next_state, ocean


def solution(mesh):
    placed = (
        P(("member", "lat"), "lon", None, None),
        P(None, "lat", "lon", None, None, None),
        P(None, "lat", "lon", None),
        P("lat", "lon", None),
        P(("lon", "lat"), None, None),
        P(("lon", "lat"), None),
        P(("lon", "lat"), None, None, None),
    )
    return jax.shard_map(
        local,
        mesh=mesh,
        in_specs=placed,
        out_specs=(
            P(("member", "lat"), "lon", None, None),
            P(("member", "lon", "lat"), None, None),
        ),
        check_vma=False,
    )
```

time: 352 us -> 99 us (0.28)
  waiting for transfers between devices: 213 us -> 46.7 us
  local copies, waits for them, and re-layouts: 38.8 us -> 3.67 us
  matrix products: 24.7 us -> 0 us
  Pallas kernels: 0 us -> 22.5 us
  other arithmetic: 22.3 us -> 1.57 us
  starting transfers between devices: 37.8 us -> 23.3 us
  between operations: 14.7 us -> 0.92 us
    ppermute x19 -> x37, waiting for transfers between devices: 205 us -> 46.7 us  [the longest x1 7.64 us: local(): below = lax.ppermute(going_up, 'lon', up)]
    dot_general x5 -> x0, matrix products: 24.7 us -> none  [the longest x4 19.8 us: rate(): jnp.einsum('qabkij,abkjf->qabif', weights, nearby, preferred_element_type...]
    pallas_call x0 -> x17, Pallas kernels: none -> 22.5 us  [the longest x13 13.3 us: vmem_call(): pl.pallas_call(kernel, out_shape=[pltpu.VMEM(shape, dtype) for shape, dty...]
    gather x5 -> x0, local copies, waits for them, and re-layouts: 20.9 us -> none  [the longest x4 16.2 us: rate(): nearby = extended[ext_index]]
    ppermute x19 -> x37, starting transfers between devices: 37.7 us -> 23.3 us  [the longest x4 8.73 us: local(): halo_b = lax.ppermute(edge_b, 'lon', to_b)]
    unnamed x69 -> x7, local copies, waits for them, and re-layouts: 12.9 us -> 2.7 us
    concatenate x10 -> x1, other arithmetic: 9.75 us -> 0.08 us  [as_row(): jnp.concatenate([part.reshape(-1).astype(jnp.int32) for part in parts])]
    all_gather x1 -> x0, waiting for transfers between devices: 8.66 us -> none  [local(): band_pair = lax.all_gather(final_tiles, 'lat', axis=0, tiled=True)]
  transfers between devices with their start and end apart: 20 -> 37, of which waited for: 16 -> 18; matrix products, arithmetic and copies ran while one was open for 2% -> 3% of each run, Pallas kernels for 0% -> 17%
where the time goes in v3:
time: 99 us; the launch traced here: 98.7 us
  waiting for transfers between devices  46.7 us (47%)
  starting transfers between devices  23.3 us (24%)
  Pallas kernels  22.5 us (23%)
  local copies, waits for them, and re-layouts  3.67 us (4%)
  other arithmetic  1.57 us (2%)
    pallas_call x13, Pallas kernels, vmem_call(): pl.pallas_call(kernel, out_shape=[pltpu.VMEM(shape, dtype) for shape, dty...  13.3 us
    ppermute x4, starting transfers between devices, local(): halo_b = lax.ppermute(edge_b, 'lon', to_b)  8.73 us
    ppermute x1, waiting for transfers between devices, local(): below = lax.ppermute(going_up, 'lon', up)  7.64 us
    ppermute x4, waiting for transfers between devices, local(): halo_a = lax.ppermute(edge_a, 'lon', to_a)  7.29 us
    ppermute x1, waiting for transfers between devices, local(): lax.ppermute(after(center_i, native, next_state, turned_interp), 'lon', t...  6.59 us
    ppermute x4, waiting for transfers between devices, local(): halo_b = lax.ppermute(edge_b, 'lon', to_b)  6.3 us
    ppermute x1, waiting for transfers between devices, local(): lax.ppermute(after(final_e, center_i, next_state, turned_interp), 'lon',...  5.11 us
    ppermute x1, waiting for transfers between devices, local(): center_i = lax.ppermute(final_i, 'lon', opposite)  4.83 us
  transfers between devices with their start and end apart: 37, of which 18 were waited for; matrix products, arithmetic and copies ran while one was open for 3% of the time, Pallas kernels for 17%

profile of v3, /device:TPU:0, one launch (start us, length us, event | category | flops | bytes accessed | tf_op | source)
XLA Modules:
  0.0 98.7 jit_solution(5938189647387537615)
XLA Ops:
  2.7 2.9 %collective-permute-start.3 = (bf16[2,1,128,256]{3,2,1,0:T(8,128)(2,1)S(1)}, bf16[2,1,128,256]{3,2,1,0:T(8,128)(2,1)S(1)}, u32[]{:S(2)}, u32[]{:S(2)}) collective-permute-start(bf16[2,1,128,256]{3,2,1,0:T(8,128)(2,1)S(1)} %get-tuple-element.50.refs_3_), channel_id=1, source_target_pairs={{0,2},{2,0},{4,6},{6,4},{8,10},{10,8},{12,14},{14,12},{1,3},{3,1},... | collective-permute-start | bytes 393224 | tf_op jit(solution)/shard_map/ppermute | solution.py:319
  5.7 3.6 %collective-permute-start.4 = (bf16[2,1,128,256]{3,2,1,0:T(8,128)(2,1)S(1)}, bf16[2,1,128,256]{3,2,1,0:T(8,128)(2,1)S(1)}, u32[]{:S(2)}, u32[]{:S(2)}) collective-permute-start(bf16[2,1,128,256]{3,2,1,0:T(8,128)(2,1)S(1)} %get-tuple-element.51.refs_4_), channel_id=1, source_target_pairs={{0,14},{2,4},{4,2},{6,8},{8,6},{10,12},{12,10},{14,0},{1,15},{3,5}... | collective-permute-start | bytes 393224 | tf_op jit(solution)/shard_map/ppermute | solution.py:320
  13.2 3.0 %setup.1 = (f32[2,4,2,128,128]{4,3,2,1,0:T(8,128)S(1)}, bf16[4,2,2,6,128,128]{5,4,3,2,1,0:T(8,128)(2,1)S(1)}, bf16[4,2,2,6,128,128]{5,4,3,2,1,0:T(8,128)(2,1)S(1)}) custom-call(s32[1,128]{1,0:T(1,128)S(1)} %pad_bitcast_fusion.1.scalar_ref, f32[3,2,4,128]{3,2,1,0:T(4,128)S(1)} %copy-done.2, bf16[4,2,4,6,128,128]{5,4,3,2,1,0:T(8,128)(2,1)} %w_ref.1), custom_call_target="tpu_custom_call" | custom-call | tf_op jit(solution)/shard_map/setup/pallas_call | solution.py:298
  19.5 1.9 %collective-permute-start.10 = (bf16[2,1,128,256]{3,2,1,0:T(8,128)(2,1)S(1)}, bf16[2,1,128,256]{3,2,1,0:T(8,128)(2,1)S(1)}, u32[]{:S(2)}, u32[]{:S(2)}) collective-permute-start(bf16[2,1,128,256]{3,2,1,0:T(8,128)(2,1)S(1)} %get-tuple-element.59.refs_5_), channel_id=1, source_target_pairs={{0,14},{2,4},{4,2},{6,8},{8,6},{10,12},{12,10},{14,0},{1,15},{3,5}... | collective-permute-start | bytes 393224 | tf_op jit(solution)/shard_map/ppermute | solution.py:320
  23.5 2.3 %collective-permute-done.9.refs_7_ = bf16[2,1,128,256]{3,2,1,0:T(8,128)(2,1)S(1)} collective-permute-done((bf16[2,1,128,256]{3,2,1,0:T(8,128)(2,1)S(1)}, bf16[2,1,128,256]{3,2,1,0:T(8,128)(2,1)S(1)}, u32[]{:S(2)}, u32[]{:S(2)}) %collective-permute-start.9) | collective-permute-done | bytes 131104 | tf_op jit(solution)/shard_map/ppermute | solution.py:319
  25.8 2.2 %collective-permute-done.10.refs_8_ = bf16[2,1,128,256]{3,2,1,0:T(8,128)(2,1)S(1)} collective-permute-done((bf16[2,1,128,256]{3,2,1,0:T(8,128)(2,1)S(1)}, bf16[2,1,128,256]{3,2,1,0:T(8,128)(2,1)S(1)}, u32[]{:S(2)}, u32[]{:S(2)}) %collective-permute-start.10) | collective-permute-done | bytes 131104 | tf_op jit(solution)/shard_map/ppermute | solution.py:320
  31.4 1.6 %collective-permute-start.16 = (bf16[2,1,128,256]{3,2,1,0:T(8,128)(2,1)S(1)}, bf16[2,1,128,256]{3,2,1,0:T(8,128)(2,1)S(1)}, u32[]{:S(2)}, u32[]{:S(2)}) collective-permute-start(bf16[2,1,128,256]{3,2,1,0:T(8,128)(2,1)S(1)} %get-tuple-element.66.refs_6_), channel_id=1, source_target_pairs={{0,14},{2,4},{4,2},{6,8},{8,6},{10,12},{12,10},{14,0},{1,15},{3,5}... | collective-permute-start | bytes 393224 | tf_op jit(solution)/shard_map/ppermute | solution.py:320
  35.2 2.3 %collective-permute-done.15.refs_8_ = bf16[2,1,128,256]{3,2,1,0:T(8,128)(2,1)S(1)} collective-permute-done((bf16[2,1,128,256]{3,2,1,0:T(8,128)(2,1)S(1)}, bf16[2,1,128,256]{3,2,1,0:T(8,128)(2,1)S(1)}, u32[]{:S(2)}, u32[]{:S(2)}) %collective-permute-start.15) | collective-permute-done | bytes 131104 | tf_op jit(solution)/shard_map/ppermute | solution.py:319
  37.5 2.1 %collective-permute-done.16.refs_9_ = bf16[2,1,128,256]{3,2,1,0:T(8,128)(2,1)S(1)} collective-permute-done((bf16[2,1,128,256]{3,2,1,0:T(8,128)(2,1)S(1)}, bf16[2,1,128,256]{3,2,1,0:T(8,128)(2,1)S(1)}, u32[]{:S(2)}, u32[]{:S(2)}) %collective-permute-start.16) | collective-permute-done | bytes 131104 | tf_op jit(solution)/shard_map/ppermute | solution.py:320
  39.6 1.6 %inner.5 = (f32[2,2,128,256]{3,2,1,0:T(8,128)S(1)}, f32[2,2,128,256]{3,2,1,0:T(8,128)S(1)}, bf16[2,2,128,256]{3,2,1,0:T(8,128)(2,1)S(1)}, bf16[1,2,128,256]{3,2,1,0:T(8,128)(2,1)S(1)}) custom-call(s32[1,128]{1,0:T(1,128)S(1)} %pad_bitcast_fusion.1.scalar_ref, bf16[4,2,2,6,128,128]{5,4,3,2,1,0:T(8,128)(2,1)S(1)} %get-tuple-element.46.w_ref, ...), custom_call_target="tpu_custom_call" | custom-call | flops 1000 | bytes 1000 | tf_op jit(solution)/shard_map/inner/pallas_call | solution.py:28
  44.4 1.6 %collective-permute-start.21 = (bf16[2,1,128,256]{3,2,1,0:T(8,128)(2,1)S(1)}, bf16[2,1,128,256]{3,2,1,0:T(8,128)(2,1)S(1)}, u32[]{:S(2)}, u32[]{:S(2)}) collective-permute-start(bf16[2,1,128,256]{3,2,1,0:T(8,128)(2,1)S(1)} %get-tuple-element.74.refs_5_), channel_id=1, source_target_pairs={{0,14},{2,4},{4,2},{6,8},{8,6},{10,12},{12,10},{14,0},{1,15},{3,5}... | collective-permute-start | bytes 393224 | tf_op jit(solution)/shard_map/ppermute | solution.py:320
  47.5 2.7 %collective-permute-done.20.refs_7_ = bf16[2,1,128,256]{3,2,1,0:T(8,128)(2,1)S(1)} collective-permute-done((bf16[2,1,128,256]{3,2,1,0:T(8,128)(2,1)S(1)}, bf16[2,1,128,256]{3,2,1,0:T(8,128)(2,1)S(1)}, u32[]{:S(2)}, u32[]{:S(2)}) %collective-permute-start.20) | collective-permute-done | bytes 131104 | tf_op jit(solution)/shard_map/ppermute | solution.py:319
  50.2 2.1 %collective-permute-done.21.refs_8_ = bf16[2,1,128,256]{3,2,1,0:T(8,128)(2,1)S(1)} collective-permute-done((bf16[2,1,128,256]{3,2,1,0:T(8,128)(2,1)S(1)}, bf16[2,1,128,256]{3,2,1,0:T(8,128)(2,1)S(1)}, u32[]{:S(2)}, u32[]{:S(2)}) %collective-permute-start.21) | collective-permute-done | bytes 131104 | tf_op jit(solution)/shard_map/ppermute | solution.py:320
  52.7 1.8 %collective-permute-start.24 = (bf16[2,2,128,256]{3,2,1,0:T(8,128)(2,1)S(1)}, bf16[2,2,128,256]{3,2,1,0:T(8,128)(2,1)S(1)}, u32[]{:S(2)}, u32[]{:S(2)}) collective-permute-start(bf16[2,2,128,256]{3,2,1,0:T(8,128)(2,1)S(1)} %get-tuple-element.82), channel_id=1, source_target_pairs={{0,8},{2,10},{4,12},{6,14},{8,0},{10,2},{12,4},{14,6},{1,9},{3,11}... | collective-permute-start | bytes 786440 | tf_op jit(solution)/shard_map/ppermute | solution.py:396
  56.0 1.7 %edge_last.1 = (f32[2,2,128,256]{3,2,1,0:T(8,128)S(1)}, bf16[2,2,128,256]{3,2,1,0:T(8,128)(2,1)S(1)}) custom-call(s32[1,128]{1,0:T(1,128)S(1)} %pad_bitcast_fusion.1.scalar_ref, bf16[4,2,2,6,128,128]{5,4,3,2,1,0:T(8,128)(2,1)S(1)} %get-tuple-element.56.w_ref, f32[2,4,2,128,128]{4,3,2,1,0:T(8,128)S(1)} %get-tuple-element.47.coef_ref, ...), custom_call_target="tpu_custom_call" | custom-call | flops 1000 | bytes 1000 | tf_op jit(solution)/shard_map/edge_last/pallas_call | solution.py:28
  58.9 2.2 %turn_interp.1.interp_ref = bf16[32,128,256]{2,1,0:T(8,128)(2,1)S(1)} custom-call(bf16[32,2,128,128]{3,2,1,0:T(8,128)(2,1)} %interp_ref), custom_call_target="tpu_custom_call" | custom-call | tf_op jit(solution)/shard_map/turn_interp/pallas_call | solution.py:359
  61.1 4.8 %collective-permute-done.24.refs_0_ = bf16[2,2,128,256]{3,2,1,0:T(8,128)(2,1)S(1)} collective-permute-done((bf16[2,2,128,256]{3,2,1,0:T(8,128)(2,1)S(1)}, bf16[2,2,128,256]{3,2,1,0:T(8,128)(2,1)S(1)}, u32[]{:S(2)}, u32[]{:S(2)}) %collective-permute-start.24) | collective-permute-done | bytes 262176 | tf_op jit(solution)/shard_map/ppermute | solution.py:396
  66.8 6.6 %collective-permute-done.27.refs_0_.refs_2_ = bf16[2,2,128,256]{3,2,1,0:T(8,128)(2,1)S(1)} collective-permute-done((bf16[2,2,128,256]{3,2,1,0:T(8,128)(2,1)S(1)}, bf16[2,2,128,256]{3,2,1,0:T(8,128)(2,1)S(1)}, u32[]{:S(2)}, u32[]{:S(2)}) %collective-permute-start.27) | collective-permute-done | bytes 262176 | tf_op jit(solution)/shard_map/ppermute | solution.py:399
  73.6 5.1 %collective-permute-done.31.refs_0_.refs_1_.refs_3_ = bf16[2,2,128,256]{3,2,1,0:T(8,128)(2,1)S(1)} collective-permute-done((bf16[2,2,128,256]{3,2,1,0:T(8,128)(2,1)S(1)}, bf16[2,2,128,256]{3,2,1,0:T(8,128)(2,1)S(1)}, u32[]{:S(2)}, u32[]{:S(2)}) %collective-permute-start.31) | collective-permute-done | bytes 262176 | tf_op jit(solution)/shard_map/ppermute | solution.py:398
  78.9 1.8 %collective-permute-start.32 = (bf16[2,2,128,256]{3,2,1,0:T(8,128)(2,1)S(1)}, bf16[2,2,128,256]{3,2,1,0:T(8,128)(2,1)S(1)}, u32[]{:S(2)}, u32[]{:S(2)}) collective-permute-start(bf16[2,2,128,256]{3,2,1,0:T(8,128)(2,1)S(1)} %get-tuple-element.86), channel_id=1, source_target_pairs={{0,2},{2,4},{4,6},{6,0},{8,10},{10,12},{12,14},{14,8},{1,3},{3,5},... | collective-permute-start | bytes 786440 | tf_op jit(solution)/shard_map/ppermute | solution.py:405
  82.4 2.0 %collective-permute-done.29.refs_4_ = bf16[2,2,128,256]{3,2,1,0:T(8,128)(2,1)S(1)} collective-permute-done((bf16[2,2,128,256]{3,2,1,0:T(8,128)(2,1)S(1)}, bf16[2,2,128,256]{3,2,1,0:T(8,128)(2,1)S(1)}, u32[]{:S(2)}, u32[]{:S(2)}) %collective-permute-start.29) | collective-permute-done | bytes 262176 | tf_op jit(solution)/shard_map/ppermute | solution.py:400
  84.4 7.6 %collective-permute-done.32.refs_1_ = bf16[2,2,128,256]{3,2,1,0:T(8,128)(2,1)S(1)} collective-permute-done((bf16[2,2,128,256]{3,2,1,0:T(8,128)(2,1)S(1)}, bf16[2,2,128,256]{3,2,1,0:T(8,128)(2,1)S(1)}, u32[]{:S(2)}, u32[]{:S(2)}) %collective-permute-start.32) | collective-permute-done | bytes 262176 | tf_op jit(solution)/shard_map/ppermute | solution.py:405
  92.0 2.2 %collective-permute-done.35.refs_5_ = bf16[2,2,128,256]{3,2,1,0:T(8,128)(2,1)S(1)} collective-permute-done((bf16[2,2,128,256]{3,2,1,0:T(8,128)(2,1)S(1)}, bf16[2,2,128,256]{3,2,1,0:T(8,128)(2,1)S(1)}, u32[]{:S(2)}, u32[]{:S(2)}) %collective-permute-start.35) | collective-permute-done | bytes 262176 | tf_op jit(solution)/shard_map/ppermute | solution.py:406
  95.9 2.8 %ocean.1 = bf16[32,128,256]{2,1,0:T(8,128)(2,1)} custom-call(s32[32,2]{1,0:T(8,128)S(1)} %fusion.3.scalar_ref, bf16[32,128,256]{2,1,0:T(8,128)(2,1)S(1)} %turn_interp.1.interp_ref, bf16[48,128,256]{2,1,0:T(8,128)(2,1)S(1)} %collect.3.tiles_ref), custom_call_target="tpu_custom_call" | custom-call | tf_op jit(solution)/shard_map/ocean/pallas_call | solution.py:413
  (85 shorter events, 29.2 us)
Async XLA Ops:
  2.1 14.7 %collective-permute-start = (bf16[1,2,128,256]{3,2,1,0:T(8,128)(2,1)S(1)}, bf16[1,2,128,256]{3,2,1,0:T(8,128)(2,1)S(1)}, u32[]{:S(2)}, u32[]{:S(2)}) collective-permute-start(bf16[1,2,128,256]{3,2,1,0:T(8,128)(2,1)S(1)} %get-tuple-element.49), channel_id=1, source_target_pairs={{0,1},{1,0},{2,3},{3,2},{4,5},{5,4},{6,7},{7,6},{8,9},{9,8},{10,11... | collective-permute-start | bytes 393224 | tf_op jit(solution)/shard_map/ppermute | solution.py:244
  2.7 14.2 %collective-permute-start.1 = (bf16[1,2,128,256]{3,2,1,0:T(8,128)(2,1)S(1)}, bf16[1,2,128,256]{3,2,1,0:T(8,128)(2,1)S(1)}, u32[]{:S(2)}, u32[]{:S(2)}) collective-permute-start(bf16[1,2,128,256]{3,2,1,0:T(8,128)(2,1)S(1)} %get-tuple-element.52), channel_id=1, source_target_pairs={{0,1},{1,0},{2,3},{3,2},{4,5},{5,4},{6,7},{7,6},{8,9},{9,8},{10,11... | collective-permute-start | bytes 393224 | tf_op jit(solution)/shard_map/ppermute | solution.py:244
  2.7 13.5 %collective-permute-start.3 = (bf16[2,1,128,256]{3,2,1,0:T(8,128)(2,1)S(1)}, bf16[2,1,128,256]{3,2,1,0:T(8,128)(2,1)S(1)}, u32[]{:S(2)}, u32[]{:S(2)}) collective-permute-start(bf16[2,1,128,256]{3,2,1,0:T(8,128)(2,1)S(1)} %get-tuple-element.50.refs_3_), channel_id=1, source_target_pairs={{0,2},{2,0},{4,6},{6,4},{8,10},{10,8},{12,14},{14,12},{1,3},{3,1},... | collective-permute-start | bytes 393224 | tf_op jit(solution)/shard_map/ppermute | solution.py:319
  5.7 10.6 %collective-permute-start.4 = (bf16[2,1,128,256]{3,2,1,0:T(8,128)(2,1)S(1)}, bf16[2,1,128,256]{3,2,1,0:T(8,128)(2,1)S(1)}, u32[]{:S(2)}, u32[]{:S(2)}) collective-permute-start(bf16[2,1,128,256]{3,2,1,0:T(8,128)(2,1)S(1)} %get-tuple-element.51.refs_4_), channel_id=1, source_target_pairs={{0,14},{2,4},{4,2},{6,8},{8,6},{10,12},{12,10},{14,0},{1,15},{3,5}... | collective-permute-start | bytes 393224 | tf_op jit(solution)/shard_map/ppermute | solution.py:320
  19.4 6.4 %collective-permute-start.9 = (bf16[2,1,128,256]{3,2,1,0:T(8,128)(2,1)S(1)}, bf16[2,1,128,256]{3,2,1,0:T(8,128)(2,1)S(1)}, u32[]{:S(2)}, u32[]{:S(2)}) collective-permute-start(bf16[2,1,128,256]{3,2,1,0:T(8,128)(2,1)S(1)} %get-tuple-element.58.refs_4_), channel_id=1, source_target_pairs={{0,2},{2,0},{4,6},{6,4},{8,10},{10,8},{12,14},{14,12},{1,3},{3,1},... | collective-permute-start | bytes 393224 | tf_op jit(solution)/shard_map/ppermute | solution.py:319
  19.5 8.5 %collective-permute-start.10 = (bf16[2,1,128,256]{3,2,1,0:T(8,128)(2,1)S(1)}, bf16[2,1,128,256]{3,2,1,0:T(8,128)(2,1)S(1)}, u32[]{:S(2)}, u32[]{:S(2)}) collective-permute-start(bf16[2,1,128,256]{3,2,1,0:T(8,128)(2,1)S(1)} %get-tuple-element.59.refs_5_), channel_id=1, source_target_pairs={{0,14},{2,4},{4,2},{6,8},{8,6},{10,12},{12,10},{14,0},{1,15},{3,5}... | collective-permute-start | bytes 393224 | tf_op jit(solution)/shard_map/ppermute | solution.py:320
  22.9 5.1 %collective-permute-start.2 = (bf16[1,2,128,256]{3,2,1,0:T(8,128)(2,1)S(1)}, bf16[1,2,128,256]{3,2,1,0:T(8,128)(2,1)S(1)}, u32[]{:S(2)}, u32[]{:S(2)}) collective-permute-start(bf16[1,2,128,256]{3,2,1,0:T(8,128)(2,1)S(1)} %get-tuple-element.55), channel_id=1, source_target_pairs={{0,1},{1,0},{2,3},{3,2},{4,5},{5,4},{6,7},{7,6},{8,9},{9,8},{10,11... | collective-permute-start | bytes 393224 | tf_op jit(solution)/shard_map/ppermute | solution.py:244
  23.0 5.0 %collective-permute-start.7 = (bf16[1,2,128,256]{3,2,1,0:T(8,128)(2,1)S(1)}, bf16[1,2,128,256]{3,2,1,0:T(8,128)(2,1)S(1)}, u32[]{:S(2)}, u32[]{:S(2)}) collective-permute-start(bf16[1,2,128,256]{3,2,1,0:T(8,128)(2,1)S(1)} %get-tuple-element.60), channel_id=1, source_target_pairs={{0,1},{1,0},{2,3},{3,2},{4,5},{5,4},{6,7},{7,6},{8,9},{9,8},{10,11... | collective-permute-start | bytes 393224 | tf_op jit(solution)/shard_map/ppermute | solution.py:244
  30.9 6.6 %collective-permute-start.15 = (bf16[2,1,128,256]{3,2,1,0:T(8,128)(2,1)S(1)}, bf16[2,1,128,256]{3,2,1,0:T(8,128)(2,1)S(1)}, u32[]{:S(2)}, u32[]{:S(2)}) collective-permute-start(bf16[2,1,128,256]{3,2,1,0:T(8,128)(2,1)S(1)} %get-tuple-element.65.refs_5_), channel_id=1, source_target_pairs={{0,2},{2,0},{4,6},{6,4},{8,10},{10,8},{12,14},{14,12},{1,3},{3,1},... | collective-permute-start | bytes 393224 | tf_op jit(solution)/shard_map/ppermute | solution.py:319
  31.4 8.1 %collective-permute-start.16 = (bf16[2,1,128,256]{3,2,1,0:T(8,128)(2,1)S(1)}, bf16[2,1,128,256]{3,2,1,0:T(8,128)(2,1)S(1)}, u32[]{:S(2)}, u32[]{:S(2)}) collective-permute-start(bf16[2,1,128,256]{3,2,1,0:T(8,128)(2,1)S(1)} %get-tuple-element.66.refs_6_), channel_id=1, source_target_pairs={{0,14},{2,4},{4,2},{6,8},{8,6},{10,12},{12,10},{14,0},{1,15},{3,5}... | collective-permute-start | bytes 393224 | tf_op jit(solution)/shard_map/ppermute | solution.py:320
  34.6 5.0 %collective-permute-start.8 = (bf16[1,2,128,256]{3,2,1,0:T(8,128)(2,1)S(1)}, bf16[1,2,128,256]{3,2,1,0:T(8,128)(2,1)S(1)}, u32[]{:S(2)}, u32[]{:S(2)}) collective-permute-start(bf16[1,2,128,256]{3,2,1,0:T(8,128)(2,1)S(1)} %get-tuple-element.63), channel_id=1, source_target_pairs={{0,1},{1,0},{2,3},{3,2},{4,5},{5,4},{6,7},{7,6},{8,9},{9,8},{10,11... | collective-permute-start | bytes 393224 | tf_op jit(solution)/shard_map/ppermute | solution.py:244
  43.5 6.7 %collective-permute-start.20 = (bf16[2,1,128,256]{3,2,1,0:T(8,128)(2,1)S(1)}, bf16[2,1,128,256]{3,2,1,0:T(8,128)(2,1)S(1)}, u32[]{:S(2)}, u32[]{:S(2)}) collective-permute-start(bf16[2,1,128,256]{3,2,1,0:T(8,128)(2,1)S(1)} %get-tuple-element.73.refs_4_), channel_id=1, source_target_pairs={{0,2},{2,0},{4,6},{6,4},{8,10},{10,8},{12,14},{14,12},{1,3},{3,1},... | collective-permute-start | bytes 393224 | tf_op jit(solution)/shard_map/ppermute | solution.py:319
  44.4 7.9 %collective-permute-start.21 = (bf16[2,1,128,256]{3,2,1,0:T(8,128)(2,1)S(1)}, bf16[2,1,128,256]{3,2,1,0:T(8,128)(2,1)S(1)}, u32[]{:S(2)}, u32[]{:S(2)}) collective-permute-start(bf16[2,1,128,256]{3,2,1,0:T(8,128)(2,1)S(1)} %get-tuple-element.74.refs_5_), channel_id=1, source_target_pairs={{0,14},{2,4},{4,2},{6,8},{8,6},{10,12},{12,10},{14,0},{1,15},{3,5}... | collective-permute-start | bytes 393224 | tf_op jit(solution)/shard_map/ppermute | solution.py:320
  52.3 8.8 %collective-permute-start.26 = (bf16[2,2,128,256]{3,2,1,0:T(8,128)(2,1)S(1)}, bf16[2,2,128,256]{3,2,1,0:T(8,128)(2,1)S(1)}, u32[]{:S(2)}, u32[]{:S(2)}) collective-permute-start(bf16[2,2,128,256]{3,2,1,0:T(8,128)(2,1)S(1)} %get-tuple-element.82), channel_id=1, source_target_pairs={{0,2},{2,0},{4,6},{6,4},{8,10},{10,8},{12,14},{14,12},{1,3},{3,1},... | collective-permute-start | bytes 786440 | tf_op jit(solution)/shard_map/ppermute | solution.py:397
  52.7 13.3 %collective-permute-start.24 = (bf16[2,2,128,256]{3,2,1,0:T(8,128)(2,1)S(1)}, bf16[2,2,128,256]{3,2,1,0:T(8,128)(2,1)S(1)}, u32[]{:S(2)}, u32[]{:S(2)}) collective-permute-start(bf16[2,2,128,256]{3,2,1,0:T(8,128)(2,1)S(1)} %get-tuple-element.82), channel_id=1, source_target_pairs={{0,8},{2,10},{4,12},{6,14},{8,0},{10,2},{12,4},{14,6},{1,9},{3,11}... | collective-permute-start | bytes 786440 | tf_op jit(solution)/shard_map/ppermute | solution.py:396
  65.9 7.5 %collective-permute-start.27 = (bf16[2,2,128,256]{3,2,1,0:T(8,128)(2,1)S(1)}, bf16[2,2,128,256]{3,2,1,0:T(8,128)(2,1)S(1)}, u32[]{:S(2)}, u32[]{:S(2)}) collective-permute-start(bf16[2,2,128,256]{3,2,1,0:T(8,128)(2,1)S(1)} %collective-permute-done.24.refs_0_), channel_id=1, source_target_pairs={{0,2},{2,0},{4,6},{6,4},{8,10},{10,8},{12,14},{14,12},{1,3},{3,1},... | collective-permute-start | bytes 786440 | tf_op jit(solution)/shard_map/ppermute | solution.py:399
  66.8 11.9 %collective-permute-start.31 = (bf16[2,2,128,256]{3,2,1,0:T(8,128)(2,1)S(1)}, bf16[2,2,128,256]{3,2,1,0:T(8,128)(2,1)S(1)}, u32[]{:S(2)}, u32[]{:S(2)}) collective-permute-start(bf16[2,2,128,256]{3,2,1,0:T(8,128)(2,1)S(1)} %get-tuple-element.85.first_ref), channel_id=1, source_target_pairs={{0,8},{2,10},{4,12},{6,14},{8,0},{10,2},{12,4},{14,6},{1,9},{3,11}... | collective-permute-start | bytes 786440 | tf_op jit(solution)/shard_map/ppermute | solution.py:398
  66.8 15.1 %collective-permute-start.25 = (bf16[2,2,128,256]{3,2,1,0:T(8,128)(2,1)S(1)}, bf16[2,2,128,256]{3,2,1,0:T(8,128)(2,1)S(1)}, u32[]{:S(2)}, u32[]{:S(2)}) collective-permute-start(bf16[2,2,128,256]{3,2,1,0:T(8,128)(2,1)S(1)} %collective-permute-done.24.refs_0_), channel_id=1, source_target_pairs={{0,1},{1,0},{2,3},{3,2},{4,5},{5,4},{6,7},{7,6},{8,9},{9,8},{10,11... | collective-permute-start | bytes 786440 | tf_op jit(solution)/shard_map/ppermute | solution.py:244
  73.6 10.8 %collective-permute-start.29 = (bf16[2,2,128,256]{3,2,1,0:T(8,128)(2,1)S(1)}, bf16[2,2,128,256]{3,2,1,0:T(8,128)(2,1)S(1)}, u32[]{:S(2)}, u32[]{:S(2)}) collective-permute-start(bf16[2,2,128,256]{3,2,1,0:T(8,128)(2,1)S(1)} %pick.2), channel_id=1, source_target_pairs={{0,4},{2,6},{4,0},{6,2},{8,12},{10,14},{12,8},{14,10},{1,5},{3,7},... | collective-permute-start | bytes 786440 | tf_op jit(solution)/shard_map/ppermute | solution.py:400
  78.9 13.1 %collective-permute-start.32 = (bf16[2,2,128,256]{3,2,1,0:T(8,128)(2,1)S(1)}, bf16[2,2,128,256]{3,2,1,0:T(8,128)(2,1)S(1)}, u32[]{:S(2)}, u32[]{:S(2)}) collective-permute-start(bf16[2,2,128,256]{3,2,1,0:T(8,128)(2,1)S(1)} %get-tuple-element.86), channel_id=1, source_target_pairs={{0,2},{2,4},{4,6},{6,0},{8,10},{10,12},{12,14},{14,8},{1,3},{3,5},... | collective-permute-start | bytes 786440 | tf_op jit(solution)/shard_map/ppermute | solution.py:405
  80.7 13.5 %collective-permute-start.35 = (bf16[2,2,128,256]{3,2,1,0:T(8,128)(2,1)S(1)}, bf16[2,2,128,256]{3,2,1,0:T(8,128)(2,1)S(1)}, u32[]{:S(2)}, u32[]{:S(2)}) collective-permute-start(bf16[2,2,128,256]{3,2,1,0:T(8,128)(2,1)S(1)} %get-tuple-element.87), channel_id=1, source_target_pairs={{0,6},{2,0},{4,2},{6,4},{8,14},{10,8},{12,10},{14,12},{1,7},{3,1},... | collective-permute-start | bytes 786440 | tf_op jit(solution)/shard_map/ppermute | solution.py:406
  81.9 12.3 %collective-permute-start.28 = (bf16[2,2,128,256]{3,2,1,0:T(8,128)(2,1)S(1)}, bf16[2,2,128,256]{3,2,1,0:T(8,128)(2,1)S(1)}, u32[]{:S(2)}, u32[]{:S(2)}) collective-permute-start(bf16[2,2,128,256]{3,2,1,0:T(8,128)(2,1)S(1)} %collective-permute-done.27.refs_0_.refs_2_), channel_id=1, source_target_pairs={{0,1},{1,0},{2,3},{3,2},{4,5},{5,4},{6,7},{7,6},{8,9},{9,8},{10,11... | collective-permute-start | bytes 786440 | tf_op jit(solution)/shard_map/ppermute | solution.py:244
  81.9 12.4 %collective-permute-start.34 = (bf16[2,2,128,256]{3,2,1,0:T(8,128)(2,1)S(1)}, bf16[2,2,128,256]{3,2,1,0:T(8,128)(2,1)S(1)}, u32[]{:S(2)}, u32[]{:S(2)}) collective-permute-start(bf16[2,2,128,256]{3,2,1,0:T(8,128)(2,1)S(1)} %collective-permute-done.31.refs_0_.refs_1_.refs_3_), channel_id=1, source_target_pairs={{0,1},{1,0},{2,3},{3,2},{4,5},{5,4},{6,7},{7,6},{8,9},{9,8},{10,11... | collective-permute-start | bytes 786440 | tf_op jit(solution)/shard_map/ppermute | solution.py:244
  84.4 9.9 %collective-permute-start.30 = (bf16[2,2,128,256]{3,2,1,0:T(8,128)(2,1)S(1)}, bf16[2,2,128,256]{3,2,1,0:T(8,128)(2,1)S(1)}, u32[]{:S(2)}, u32[]{:S(2)}) collective-permute-start(bf16[2,2,128,256]{3,2,1,0:T(8,128)(2,1)S(1)} %collective-permute-done.29.refs_4_), channel_id=1, source_target_pairs={{0,1},{1,0},{2,3},{3,2},{4,5},{5,4},{6,7},{7,6},{8,9},{9,8},{10,11... | collective-permute-start | bytes 786440 | tf_op jit(solution)/shard_map/ppermute | solution.py:244
  (16 other events, 38.6 us)

commit v4 on v3

--- a/solution.py
+++ b/solution.py
@@ -55,21 +55,32 @@
     erow_ref[0, 1] = edge_b_ref[send, 0]
 
 
-def setup_kernel(scalar_ref, pos_ref, w_ref, coef_ref, inner_ref, edge_ref, sems):
+def setup_kernel(
+    scalar_ref, pos_hbm, codes_hbm, w_ref, coef_ref, codes_ref, inner_ref, edge_ref, pos_ref, sems, small_sems
+):
+    small = [
+        pltpu.make_async_copy(pos_hbm, pos_ref, small_sems.at[0]),
+        pltpu.make_async_copy(codes_hbm, codes_ref, small_sems.at[1]),
+    ]
+    for copy in small:
+        copy.start()
+    rows, cols, nodes = pos_ref.shape[1:]
     copies = []
-    for c in range(pos_ref.shape[2]):
-        on_edge = c in (0, pos_ref.shape[2] - 1)
+    for c in range(cols):
+        on_edge = c in (0, cols - 1)
         target, place = (edge_ref, min(c, 1)) if on_edge else (inner_ref, c - 1)
-        copies.append(
-            pltpu.make_async_copy(
-                w_ref.at[:, :, pl.ds(scalar_ref[0, 1 + c], 1)],
-                target.at[:, :, pl.ds(place, 1)],
-                sems.at[c],
-            )
-        )
+        for q in range(w_ref.shape[0]):
+            copies.append(
+                pltpu.make_async_copy(
+                    w_ref.at[q, :, pl.ds(scalar_ref[0, 1 + c], 1)],
+                    target.at[q, :, pl.ds(place, 1)],
+                    sems.at[q, c],
+                )
+            )
     for copy in copies:
         copy.start()
-    rows, cols, nodes = pos_ref.shape[1:]
+    for copy in small:
+        copy.wait()
     low = lax.broadcasted_iota(jnp.int32, (nodes, nodes), 1) < nodes // 2
     for a in range(rows):
         for b in range(cols):
@@ -125,7 +136,7 @@
     return fa - x01 * radial, fb - x2_low * radial
 
 
-def stage_kernel(edge, number, stages, scale, scalar_ref, w_ref, coef_ref, *refs):
+def stage_kernel(edge, number, stages, scale, scalar_ref, codes_ref, w_ref, coef_ref, *refs):
     refs = list(refs)
     ext = refs.pop()
     rows, cols = coef_ref.shape[:2]
@@ -158,12 +169,21 @@
     blend_ref = refs.pop(0) if blend else None
     next_ref, *outs = refs
     columns = (0, cols - 1) if edge else tuple(range(1, cols - 1))
+    eastward = 1 - 2 * scalar_ref[0, 1 + cols]
+
+    def neighbour(code, a, c):
+        third = (code * 11) // 32
+        row = a + third - 1
+        row = jnp.where(row < 0, rows, row)
+        return row * wide + 1 + c + eastward * (code - 3 * third - 1)
+
     low = lax.broadcasted_iota(jnp.int32, (nodes, feats // 2), 1) < feats // 4
     for a in range(rows):
         for place, c in enumerate(columns):
             b = scalar_ref[0, 1 + c]
-            base = 1 + cols + (a * cols + c) * taps
-            near = jnp.concatenate([ext[scalar_ref[0, base + k]] for k in range(taps)], axis=0)
+            near = jnp.concatenate(
+                [ext[neighbour(codes_ref[a, b, k], a, c)] for k in range(taps)], axis=0
+            )
             weights = jnp.concatenate(
                 [
                     jnp.concatenate([w_ref[q, a, place, k] for k in range(taps)], axis=1)
@@ -218,15 +238,40 @@
         out_ref[pl.ds(place, flat.shape[0])] = flat[...]
 
 
-def ocean_kernel(scalar_ref, interp_ref, tiles_ref, out_ref):
-    block = out_ref.shape[0]
-    taps = scalar_ref.shape[1]
-    first = pl.program_id(0) * block
-    for o in range(block):
-        near = jnp.concatenate(
-            [tiles_ref[scalar_ref[first + o, j]] for j in range(taps)], axis=0
-        )
-        out_ref[o] = jnp.dot(interp_ref[first + o], near, preferred_element_type=F32).astype(BF16)
+def ocean_kernel(
+    sizes, scalar_ref, owner_ref, local_ref, interp_ref, tiles_ref, out_ref, slot_ref, buffer, sems
+):
+    lon_count, lat_count, rows, cols, block = sizes
+    my_lon, my_lat = scalar_ref[0, 2 + cols], 1 - scalar_ref[0, 0]
+    middle = lon_count // 2
+    owners, local_ids = owner_ref[...], local_ref[...]
+    owner_lon = owners // lat_count
+    relative = (owner_lon - my_lon + (middle + 1 + lon_count)) % lon_count
+    even = 1 - my_lon % 2
+    towards = (relative == 2).astype(jnp.int32)
+    kind = jnp.where(relative == 1, 0, 2 - (towards == even).astype(jnp.int32))
+    away = (owners % lat_count != my_lat).astype(jnp.int32)
+    row, col = local_ids // cols, local_ids % cols
+    col = jnp.where(owner_lon % 2 == 0, cols - 1 - col, col)
+    inner_count = rows * (cols - 2)
+    inner_slot = (kind * 2 + away) * inner_count + row * (cols - 2) + col - 1
+    edge_slot = 6 * inner_count + (relative * 2 + away) * (2 * rows)
+    edge_slot += 2 * row + (col != 0).astype(jnp.int32)
+    slot_ref[...] = jnp.where((col == 0) | (col == cols - 1), edge_slot, inner_slot)
+
+    taps, tiles = slot_ref.shape
+    copies = []
+    for o in range(tiles):
+        near = jnp.concatenate([tiles_ref[slot_ref[j, o]] for j in range(taps)], axis=0)
+        buffer[o] = jnp.dot(interp_ref[o], near, preferred_element_type=F32).astype(BF16)
+        if o % block == block - 1:
+            part = pl.ds(o + 1 - block, block)
+            copies.append(
+                pltpu.make_async_copy(buffer.at[part], out_ref.at[part], sems.at[o // block])
+            )
+            copies[-1].start()
+    for copy in copies:
+        copy.wait()
 
 
 def local(state, weights, positions, stencil_codes, ovl_owner, ovl_local, interp):
@@ -243,43 +288,19 @@
     def flip(value):
         return lax.ppermute(value, "lat", swap)
 
-    a_is_east = my_lon % 2 == 0
-    tile_row = lax.broadcasted_iota(jnp.int32, stencil_codes.shape, 0)
-    tile_col = lax.broadcasted_iota(jnp.int32, stencil_codes.shape, 1)
-    near_col = tile_col + stencil_codes % 3 - 1
-    ext_row = tile_row + stencil_codes // 3 - 1
-    ext_row = jnp.where(ext_row < 0, rows, ext_row)
-    ext_col = jnp.where(a_is_east, cols - 1 - near_col, near_col)
-    index = ext_row * (cols + 2) + ext_col + 1
-    index = jnp.where(a_is_east, index[:, ::-1], index)
+    a_is_east = (my_lon % 2 == 0).astype(jnp.int32)
     order = jnp.arange(cols, dtype=jnp.int32)
-    order = jnp.where(a_is_east, cols - 1 - order, order)
-    send = (1 - my_lat).astype(jnp.int32).reshape(1)
-
-    def as_row(parts):
-        flat = jnp.concatenate([part.reshape(-1).astype(jnp.int32) for part in parts])
-        return jnp.pad(flat, (0, -flat.size % 128)).reshape(1, -1)
-
+    order = jnp.where(a_is_east == 1, cols - 1 - order, order)
     middle = lon_count // 2
     in_half = my_lon % middle
+    turns = (in_half == middle - 2) | (in_half == 1)
+    last_of_half, first_of_half = in_half == middle - 1, in_half == 0
+    numbers = [1 - my_lat, *order, a_is_east, my_lon, turns, last_of_half, first_of_half]
+    numbers = jnp.stack([number.astype(jnp.int32) for number in numbers])
+    scalars = jnp.pad(numbers, (0, -numbers.size % 128)).reshape(1, -1)
+    flags = cols + 3
     ocean_dev, intersections = ovl_local.shape
-    target = (my_lon + middle) % lon_count
-    owners = ovl_owner.reshape(ocean_dev, intersections)
-    owner_lon = owners // lat_count
-    relative = (owner_lon - target + 1 + lon_count) % lon_count
-    kind = jnp.where(relative == 1, 0, jnp.where((relative == 2) == a_is_east, 1, 2))
-    away = (owners % lat_count != my_lat).astype(jnp.int32)
-    owner_row, owner_col = ovl_local // cols, ovl_local % cols
-    owner_col = jnp.where(owner_lon % 2 == 0, cols - 1 - owner_col, owner_col)
     inner_count = rows * (cols - 2)
-    inner_slot = (kind * 2 + away) * inner_count + owner_row * (cols - 2) + owner_col - 1
-    edge_slot = 6 * inner_count + (relative * 2 + away) * (2 * rows)
-    edge_slot += 2 * owner_row + (owner_col != 0)
-    slot = jnp.where((owner_col == 0) | (owner_col == cols - 1), edge_slot, inner_slot)
-
-    turns = (in_half == middle - 2) | (in_half == 1)
-    scalars = as_row([send, order, index, turns, in_half == middle - 1, in_half == 0])
-    flags = 1 + cols + index.size
 
     tile = (nodes, feats)
     inner_s = ((rows, cols - 2) + tile, BF16)
@@ -291,23 +312,29 @@
         prep_kernel,
         "prep",
         [inner_s, irow_s, edge_s, edge_s, erow_s],
-        [as_row([send, order]), state],
+        [scalars, state],
     )
 
     quarter = weights.shape[:2]
-    coef, w_inner, w_edge = pl.pallas_call(
+    coef, codes, w_inner, w_edge = pl.pallas_call(
         setup_kernel,
         out_shape=[
             pltpu.VMEM((rows, cols, 2, nodes, nodes), F32),
+            pltpu.VMEM(stencil_codes.shape, jnp.int32),
             pltpu.VMEM(quarter + (cols - 2,) + weights.shape[3:], BF16),
             pltpu.VMEM(quarter + (2,) + weights.shape[3:], BF16),
         ],
-        in_specs=[VMEM, VMEM, HBM],
-        out_specs=[VMEM] * 3,
-        scratch_shapes=[pltpu.SemaphoreType.DMA((cols,))],
+        in_specs=[VMEM] + [HBM] * 3,
+        out_specs=[VMEM] * 4,
+        scratch_shapes=[
+            pltpu.VMEM(positions.shape, F32),
+            pltpu.SemaphoreType.DMA((weights.shape[0], cols)),
+            pltpu.SemaphoreType.DMA((2,)),
+        ],
         compiler_params=pltpu.CompilerParams(vmem_limit_bytes=4 * MIB),
         name="setup",
-    )(in_vmem(scalars), in_vmem(after(positions, slot)), in_hbm(weights))
+    )(in_vmem(scalars), in_hbm(positions), in_hbm(stencil_codes), in_hbm(weights))
+
     scales = (0.5 * STEP_SIZE, 0.5 * STEP_SIZE, STEP_SIZE, STEP_SIZE / 6.0)
     stages = len(scales)
 
@@ -318,12 +345,13 @@
         inner, irow, edge_a, edge_b, erow = own
         halo_a = lax.ppermute(edge_a, "lon", to_a)
         halo_b = lax.ppermute(edge_b, "lon", to_b)
-        if number == 0:
-            halo_a = after(halo_a, w_edge)
         near = [inner, flip(irow), edge_a, edge_b, flip(erow)]
-        far = [halo_a, halo_b, flip(halo_a), flip(halo_b)]
-        own = []
+        own = {}
         for edge in (False, True):
+            if edge:
+                halo_a, halo_b = lax.optimization_barrier((halo_a, halo_b, own[False][0]))[:2]
+                corner_a, corner_b = flip(halo_a), flip(halo_b)
+            far = [halo_a, halo_b, corner_a, corner_b] if edge else []
             field_s = ((rows, 2 if edge else cols - 2) + tile, F32)
             outs = [edge_s, edge_s, erow_s] if edge else [inner_s, irow_s]
             if last:
@@ -333,20 +361,24 @@
                 functools.partial(stage_kernel, edge, number, stages, scale),
                 ("edge" if edge else "inner") + ("_last" if last else ""),
                 outs,
-                [scalars, w_edge if edge else w_inner, coef]
+                [scalars, codes, w_edge if edge else w_inner, coef]
                 + ([] if last else [state])
                 + fields[edge]
                 + near
-                + (far if edge else []),
+                + far,
                 [pltpu.VMEM(((rows + 1) * (cols + 2),) + tile, BF16)],
             )
             if blend:
                 fields[edge], results = list(results[:2]), results[2:]
             else:
                 fields[edge], results = (fields[edge] + [results[0]])[-2:], results[1:]
-            own += results
+            own[edge] = results
+        own = own[False] + own[True]
     next_i, next_e = fields[False][-1], fields[True][-1]
     final_i, final_e = own
+    opposite = [(i, (i + middle) % lon_count) for i in range(lon_count)]
+    center_i = lax.ppermute(final_i, "lon", opposite)
+    center_e = lax.ppermute(final_e, "lon", opposite)
 
     (next_state,) = pl.pallas_call(
         join_kernel,
@@ -366,7 +398,6 @@
         name="turn_interp",
     )(in_hbm(after(interp, next_e)))
 
-    opposite = [(i, (i + middle) % lon_count) for i in range(lon_count)]
 
     def within_half(step):
         return [(i, i - i % middle + (i + step(i)) % middle) for i in range(lon_count)]
@@ -392,10 +423,7 @@
             aliases=None if tiles is None else {0: 0},
         )[0]
 
-    final_i = after(final_i, halo_a, halo_b)
-    center_i = lax.ppermute(final_i, "lon", opposite)
     native = lax.ppermute(final_i, "lon", to_a)
-    center_e = lax.ppermute(after(final_e, center_i, next_state, turned_interp), "lon", opposite)
     paired = lax.ppermute(after(center_i, native, next_state, turned_interp), "lon", to_a)
     passed = lax.ppermute(pick(flags, native, paired)[0], "lon", onward)
     tiles = collect(
@@ -409,16 +437,25 @@
         6 * inner_count,
         [below, flip(below), center_e, flip(center_e), above, flip(above)],
     )
-    block = 8
+    block = 4
     ocean = pl.pallas_call(
-        ocean_kernel,
-        grid=(ocean_dev // block,),
-        out_shape=jax.ShapeDtypeStruct((ocean_dev, nodes, feats), BF16),
-        in_specs=[VMEM] * 3,
-        out_specs=pl.BlockSpec((block, nodes, feats), lambda g: (g, 0, 0)),
-        compiler_params=pltpu.CompilerParams(vmem_limit_bytes=4 * MIB),
+        functools.partial(ocean_kernel, (lon_count, lat_count, rows, cols, block)),
+        out_shape=pltpu.HBM((ocean_dev, nodes, feats), BF16),
+        in_specs=[VMEM] * 5,
+        out_specs=HBM,
+        scratch_shapes=[
+            pltpu.VMEM((intersections, ocean_dev), jnp.int32),
+            pltpu.VMEM((ocean_dev, nodes, feats), BF16),
+            pltpu.SemaphoreType.DMA((ocean_dev // block,)),
+        ],
+        compiler_params=pltpu.CompilerParams(vmem_limit_bytes=6 * MIB),
         name="ocean",
-    )(in_vmem(slot), in_vmem(turned_interp), in_vmem(tiles))
+    )(
+        *[
+            in_vmem(array)
+            for array in (scalars, ovl_owner[:, :, 0].T, ovl_local.T, turned_interp, tiles)
+        ]
+    )
     return next_state, ocean
 
 

time: 99 us -> 93.4 us (0.943)
  waiting for transfers between devices: 46.7 us -> 38.5 us
  starting transfers between devices: 23.3 us -> 29.5 us
  local copies, waits for them, and re-layouts: 3.67 us -> 1.33 us
  other arithmetic: 1.57 us -> 0.01 us
    ppermute x4, waiting for transfers between devices: 6.3 us -> 1 us  [local(): halo_b = lax.ppermute(edge_b, 'lon', to_b)]
    ppermute x4, starting transfers between devices: 8.73 us -> 13.4 us  [local(): halo_b = lax.ppermute(edge_b, 'lon', to_b)]
    ppermute x1, waiting for transfers between devices: 6.59 us -> 2.33 us  [local(): lax.ppermute(after(center_i, native, next_state, turned_interp), 'lon', t...]
    ppermute x1, waiting for transfers between devices: 4.83 us -> 8.72 us  [local(): center_i = lax.ppermute(final_i, 'lon', opposite)]
    ppermute x1, waiting for transfers between devices: 1.96 us -> 5.74 us  [local(): passed = lax.ppermute(pick(flags, native, paired)[0], 'lon', onward)]
    ppermute x1, waiting for transfers between devices: 7.64 us -> 4.44 us  [local(): below = lax.ppermute(going_up, 'lon', up)]
    ppermute x1, waiting for transfers between devices: 2.2 us -> 0.24 us  [local(): above = lax.ppermute(going_down, 'lon', down)]
    ppermute x1, starting transfers between devices: 0.01 us -> 1.59 us  [local(): center_e = lax.ppermute(final_e, 'lon', opposite)]
  transfers between devices with their start and end apart: 37 -> 37, of which waited for: 18 -> 19; matrix products, arithmetic and copies ran while one was open for 3% -> 0% of each run, Pallas kernels for 17% -> 22%
where the time goes in v4:
time: 93.4 us; the launch traced here: 93.2 us
  waiting for transfers between devices  38.5 us (41%)
  starting transfers between devices  29.5 us (32%)
  Pallas kernels  22.7 us (24%)
  local copies, waits for them, and re-layouts  1.33 us (1%)
  between operations  1.08 us (1%)
    pallas_call x13, Pallas kernels, vmem_call(): pl.pallas_call(kernel, out_shape=[pltpu.VMEM(shape, dtype) for shape, dty...  14.5 us
    ppermute x4, starting transfers between devices, local(): halo_b = lax.ppermute(edge_b, 'lon', to_b)  13.4 us
    ppermute x1, waiting for transfers between devices, local(): center_i = lax.ppermute(final_i, 'lon', opposite)  8.72 us
    ppermute x4, waiting for transfers between devices, local(): halo_a = lax.ppermute(edge_a, 'lon', to_a)  6.39 us
    ppermute x1, waiting for transfers between devices, local(): passed = lax.ppermute(pick(flags, native, paired)[0], 'lon', onward)  5.74 us
    ppermute x22, waiting for transfers between devices, flip(): return lax.ppermute(value, 'lat', swap)  5.29 us
    ppermute x22, starting transfers between devices, flip(): return lax.ppermute(value, 'lat', swap)  4.74 us
    ppermute x1, waiting for transfers between devices, local(): below = lax.ppermute(going_up, 'lon', up)  4.44 us
  transfers between devices with their start and end apart: 37, of which 19 were waited for; matrix products, arithmetic and copies ran while one was open for 0% of the time, Pallas kernels for 22%

profile of v4, /device:TPU:0, one launch (start us, length us, event | category | flops | bytes accessed | tf_op | source)
XLA Modules:
  0.0 93.2 jit_solution(11227756812691669344)
XLA Ops:
  2.8 2.9 %collective-permute-start.3 = (bf16[2,1,128,256]{3,2,1,0:T(8,128)(2,1)S(1)}, bf16[2,1,128,256]{3,2,1,0:T(8,128)(2,1)S(1)}, u32[]{:S(2)}, u32[]{:S(2)}) collective-permute-start(bf16[2,1,128,256]{3,2,1,0:T(8,128)(2,1)S(1)} %get-tuple-element.55.refs_3_), channel_id=1, source_target_pairs={{0,2},{2,0},{4,6},{6,4},{8,10},{10,8},{12,14},{14,12},{1,3},{3,1},... | collective-permute-start | bytes 393224 | tf_op jit(solution)/shard_map/ppermute | solution.py:346
  5.7 3.6 %collective-permute-start.4 = (bf16[2,1,128,256]{3,2,1,0:T(8,128)(2,1)S(1)}, bf16[2,1,128,256]{3,2,1,0:T(8,128)(2,1)S(1)}, u32[]{:S(2)}, u32[]{:S(2)}) collective-permute-start(bf16[2,1,128,256]{3,2,1,0:T(8,128)(2,1)S(1)} %get-tuple-element.56.refs_4_), channel_id=1, source_target_pairs={{0,14},{2,4},{4,2},{6,8},{8,6},{10,12},{12,10},{14,0},{1,15},{3,5}... | collective-permute-start | bytes 393224 | tf_op jit(solution)/shard_map/ppermute | solution.py:347
  9.3 3.0 %setup.1 = (f32[2,4,2,128,128]{4,3,2,1,0:T(8,128)S(1)}, s32[2,4,6]{2,1,0:T(4,128)S(1)}, bf16[4,2,2,6,128,128]{5,4,3,2,1,0:T(8,128)(2,1)S(1)}, bf16[4,2,2,6,128,128]{5,4,3,2,1,0:T(8,128)(2,1)S(1)}) custom-call(s32[1,128]{1,0:T(1,128)S(1)} %pad_bitcast_fusion.scalar_ref, f32[3,2,4,128]{3,2,1,0:T(4,128)} %pos_hbm.1, s32[2,4,6]{2,1,0:T(4,128)} %codes_hbm.1, ...), custom_call_target="tpu_custom_call" | custom-call | tf_op jit(solution)/shard_map/setup/pallas_call | solution.py:319
  12.3 1.7 %inner.3 = (f32[2,2,128,256]{3,2,1,0:T(8,128)S(1)}, bf16[2,2,128,256]{3,2,1,0:T(8,128)(2,1)S(1)}, bf16[1,2,128,256]{3,2,1,0:T(8,128)(2,1)S(1)}) custom-call(s32[1,128]{1,0:T(1,128)S(1)} %pad_bitcast_fusion.scalar_ref, s32[2,4,6]{2,1,0:T(4,128)S(1)} %get-tuple-element.50.codes_ref, bf16[4,2,2,6,128,128]{5,4,3,2,1,0:T(8,128)(2,1)S(1)} %get-tuple-element.51.w_ref, ...), custom_call_target="tpu_custom_call" | custom-call | flops 1000 | bytes 1000 | tf_op jit(solution)/shard_map/inner/pallas_call | solution.py:28
  15.6 1.7 %edge.3 = (f32[2,2,128,256]{3,2,1,0:T(8,128)S(1)}, bf16[2,1,128,256]{3,2,1,0:T(8,128)(2,1)S(1)}, bf16[2,1,128,256]{3,2,1,0:T(8,128)(2,1)S(1)}, bf16[1,2,128,256]{3,2,1,0:T(8,128)(2,1)S(1)}) custom-call(s32[1,128]{1,0:T(1,128)S(1)} %pad_bitcast_fusion.scalar_ref, s32[2,4,6]{2,1,0:T(4,128)S(1)} %get-tuple-element.50.codes_ref, ...), custom_call_target="tpu_custom_call" | custom-call | flops 1000 | bytes 1000 | tf_op jit(solution)/shard_map/edge/pallas_call | solution.py:28
  17.7 3.5 %collective-permute-start.10 = (bf16[2,1,128,256]{3,2,1,0:T(8,128)(2,1)S(1)}, bf16[2,1,128,256]{3,2,1,0:T(8,128)(2,1)S(1)}, u32[]{:S(2)}, u32[]{:S(2)}) collective-permute-start(bf16[2,1,128,256]{3,2,1,0:T(8,128)(2,1)S(1)} %get-tuple-element.65.refs_5_), channel_id=1, source_target_pairs={{0,14},{2,4},{4,2},{6,8},{8,6},{10,12},{12,10},{14,0},{1,15},{3,5}... | collective-permute-start | bytes 393224 | tf_op jit(solution)/shard_map/ppermute | solution.py:347
  21.2 1.7 %inner.4 = (f32[2,2,128,256]{3,2,1,0:T(8,128)S(1)}, bf16[2,2,128,256]{3,2,1,0:T(8,128)(2,1)S(1)}, bf16[1,2,128,256]{3,2,1,0:T(8,128)(2,1)S(1)}) custom-call(s32[1,128]{1,0:T(1,128)S(1)} %pad_bitcast_fusion.scalar_ref, s32[2,4,6]{2,1,0:T(4,128)S(1)} %get-tuple-element.50.codes_ref, bf16[4,2,2,6,128,128]{5,4,3,2,1,0:T(8,128)(2,1)S(1)} %get-tuple-element.51.w_ref, ...), custom_call_target="tpu_custom_call" | custom-call | flops 1000 | bytes 1000 | tf_op jit(solution)/shard_map/inner/pallas_call | solution.py:28
  22.9 3.2 %collective-permute-done.9.refs_7_ = bf16[2,1,128,256]{3,2,1,0:T(8,128)(2,1)S(1)} collective-permute-done((bf16[2,1,128,256]{3,2,1,0:T(8,128)(2,1)S(1)}, bf16[2,1,128,256]{3,2,1,0:T(8,128)(2,1)S(1)}, u32[]{:S(2)}, u32[]{:S(2)}) %collective-permute-start.9) | collective-permute-done | bytes 131104 | tf_op jit(solution)/shard_map/ppermute | solution.py:346
  27.7 1.7 %edge.4 = (f32[2,2,128,256]{3,2,1,0:T(8,128)S(1)}, bf16[2,1,128,256]{3,2,1,0:T(8,128)(2,1)S(1)}, bf16[2,1,128,256]{3,2,1,0:T(8,128)(2,1)S(1)}, bf16[1,2,128,256]{3,2,1,0:T(8,128)(2,1)S(1)}) custom-call(s32[1,128]{1,0:T(1,128)S(1)} %pad_bitcast_fusion.scalar_ref, s32[2,4,6]{2,1,0:T(4,128)S(1)} %get-tuple-element.50.codes_ref, ...), custom_call_target="tpu_custom_call" | custom-call | flops 1000 | bytes 1000 | tf_op jit(solution)/shard_map/edge/pallas_call | solution.py:28
  30.1 3.2 %collective-permute-start.16 = (bf16[2,1,128,256]{3,2,1,0:T(8,128)(2,1)S(1)}, bf16[2,1,128,256]{3,2,1,0:T(8,128)(2,1)S(1)}, u32[]{:S(2)}, u32[]{:S(2)}) collective-permute-start(bf16[2,1,128,256]{3,2,1,0:T(8,128)(2,1)S(1)} %get-tuple-element.74.refs_6_), channel_id=1, source_target_pairs={{0,14},{2,4},{4,2},{6,8},{8,6},{10,12},{12,10},{14,0},{1,15},{3,5}... | collective-permute-start | bytes 393224 | tf_op jit(solution)/shard_map/ppermute | solution.py:347
  33.2 1.7 %inner.5 = (f32[2,2,128,256]{3,2,1,0:T(8,128)S(1)}, f32[2,2,128,256]{3,2,1,0:T(8,128)S(1)}, bf16[2,2,128,256]{3,2,1,0:T(8,128)(2,1)S(1)}, bf16[1,2,128,256]{3,2,1,0:T(8,128)(2,1)S(1)}) custom-call(s32[1,128]{1,0:T(1,128)S(1)} %pad_bitcast_fusion.scalar_ref, s32[2,4,6]{2,1,0:T(4,128)S(1)} %get-tuple-element.50.codes_ref, ...), custom_call_target="tpu_custom_call" | custom-call | flops 1000 | bytes 1000 | tf_op jit(solution)/shard_map/inner/pallas_call | solution.py:28
  35.0 3.2 %collective-permute-done.15.refs_8_ = bf16[2,1,128,256]{3,2,1,0:T(8,128)(2,1)S(1)} collective-permute-done((bf16[2,1,128,256]{3,2,1,0:T(8,128)(2,1)S(1)}, bf16[2,1,128,256]{3,2,1,0:T(8,128)(2,1)S(1)}, u32[]{:S(2)}, u32[]{:S(2)}) %collective-permute-start.15) | collective-permute-done | bytes 131104 | tf_op jit(solution)/shard_map/ppermute | solution.py:346
  39.7 1.7 %edge.5 = (f32[2,2,128,256]{3,2,1,0:T(8,128)S(1)}, f32[2,2,128,256]{3,2,1,0:T(8,128)S(1)}, bf16[2,1,128,256]{3,2,1,0:T(8,128)(2,1)S(1)}, bf16[2,1,128,256]{3,2,1...) custom-call(s32[1,128]{1,0:T(1,128)S(1)} %pad_bitcast_fusion.scalar_ref, s32[2,4,6]{2,1,0:T(4,128)S(1)} %get-tuple-element.50.codes_ref, ...), custom_call_target="tpu_custom_call" | custom-call | flops 1000 | bytes 1000 | tf_op jit(solution)/shard_map/edge/pallas_call | solution.py:28
  42.1 3.2 %collective-permute-start.21 = (bf16[2,1,128,256]{3,2,1,0:T(8,128)(2,1)S(1)}, bf16[2,1,128,256]{3,2,1,0:T(8,128)(2,1)S(1)}, u32[]{:S(2)}, u32[]{:S(2)}) collective-permute-start(bf16[2,1,128,256]{3,2,1,0:T(8,128)(2,1)S(1)} %get-tuple-element.84.refs_5_), channel_id=1, source_target_pairs={{0,14},{2,4},{4,2},{6,8},{8,6},{10,12},{12,10},{14,0},{1,15},{3,5}... | collective-permute-start | bytes 393224 | tf_op jit(solution)/shard_map/ppermute | solution.py:347
  45.3 1.7 %inner_last.1 = (f32[2,2,128,256]{3,2,1,0:T(8,128)S(1)}, bf16[2,2,128,256]{3,2,1,0:T(8,128)(2,1)S(1)}) custom-call(s32[1,128]{1,0:T(1,128)S(1)} %pad_bitcast_fusion.scalar_ref, s32[2,4,6]{2,1,0:T(4,128)S(1)} %get-tuple-element.50.codes_ref, bf16[4,2,2,6,128,128]{5,4,3,2,1,0:T(8,128)(2,1)S(1)} %get-tuple-element.51.w_ref, ...), custom_call_target="tpu_custom_call" | custom-call | flops 1000 | bytes 1000 | tf_op jit(solution)/shard_map/inner_last/pallas_call | solution.py:28
  47.1 2.2 %collective-permute-start.24 = (bf16[2,2,128,256]{3,2,1,0:T(8,128)(2,1)S(1)}, bf16[2,2,128,256]{3,2,1,0:T(8,128)(2,1)S(1)}, u32[]{:S(2)}, u32[]{:S(2)}) collective-permute-start(bf16[2,2,128,256]{3,2,1,0:T(8,128)(2,1)S(1)} %get-tuple-element.89), channel_id=1, source_target_pairs={{0,8},{2,10},{4,12},{6,14},{8,0},{10,2},{12,4},{14,6},{1,9},{3,11}... | collective-permute-start | bytes 786440 | tf_op jit(solution)/shard_map/ppermute | solution.py:380
  51.8 1.9 %edge_last.1 = (f32[2,2,128,256]{3,2,1,0:T(8,128)S(1)}, bf16[2,2,128,256]{3,2,1,0:T(8,128)(2,1)S(1)}) custom-call(s32[1,128]{1,0:T(1,128)S(1)} %pad_bitcast_fusion.scalar_ref, s32[2,4,6]{2,1,0:T(4,128)S(1)} %get-tuple-element.50.codes_ref, bf16[4,2,2,6,128,128]{5,4,3,2,1,0:T(8,128)(2,1)S(1)} %get-tuple-element.61.w_ref, ...), custom_call_target="tpu_custom_call" | custom-call | flops 1000 | bytes 1000 | tf_op jit(solution)/shard_map/edge_last/pallas_call | solution.py:28
  56.4 2.2 %turn_interp.1.interp_ref = bf16[32,128,256]{2,1,0:T(8,128)(2,1)S(1)} custom-call(bf16[32,2,128,128]{3,2,1,0:T(8,128)(2,1)} %interp_ref), custom_call_target="tpu_custom_call" | custom-call | tf_op jit(solution)/shard_map/turn_interp/pallas_call | solution.py:391
  58.6 8.7 %collective-permute-done.24.refs_0_ = bf16[2,2,128,256]{3,2,1,0:T(8,128)(2,1)S(1)} collective-permute-done((bf16[2,2,128,256]{3,2,1,0:T(8,128)(2,1)S(1)}, bf16[2,2,128,256]{3,2,1,0:T(8,128)(2,1)S(1)}, u32[]{:S(2)}, u32[]{:S(2)}) %collective-permute-start.24) | collective-permute-done | bytes 262176 | tf_op jit(solution)/shard_map/ppermute | solution.py:380
  68.3 4.4 %collective-permute-done.31.refs_0_.refs_1_.refs_3_ = bf16[2,2,128,256]{3,2,1,0:T(8,128)(2,1)S(1)} collective-permute-done((bf16[2,2,128,256]{3,2,1,0:T(8,128)(2,1)S(1)}, bf16[2,2,128,256]{3,2,1,0:T(8,128)(2,1)S(1)}, u32[]{:S(2)}, u32[]{:S(2)}) %collective-permute-start.31) | collective-permute-done | bytes 262176 | tf_op jit(solution)/shard_map/ppermute | solution.py:381
  72.9 2.3 %collective-permute-done.27.refs_0_.refs_2_ = bf16[2,2,128,256]{3,2,1,0:T(8,128)(2,1)S(1)} collective-permute-done((bf16[2,2,128,256]{3,2,1,0:T(8,128)(2,1)S(1)}, bf16[2,2,128,256]{3,2,1,0:T(8,128)(2,1)S(1)}, u32[]{:S(2)}, u32[]{:S(2)}) %collective-permute-start.27) | collective-permute-done | bytes 262176 | tf_op jit(solution)/shard_map/ppermute | solution.py:427
  78.9 5.7 %collective-permute-done.29.refs_4_ = bf16[2,2,128,256]{3,2,1,0:T(8,128)(2,1)S(1)} collective-permute-done((bf16[2,2,128,256]{3,2,1,0:T(8,128)(2,1)S(1)}, bf16[2,2,128,256]{3,2,1,0:T(8,128)(2,1)S(1)}, u32[]{:S(2)}, u32[]{:S(2)}) %collective-permute-start.29) | collective-permute-done | bytes 262176 | tf_op jit(solution)/shard_map/ppermute | solution.py:428
  84.7 4.4 %collective-permute-done.32.refs_1_ = bf16[2,2,128,256]{3,2,1,0:T(8,128)(2,1)S(1)} collective-permute-done((bf16[2,2,128,256]{3,2,1,0:T(8,128)(2,1)S(1)}, bf16[2,2,128,256]{3,2,1,0:T(8,128)(2,1)S(1)}, u32[]{:S(2)}, u32[]{:S(2)}) %collective-permute-start.32) | collective-permute-done | bytes 262176 | tf_op jit(solution)/shard_map/ppermute | solution.py:433
  91.1 1.9 %ocean.1 = bf16[32,128,256]{2,1,0:T(8,128)(2,1)} custom-call(s32[1,128]{1,0:T(1,128)S(1)} %pad_bitcast_fusion.scalar_ref, s32[2,32]{1,0:T(2,128)S(1)} %bitcast.12, s32[2,32]{1,0:T(2,128)S(1)} %bitcast.13, bf16[32,128,256]{2,1,0:T(8,128)(2,1)S(1)} %turn_interp.1.interp_ref, bf16[48,128,256]{2,1,0:T(8,128)(2,1)S(1)} %collect.3.tiles_ref), custom_call_target="tpu_custom_call" | custom-call | tf_op jit(solution)/shard_map/ocean/pallas_call | solution.py:441
  (76 shorter events, 20.7 us)
Async XLA Ops:
  2.2 10.1 %collective-permute-start = (bf16[1,2,128,256]{3,2,1,0:T(8,128)(2,1)S(1)}, bf16[1,2,128,256]{3,2,1,0:T(8,128)(2,1)S(1)}, u32[]{:S(2)}, u32[]{:S(2)}) collective-permute-start(bf16[1,2,128,256]{3,2,1,0:T(8,128)(2,1)S(1)} %get-tuple-element.54), channel_id=1, source_target_pairs={{0,1},{1,0},{2,3},{3,2},{4,5},{5,4},{6,7},{7,6},{8,9},{9,8},{10,11... | collective-permute-start | bytes 393224 | tf_op jit(solution)/shard_map/ppermute | solution.py:289
  2.7 9.6 %collective-permute-start.1 = (bf16[1,2,128,256]{3,2,1,0:T(8,128)(2,1)S(1)}, bf16[1,2,128,256]{3,2,1,0:T(8,128)(2,1)S(1)}, u32[]{:S(2)}, u32[]{:S(2)}) collective-permute-start(bf16[1,2,128,256]{3,2,1,0:T(8,128)(2,1)S(1)} %get-tuple-element.57), channel_id=1, source_target_pairs={{0,1},{1,0},{2,3},{3,2},{4,5},{5,4},{6,7},{7,6},{8,9},{9,8},{10,11... | collective-permute-start | bytes 393224 | tf_op jit(solution)/shard_map/ppermute | solution.py:289
  2.8 11.2 %collective-permute-start.3 = (bf16[2,1,128,256]{3,2,1,0:T(8,128)(2,1)S(1)}, bf16[2,1,128,256]{3,2,1,0:T(8,128)(2,1)S(1)}, u32[]{:S(2)}, u32[]{:S(2)}) collective-permute-start(bf16[2,1,128,256]{3,2,1,0:T(8,128)(2,1)S(1)} %get-tuple-element.55.refs_3_), channel_id=1, source_target_pairs={{0,2},{2,0},{4,6},{6,4},{8,10},{10,8},{12,14},{14,12},{1,3},{3,1},... | collective-permute-start | bytes 393224 | tf_op jit(solution)/shard_map/ppermute | solution.py:346
  5.7 8.3 %collective-permute-start.4 = (bf16[2,1,128,256]{3,2,1,0:T(8,128)(2,1)S(1)}, bf16[2,1,128,256]{3,2,1,0:T(8,128)(2,1)S(1)}, u32[]{:S(2)}, u32[]{:S(2)}) collective-permute-start(bf16[2,1,128,256]{3,2,1,0:T(8,128)(2,1)S(1)} %get-tuple-element.56.refs_4_), channel_id=1, source_target_pairs={{0,14},{2,4},{4,2},{6,8},{8,6},{10,12},{12,10},{14,0},{1,15},{3,5}... | collective-permute-start | bytes 393224 | tf_op jit(solution)/shard_map/ppermute | solution.py:347
  14.6 6.6 %collective-permute-start.2 = (bf16[1,2,128,256]{3,2,1,0:T(8,128)(2,1)S(1)}, bf16[1,2,128,256]{3,2,1,0:T(8,128)(2,1)S(1)}, u32[]{:S(2)}, u32[]{:S(2)}) collective-permute-start(bf16[1,2,128,256]{3,2,1,0:T(8,128)(2,1)S(1)} %get-tuple-element.60), channel_id=1, source_target_pairs={{0,1},{1,0},{2,3},{3,2},{4,5},{5,4},{6,7},{7,6},{8,9},{9,8},{10,11... | collective-permute-start | bytes 393224 | tf_op jit(solution)/shard_map/ppermute | solution.py:289
  17.7 8.4 %collective-permute-start.9 = (bf16[2,1,128,256]{3,2,1,0:T(8,128)(2,1)S(1)}, bf16[2,1,128,256]{3,2,1,0:T(8,128)(2,1)S(1)}, u32[]{:S(2)}, u32[]{:S(2)}) collective-permute-start(bf16[2,1,128,256]{3,2,1,0:T(8,128)(2,1)S(1)} %get-tuple-element.64.refs_4_), channel_id=1, source_target_pairs={{0,2},{2,0},{4,6},{6,4},{8,10},{10,8},{12,14},{14,12},{1,3},{3,1},... | collective-permute-start | bytes 393224 | tf_op jit(solution)/shard_map/ppermute | solution.py:346
  17.7 8.4 %collective-permute-start.10 = (bf16[2,1,128,256]{3,2,1,0:T(8,128)(2,1)S(1)}, bf16[2,1,128,256]{3,2,1,0:T(8,128)(2,1)S(1)}, u32[]{:S(2)}, u32[]{:S(2)}) collective-permute-start(bf16[2,1,128,256]{3,2,1,0:T(8,128)(2,1)S(1)} %get-tuple-element.65.refs_5_), channel_id=1, source_target_pairs={{0,14},{2,4},{4,2},{6,8},{8,6},{10,12},{12,10},{14,0},{1,15},{3,5}... | collective-permute-start | bytes 393224 | tf_op jit(solution)/shard_map/ppermute | solution.py:347
  26.6 6.6 %collective-permute-start.8 = (bf16[1,2,128,256]{3,2,1,0:T(8,128)(2,1)S(1)}, bf16[1,2,128,256]{3,2,1,0:T(8,128)(2,1)S(1)}, u32[]{:S(2)}, u32[]{:S(2)}) collective-permute-start(bf16[1,2,128,256]{3,2,1,0:T(8,128)(2,1)S(1)} %get-tuple-element.69), channel_id=1, source_target_pairs={{0,1},{1,0},{2,3},{3,2},{4,5},{5,4},{6,7},{7,6},{8,9},{9,8},{10,11... | collective-permute-start | bytes 393224 | tf_op jit(solution)/shard_map/ppermute | solution.py:289
  29.8 8.4 %collective-permute-start.15 = (bf16[2,1,128,256]{3,2,1,0:T(8,128)(2,1)S(1)}, bf16[2,1,128,256]{3,2,1,0:T(8,128)(2,1)S(1)}, u32[]{:S(2)}, u32[]{:S(2)}) collective-permute-start(bf16[2,1,128,256]{3,2,1,0:T(8,128)(2,1)S(1)} %get-tuple-element.73.refs_5_), channel_id=1, source_target_pairs={{0,2},{2,0},{4,6},{6,4},{8,10},{10,8},{12,14},{14,12},{1,3},{3,1},... | collective-permute-start | bytes 393224 | tf_op jit(solution)/shard_map/ppermute | solution.py:346
  30.1 8.1 %collective-permute-start.16 = (bf16[2,1,128,256]{3,2,1,0:T(8,128)(2,1)S(1)}, bf16[2,1,128,256]{3,2,1,0:T(8,128)(2,1)S(1)}, u32[]{:S(2)}, u32[]{:S(2)}) collective-permute-start(bf16[2,1,128,256]{3,2,1,0:T(8,128)(2,1)S(1)} %get-tuple-element.74.refs_6_), channel_id=1, source_target_pairs={{0,14},{2,4},{4,2},{6,8},{8,6},{10,12},{12,10},{14,0},{1,15},{3,5}... | collective-permute-start | bytes 393224 | tf_op jit(solution)/shard_map/ppermute | solution.py:347
  38.7 6.6 %collective-permute-start.14 = (bf16[1,2,128,256]{3,2,1,0:T(8,128)(2,1)S(1)}, bf16[1,2,128,256]{3,2,1,0:T(8,128)(2,1)S(1)}, u32[]{:S(2)}, u32[]{:S(2)}) collective-permute-start(bf16[1,2,128,256]{3,2,1,0:T(8,128)(2,1)S(1)} %get-tuple-element.79), channel_id=1, source_target_pairs={{0,1},{1,0},{2,3},{3,2},{4,5},{5,4},{6,7},{7,6},{8,9},{9,8},{10,11... | collective-permute-start | bytes 393224 | tf_op jit(solution)/shard_map/ppermute | solution.py:289
  41.9 7.4 %collective-permute-start.20 = (bf16[2,1,128,256]{3,2,1,0:T(8,128)(2,1)S(1)}, bf16[2,1,128,256]{3,2,1,0:T(8,128)(2,1)S(1)}, u32[]{:S(2)}, u32[]{:S(2)}) collective-permute-start(bf16[2,1,128,256]{3,2,1,0:T(8,128)(2,1)S(1)} %get-tuple-element.83.refs_4_), channel_id=1, source_target_pairs={{0,2},{2,0},{4,6},{6,4},{8,10},{10,8},{12,14},{14,12},{1,3},{3,1},... | collective-permute-start | bytes 393224 | tf_op jit(solution)/shard_map/ppermute | solution.py:346
  42.1 8.1 %collective-permute-start.21 = (bf16[2,1,128,256]{3,2,1,0:T(8,128)(2,1)S(1)}, bf16[2,1,128,256]{3,2,1,0:T(8,128)(2,1)S(1)}, u32[]{:S(2)}, u32[]{:S(2)}) collective-permute-start(bf16[2,1,128,256]{3,2,1,0:T(8,128)(2,1)S(1)} %get-tuple-element.84.refs_5_), channel_id=1, source_target_pairs={{0,14},{2,4},{4,2},{6,8},{8,6},{10,12},{12,10},{14,0},{1,15},{3,5}... | collective-permute-start | bytes 393224 | tf_op jit(solution)/shard_map/ppermute | solution.py:347
  47.0 11.6 %collective-permute-start.26 = (bf16[2,2,128,256]{3,2,1,0:T(8,128)(2,1)S(1)}, bf16[2,2,128,256]{3,2,1,0:T(8,128)(2,1)S(1)}, u32[]{:S(2)}, u32[]{:S(2)}) collective-permute-start(bf16[2,2,128,256]{3,2,1,0:T(8,128)(2,1)S(1)} %get-tuple-element.89), channel_id=1, source_target_pairs={{0,2},{2,0},{4,6},{6,4},{8,10},{10,8},{12,14},{14,12},{1,3},{3,1},... | collective-permute-start | bytes 786440 | tf_op jit(solution)/shard_map/ppermute | solution.py:426
  47.1 20.3 %collective-permute-start.24 = (bf16[2,2,128,256]{3,2,1,0:T(8,128)(2,1)S(1)}, bf16[2,2,128,256]{3,2,1,0:T(8,128)(2,1)S(1)}, u32[]{:S(2)}, u32[]{:S(2)}) collective-permute-start(bf16[2,2,128,256]{3,2,1,0:T(8,128)(2,1)S(1)} %get-tuple-element.89), channel_id=1, source_target_pairs={{0,8},{2,10},{4,12},{6,14},{8,0},{10,2},{12,4},{14,6},{1,9},{3,11}... | collective-permute-start | bytes 786440 | tf_op jit(solution)/shard_map/ppermute | solution.py:380
  53.7 19.1 %collective-permute-start.31 = (bf16[2,2,128,256]{3,2,1,0:T(8,128)(2,1)S(1)}, bf16[2,2,128,256]{3,2,1,0:T(8,128)(2,1)S(1)}, u32[]{:S(2)}, u32[]{:S(2)}) collective-permute-start(bf16[2,2,128,256]{3,2,1,0:T(8,128)(2,1)S(1)} %get-tuple-element.95.first_ref), channel_id=1, source_target_pairs={{0,8},{2,10},{4,12},{6,14},{8,0},{10,2},{12,4},{14,6},{1,9},{3,11}... | collective-permute-start | bytes 786440 | tf_op jit(solution)/shard_map/ppermute | solution.py:381
  67.3 7.9 %collective-permute-start.27 = (bf16[2,2,128,256]{3,2,1,0:T(8,128)(2,1)S(1)}, bf16[2,2,128,256]{3,2,1,0:T(8,128)(2,1)S(1)}, u32[]{:S(2)}, u32[]{:S(2)}) collective-permute-start(bf16[2,2,128,256]{3,2,1,0:T(8,128)(2,1)S(1)} %collective-permute-done.24.refs_0_), channel_id=1, source_target_pairs={{0,2},{2,0},{4,6},{6,4},{8,10},{10,8},{12,14},{14,12},{1,3},{3,1},... | collective-permute-start | bytes 786440 | tf_op jit(solution)/shard_map/ppermute | solution.py:427
  68.3 10.1 %collective-permute-start.25 = (bf16[2,2,128,256]{3,2,1,0:T(8,128)(2,1)S(1)}, bf16[2,2,128,256]{3,2,1,0:T(8,128)(2,1)S(1)}, u32[]{:S(2)}, u32[]{:S(2)}) collective-permute-start(bf16[2,2,128,256]{3,2,1,0:T(8,128)(2,1)S(1)} %collective-permute-done.24.refs_0_), channel_id=1, source_target_pairs={{0,1},{1,0},{2,3},{3,2},{4,5},{5,4},{6,7},{7,6},{8,9},{9,8},{10,11... | collective-permute-start | bytes 786440 | tf_op jit(solution)/shard_map/ppermute | solution.py:289
  75.4 9.3 %collective-permute-start.29 = (bf16[2,2,128,256]{3,2,1,0:T(8,128)(2,1)S(1)}, bf16[2,2,128,256]{3,2,1,0:T(8,128)(2,1)S(1)}, u32[]{:S(2)}, u32[]{:S(2)}) collective-permute-start(bf16[2,2,128,256]{3,2,1,0:T(8,128)(2,1)S(1)} %pick.2), channel_id=1, source_target_pairs={{0,4},{2,6},{4,0},{6,2},{8,12},{10,14},{12,8},{14,10},{1,5},{3,7},... | collective-permute-start | bytes 786440 | tf_op jit(solution)/shard_map/ppermute | solution.py:428
  75.4 13.7 %collective-permute-start.32 = (bf16[2,2,128,256]{3,2,1,0:T(8,128)(2,1)S(1)}, bf16[2,2,128,256]{3,2,1,0:T(8,128)(2,1)S(1)}, u32[]{:S(2)}, u32[]{:S(2)}) collective-permute-start(bf16[2,2,128,256]{3,2,1,0:T(8,128)(2,1)S(1)} %get-tuple-element.96), channel_id=1, source_target_pairs={{0,2},{2,4},{4,6},{6,0},{8,10},{10,12},{12,14},{14,8},{1,3},{3,5},... | collective-permute-start | bytes 786440 | tf_op jit(solution)/shard_map/ppermute | solution.py:433
  76.7 12.6 %collective-permute-start.35 = (bf16[2,2,128,256]{3,2,1,0:T(8,128)(2,1)S(1)}, bf16[2,2,128,256]{3,2,1,0:T(8,128)(2,1)S(1)}, u32[]{:S(2)}, u32[]{:S(2)}) collective-permute-start(bf16[2,2,128,256]{3,2,1,0:T(8,128)(2,1)S(1)} %get-tuple-element.97), channel_id=1, source_target_pairs={{0,6},{2,0},{4,2},{6,4},{8,14},{10,8},{12,10},{14,12},{1,7},{3,1},... | collective-permute-start | bytes 786440 | tf_op jit(solution)/shard_map/ppermute | solution.py:434
  78.4 11.4 %collective-permute-start.34 = (bf16[2,2,128,256]{3,2,1,0:T(8,128)(2,1)S(1)}, bf16[2,2,128,256]{3,2,1,0:T(8,128)(2,1)S(1)}, u32[]{:S(2)}, u32[]{:S(2)}) collective-permute-start(bf16[2,2,128,256]{3,2,1,0:T(8,128)(2,1)S(1)} %collective-permute-done.31.refs_0_.refs_1_.refs_3_), channel_id=1, source_target_pairs={{0,1},{1,0},{2,3},{3,2},{4,5},{5,4},{6,7},{7,6},{8,9},{9,8},{10,11... | collective-permute-start | bytes 786440 | tf_op jit(solution)/shard_map/ppermute | solution.py:289
  78.4 11.2 %collective-permute-start.28 = (bf16[2,2,128,256]{3,2,1,0:T(8,128)(2,1)S(1)}, bf16[2,2,128,256]{3,2,1,0:T(8,128)(2,1)S(1)}, u32[]{:S(2)}, u32[]{:S(2)}) collective-permute-start(bf16[2,2,128,256]{3,2,1,0:T(8,128)(2,1)S(1)} %collective-permute-done.27.refs_0_.refs_2_), channel_id=1, source_target_pairs={{0,1},{1,0},{2,3},{3,2},{4,5},{5,4},{6,7},{7,6},{8,9},{9,8},{10,11... | collective-permute-start | bytes 786440 | tf_op jit(solution)/shard_map/ppermute | solution.py:289
  84.7 5.0 %collective-permute-start.30 = (bf16[2,2,128,256]{3,2,1,0:T(8,128)(2,1)S(1)}, bf16[2,2,128,256]{3,2,1,0:T(8,128)(2,1)S(1)}, u32[]{:S(2)}, u32[]{:S(2)}) collective-permute-start(bf16[2,2,128,256]{3,2,1,0:T(8,128)(2,1)S(1)} %collective-permute-done.29.refs_4_), channel_id=1, source_target_pairs={{0,1},{1,0},{2,3},{3,2},{4,5},{5,4},{6,7},{7,6},{8,9},{9,8},{10,11... | collective-permute-start | bytes 786440 | tf_op jit(solution)/shard_map/ppermute | solution.py:289
  (16 other events, 30.4 us)

commit v5 on v4

--- a/solution.py
+++ b/solution.py
@@ -56,7 +56,7 @@
 
 
 def setup_kernel(
-    scalar_ref, pos_hbm, codes_hbm, w_ref, coef_ref, codes_ref, inner_ref, edge_ref, pos_ref, sems, small_sems
+    scalar_ref, pos_hbm, codes_hbm, w_ref, coef_ref, index_ref, inner_ref, edge_ref, pos_ref, codes_ref, sems, small_sems
 ):
     small = [
         pltpu.make_async_copy(pos_hbm, pos_ref, small_sems.at[0]),
@@ -81,6 +81,13 @@
         copy.start()
     for copy in small:
         copy.wait()
+    codes = codes_ref[...]
+    third = (codes * 11) // 32
+    row = lax.broadcasted_iota(jnp.int32, codes.shape, 0) + third - 1
+    row = jnp.where(row < 0, rows, row)
+    col = lax.broadcasted_iota(jnp.int32, codes.shape, 1) + codes - 3 * third - 1
+    col = jnp.where(scalar_ref[0, 1 + cols] == 1, cols - 1 - col, col)
+    index_ref[...] = row * (cols + 2) + 1 + col
     low = lax.broadcasted_iota(jnp.int32, (nodes, nodes), 1) < nodes // 2
     for a in range(rows):
         for b in range(cols):
@@ -136,7 +143,7 @@
     return fa - x01 * radial, fb - x2_low * radial
 
 
-def stage_kernel(edge, number, stages, scale, scalar_ref, codes_ref, w_ref, coef_ref, *refs):
+def stage_kernel(edge, number, stages, scale, scalar_ref, index_ref, w_ref, coef_ref, *refs):
     refs = list(refs)
     ext = refs.pop()
     rows, cols = coef_ref.shape[:2]
@@ -169,20 +176,12 @@
     blend_ref = refs.pop(0) if blend else None
     next_ref, *outs = refs
     columns = (0, cols - 1) if edge else tuple(range(1, cols - 1))
-    eastward = 1 - 2 * scalar_ref[0, 1 + cols]
-
-    def neighbour(code, a, c):
-        third = (code * 11) // 32
-        row = a + third - 1
-        row = jnp.where(row < 0, rows, row)
-        return row * wide + 1 + c + eastward * (code - 3 * third - 1)
-
     low = lax.broadcasted_iota(jnp.int32, (nodes, feats // 2), 1) < feats // 4
     for a in range(rows):
         for place, c in enumerate(columns):
             b = scalar_ref[0, 1 + c]
             near = jnp.concatenate(
-                [ext[neighbour(codes_ref[a, b, k], a, c)] for k in range(taps)], axis=0
+                [ext[index_ref[a, b, k]] for k in range(taps)], axis=0
             )
             weights = jnp.concatenate(
                 [
@@ -203,7 +202,7 @@
                 )
             next_ref[a, place] = out
             rounded = out.astype(BF16)
-            if edge and not last:
+            if edge:
                 outs[place][a, 0] = rounded
             else:
                 outs[0][a, place] = rounded
@@ -234,7 +233,7 @@
 def collect_kernel(places, *refs):
     pieces, out_ref = refs[-1 - len(places) : -1], refs[-1]
     for place, piece in zip(places, pieces):
-        flat = piece.reshape(piece.shape[0] * piece.shape[1], *piece.shape[2:])
+        flat = piece.reshape(-1, *piece.shape[-2:])
         out_ref[pl.ds(place, flat.shape[0])] = flat[...]
 
 
@@ -254,10 +253,16 @@
     row, col = local_ids // cols, local_ids % cols
     col = jnp.where(owner_lon % 2 == 0, cols - 1 - col, col)
     inner_count = rows * (cols - 2)
-    inner_slot = (kind * 2 + away) * inner_count + row * (cols - 2) + col - 1
-    edge_slot = 6 * inner_count + (relative * 2 + away) * (2 * rows)
-    edge_slot += 2 * row + (col != 0).astype(jnp.int32)
-    slot_ref[...] = jnp.where((col == 0) | (col == cols - 1), edge_slot, inner_slot)
+    early, late = 2 * inner_count + 2 * rows, inner_count + 4 * rows
+    place = row * (cols - 2) + col - 1
+    on_far_edge = (col != 0).astype(jnp.int32)
+    edge_early = 2 * inner_count + on_far_edge * rows + row
+    edge_late = inner_count + (2 * on_far_edge + (relative == 2).astype(jnp.int32)) * rows + row
+    on_edge = (col == 0) | (col == cols - 1)
+    is_late = jnp.where(on_edge, (relative != 1).astype(jnp.int32), (kind == 2).astype(jnp.int32))
+    early_slot = jnp.where(on_edge, edge_early, kind * inner_count + place) + away * early
+    late_slot = jnp.where(on_edge, edge_late, place) + 2 * early + away * late
+    slot_ref[...] = jnp.where(is_late == 1, late_slot, early_slot)
 
     taps, tiles = slot_ref.shape
     copies = []
@@ -308,15 +313,16 @@
     edge_s = ((rows, 1) + tile, BF16)
     erow_s = ((1, 2) + tile, BF16)
 
-    own = vmem_call(
+    inner, irow, *edges = vmem_call(
         prep_kernel,
         "prep",
         [inner_s, irow_s, edge_s, edge_s, erow_s],
         [scalars, state],
     )
+    own = [inner, flip(irow), *edges]
 
     quarter = weights.shape[:2]
-    coef, codes, w_inner, w_edge = pl.pallas_call(
+    coef, index, w_inner, w_edge = pl.pallas_call(
         setup_kernel,
         out_shape=[
             pltpu.VMEM((rows, cols, 2, nodes, nodes), F32),
@@ -328,6 +334,7 @@
         out_specs=[VMEM] * 4,
         scratch_shapes=[
             pltpu.VMEM(positions.shape, F32),
+            pltpu.VMEM(stencil_codes.shape, jnp.int32),
             pltpu.SemaphoreType.DMA((weights.shape[0], cols)),
             pltpu.SemaphoreType.DMA((2,)),
         ],
@@ -345,23 +352,25 @@
         inner, irow, edge_a, edge_b, erow = own
         halo_a = lax.ppermute(edge_a, "lon", to_a)
         halo_b = lax.ppermute(edge_b, "lon", to_b)
-        near = [inner, flip(irow), edge_a, edge_b, flip(erow)]
+        near = [inner, irow, edge_a, edge_b, flip(erow)]
         own = {}
         for edge in (False, True):
             if edge:
-                halo_a, halo_b = lax.optimization_barrier((halo_a, halo_b, own[False][0]))[:2]
+                ahead = own[False]
+                if not last:
+                    ahead[1] = flip(ahead[1])
+                ahead = ahead if number else ahead[:1]
+                halo_a, halo_b = lax.optimization_barrier((halo_a, halo_b, *ahead))[:2]
                 corner_a, corner_b = flip(halo_a), flip(halo_b)
             far = [halo_a, halo_b, corner_a, corner_b] if edge else []
             field_s = ((rows, 2 if edge else cols - 2) + tile, F32)
             outs = [edge_s, edge_s, erow_s] if edge else [inner_s, irow_s]
-            if last:
-                outs = [((rows, 2 if edge else cols - 2) + tile, BF16)]
-            outs = ([field_s] if blend else []) + [field_s] + outs
+            outs = ([field_s] if blend else []) + [field_s] + (outs[:-1] if last else outs)
             results = vmem_call(
                 functools.partial(stage_kernel, edge, number, stages, scale),
                 ("edge" if edge else "inner") + ("_last" if last else ""),
                 outs,
-                [scalars, codes, w_edge if edge else w_inner, coef]
+                [scalars, index, w_edge if edge else w_inner, coef]
                 + ([] if last else [state])
                 + fields[edge]
                 + near
@@ -372,13 +381,12 @@
                 fields[edge], results = list(results[:2]), results[2:]
             else:
                 fields[edge], results = (fields[edge] + [results[0]])[-2:], results[1:]
-            own[edge] = results
+            own[edge] = list(results)
         own = own[False] + own[True]
     next_i, next_e = fields[False][-1], fields[True][-1]
-    final_i, final_e = own
+    final_i, final_a, final_b = own
     opposite = [(i, (i + middle) % lon_count) for i in range(lon_count)]
     center_i = lax.ppermute(final_i, "lon", opposite)
-    center_e = lax.ppermute(final_e, "lon", opposite)
 
     (next_state,) = pl.pallas_call(
         join_kernel,
@@ -413,30 +421,34 @@
             [scalars, *pieces],
         )
 
-    def collect(tiles, place, pieces):
-        size = pieces[0].shape[0] * pieces[0].shape[1]
+    def collect(name, size, pieces, tiles=None, place=0):
+        places = [place + sum(counted(piece) for piece in pieces[:i]) for i in range(len(pieces))]
         return vmem_call(
-            functools.partial(collect_kernel, [place + i * size for i in range(len(pieces))]),
-            "collect",
-            [((6 * rows * cols,) + tile, BF16)],
+            functools.partial(collect_kernel, places),
+            name,
+            [((size,) + tile, BF16)],
             ([] if tiles is None else [tiles]) + pieces,
             aliases=None if tiles is None else {0: 0},
         )[0]
 
+    def counted(piece):
+        return piece.size // (nodes * feats)
+
     native = lax.ppermute(final_i, "lon", to_a)
     paired = lax.ppermute(after(center_i, native, next_state, turned_interp), "lon", to_a)
+    center_a = lax.ppermute(final_a, "lon", opposite)
+    center_b = lax.ppermute(after(final_b, paired), "lon", opposite)
     passed = lax.ppermute(pick(flags, native, paired)[0], "lon", onward)
-    tiles = collect(
-        None, 0, [center_i, flip(center_i), paired, flip(paired), passed, flip(passed)]
-    )
-    going_up, going_down = pick(flags + 1, final_e, center_e, center_e)
-    below = lax.ppermute(going_up, "lon", up)
-    above = lax.ppermute(going_down, "lon", down)
-    tiles = collect(
-        tiles,
-        6 * inner_count,
-        [below, flip(below), center_e, flip(center_e), above, flip(above)],
-    )
+    late = [passed]
+    for final, center in ((final_a, center_a), (final_b, center_b)):
+        going_up, going_down = pick(flags + 1, final, center, center)
+        late += [lax.ppermute(going_up, "lon", up), lax.ppermute(going_down, "lon", down)]
+    early_size, late_size = 2 * inner_count + 2 * rows, inner_count + 4 * rows
+    size = 2 * (early_size + late_size)
+    early = collect("early", early_size, [center_i, paired, center_a, center_b])
+    late = collect("late", late_size, late)
+    tiles = collect("gather", size, [early, flip(early), late])
+    tiles = collect("gather", size, [flip(late)], tiles, size - late_size)
     block = 4
     ocean = pl.pallas_call(
         functools.partial(ocean_kernel, (lon_count, lat_count, rows, cols, block)),

time: 93.4 us -> 92 us (0.985)
  waiting for transfers between devices: 38.5 us -> 34 us
  starting transfers between devices: 29.5 us -> 32.9 us
    ppermute x1, waiting for transfers between devices: 5.74 us -> 0.01 us  [local(): passed = lax.ppermute(pick(flags, native, paired)[0], 'lon', onward)]
    ppermute x1, waiting for transfers between devices: 2.33 us -> 7.03 us  [local(): lax.ppermute(after(center_i, native, next_state, turned_interp), 'lon', t...]
    ppermute x1, waiting for transfers between devices: 8.72 us -> 4.48 us  [local(): center_i = lax.ppermute(final_i, 'lon', opposite)]
    ppermute x1, starting transfers between devices: 0.07 us -> 2.39 us  [local(): passed = lax.ppermute(pick(flags, native, paired)[0], 'lon', onward)]
    ppermute x3 -> x6, starting transfers between devices: 4.56 us -> 5.96 us  [the longest x2 4.51 us: local(): lax.ppermute(going_down, 'lon', down)]
    ppermute x22 -> x18, waiting for transfers between devices: 5.29 us -> 6.12 us  [flip(): return lax.ppermute(value, 'lat', swap)]
    ppermute x22 -> x18, starting transfers between devices: 4.74 us -> 4.15 us  [flip(): return lax.ppermute(value, 'lat', swap)]
    pallas_call x13 -> x16, Pallas kernels: 14.5 us -> 14.3 us  [vmem_call(): pl.pallas_call(kernel, out_shape=[pltpu.VMEM(shape, dtype) for shape, dty...]
  transfers between devices with their start and end apart: 37 -> 36, of which waited for: 19 -> 18; matrix products, arithmetic and copies ran while one was open for 0% -> 0% of each run, Pallas kernels for 22% -> 19%
where the time goes in v5:
time: 92 us; the launch traced here: 91.8 us
  waiting for transfers between devices  34 us (37%)
  starting transfers between devices  32.9 us (36%)
  Pallas kernels  22.5 us (24%)
  local copies, waits for them, and re-layouts  1.33 us (1%)
  between operations  1.12 us (1%)
    pallas_call x16, Pallas kernels, vmem_call(): pl.pallas_call(kernel, out_shape=[pltpu.VMEM(shape, dtype) for shape, dty...  14.3 us
    ppermute x4, starting transfers between devices, local(): halo_b = lax.ppermute(edge_b, 'lon', to_b)  13.5 us
    ppermute x1, waiting for transfers between devices, local(): lax.ppermute(after(center_i, native, next_state, turned_interp), 'lon', t...  7.03 us
    ppermute x2, waiting for transfers between devices, local(): lax.ppermute(going_up, 'lon', up)  6.72 us
    ppermute x4, waiting for transfers between devices, local(): halo_a = lax.ppermute(edge_a, 'lon', to_a)  6.26 us
    ppermute x18, waiting for transfers between devices, flip(): return lax.ppermute(value, 'lat', swap)  6.12 us
    ppermute x2, starting transfers between devices, local(): lax.ppermute(going_down, 'lon', down)  4.51 us
    ppermute x1, waiting for transfers between devices, local(): center_i = lax.ppermute(final_i, 'lon', opposite)  4.48 us
  transfers between devices with their start and end apart: 36, of which 18 were waited for; matrix products, arithmetic and copies ran while one was open for 0% of the time, Pallas kernels for 19%

profile of v5, /device:TPU:0, one launch (start us, length us, event | category | flops | bytes accessed | tf_op | source)
XLA Modules:
  0.0 91.8 jit_solution(16371646573837645011)
XLA Ops:
  2.8 2.9 %collective-permute-start.3 = (bf16[2,1,128,256]{3,2,1,0:T(8,128)(2,1)S(1)}, bf16[2,1,128,256]{3,2,1,0:T(8,128)(2,1)S(1)}, u32[]{:S(2)}, u32[]{:S(2)}) collective-permute-start(bf16[2,1,128,256]{3,2,1,0:T(8,128)(2,1)S(1)} %get-tuple-element.59.refs_3_), channel_id=1, source_target_pairs={{0,2},{2,0},{4,6},{6,4},{8,10},{10,8},{12,14},{14,12},{1,3},{3,1},... | collective-permute-start | bytes 393224 | tf_op jit(solution)/shard_map/ppermute | solution.py:353
  5.7 3.6 %collective-permute-start.4 = (bf16[2,1,128,256]{3,2,1,0:T(8,128)(2,1)S(1)}, bf16[2,1,128,256]{3,2,1,0:T(8,128)(2,1)S(1)}, u32[]{:S(2)}, u32[]{:S(2)}) collective-permute-start(bf16[2,1,128,256]{3,2,1,0:T(8,128)(2,1)S(1)} %get-tuple-element.60.refs_4_), channel_id=1, source_target_pairs={{0,14},{2,4},{4,2},{6,8},{8,6},{10,12},{12,10},{14,0},{1,15},{3,5}... | collective-permute-start | bytes 393224 | tf_op jit(solution)/shard_map/ppermute | solution.py:354
  9.3 3.0 %setup.1 = (f32[2,4,2,128,128]{4,3,2,1,0:T(8,128)S(1)}, s32[2,4,6]{2,1,0:T(4,128)S(1)}, bf16[4,2,2,6,128,128]{5,4,3,2,1,0:T(8,128)(2,1)S(1)}, bf16[4,2,2,6,128,128]{5,4,3,2,1,0:T(8,128)(2,1)S(1)}) custom-call(s32[1,128]{1,0:T(1,128)S(1)} %pad_bitcast_fusion.scalar_ref, f32[3,2,4,128]{3,2,1,0:T(4,128)} %pos_hbm.1, s32[2,4,6]{2,1,0:T(4,128)} %codes_hbm.1, ...), custom_call_target="tpu_custom_call" | custom-call | tf_op jit(solution)/shard_map/setup/pallas_call | solution.py:325
  12.3 1.6 %inner.3 = (f32[2,2,128,256]{3,2,1,0:T(8,128)S(1)}, bf16[2,2,128,256]{3,2,1,0:T(8,128)(2,1)S(1)}, bf16[1,2,128,256]{3,2,1,0:T(8,128)(2,1)S(1)}) custom-call(s32[1,128]{1,0:T(1,128)S(1)} %pad_bitcast_fusion.scalar_ref, s32[2,4,6]{2,1,0:T(4,128)S(1)} %get-tuple-element.54.index_ref, bf16[4,2,2,6,128,128]{5,4,3,2,1,0:T(8,128)(2,1)S(1)} %get-tuple-element.55.w_ref, ...), custom_call_target="tpu_custom_call" | custom-call | flops 1000 | bytes 1000 | tf_op jit(solution)/shard_map/inner/pallas_call | solution.py:28
  15.6 1.6 %edge.3 = (f32[2,2,128,256]{3,2,1,0:T(8,128)S(1)}, bf16[2,1,128,256]{3,2,1,0:T(8,128)(2,1)S(1)}, bf16[2,1,128,256]{3,2,1,0:T(8,128)(2,1)S(1)}, bf16[1,2,128,256]{3,2,1,0:T(8,128)(2,1)S(1)}) custom-call(s32[1,128]{1,0:T(1,128)S(1)} %pad_bitcast_fusion.scalar_ref, s32[2,4,6]{2,1,0:T(4,128)S(1)} %get-tuple-element.54.index_ref, ...), custom_call_target="tpu_custom_call" | custom-call | flops 1000 | bytes 1000 | tf_op jit(solution)/shard_map/edge/pallas_call | solution.py:28
  17.6 3.5 %collective-permute-start.10 = (bf16[2,1,128,256]{3,2,1,0:T(8,128)(2,1)S(1)}, bf16[2,1,128,256]{3,2,1,0:T(8,128)(2,1)S(1)}, u32[]{:S(2)}, u32[]{:S(2)}) collective-permute-start(bf16[2,1,128,256]{3,2,1,0:T(8,128)(2,1)S(1)} %get-tuple-element.69.refs_5_), channel_id=1, source_target_pairs={{0,14},{2,4},{4,2},{6,8},{8,6},{10,12},{12,10},{14,0},{1,15},{3,5}... | collective-permute-start | bytes 393224 | tf_op jit(solution)/shard_map/ppermute | solution.py:354
  22.9 3.2 %collective-permute-done.9.refs_7_ = bf16[2,1,128,256]{3,2,1,0:T(8,128)(2,1)S(1)} collective-permute-done((bf16[2,1,128,256]{3,2,1,0:T(8,128)(2,1)S(1)}, bf16[2,1,128,256]{3,2,1,0:T(8,128)(2,1)S(1)}, u32[]{:S(2)}, u32[]{:S(2)}) %collective-permute-start.9) | collective-permute-done | bytes 131104 | tf_op jit(solution)/shard_map/ppermute | solution.py:353
  27.6 1.6 %edge.4 = (f32[2,2,128,256]{3,2,1,0:T(8,128)S(1)}, bf16[2,1,128,256]{3,2,1,0:T(8,128)(2,1)S(1)}, bf16[2,1,128,256]{3,2,1,0:T(8,128)(2,1)S(1)}, bf16[1,2,128,256]{3,2,1,0:T(8,128)(2,1)S(1)}) custom-call(s32[1,128]{1,0:T(1,128)S(1)} %pad_bitcast_fusion.scalar_ref, s32[2,4,6]{2,1,0:T(4,128)S(1)} %get-tuple-element.54.index_ref, ...), custom_call_target="tpu_custom_call" | custom-call | flops 1000 | bytes 1000 | tf_op jit(solution)/shard_map/edge/pallas_call | solution.py:28
  29.9 3.2 %collective-permute-start.16 = (bf16[2,1,128,256]{3,2,1,0:T(8,128)(2,1)S(1)}, bf16[2,1,128,256]{3,2,1,0:T(8,128)(2,1)S(1)}, u32[]{:S(2)}, u32[]{:S(2)}) collective-permute-start(bf16[2,1,128,256]{3,2,1,0:T(8,128)(2,1)S(1)} %get-tuple-element.78.refs_6_), channel_id=1, source_target_pairs={{0,14},{2,4},{4,2},{6,8},{8,6},{10,12},{12,10},{14,0},{1,15},{3,5}... | collective-permute-start | bytes 393224 | tf_op jit(solution)/shard_map/ppermute | solution.py:354
  33.1 1.7 %inner.5 = (f32[2,2,128,256]{3,2,1,0:T(8,128)S(1)}, f32[2,2,128,256]{3,2,1,0:T(8,128)S(1)}, bf16[2,2,128,256]{3,2,1,0:T(8,128)(2,1)S(1)}, bf16[1,2,128,256]{3,2,1,0:T(8,128)(2,1)S(1)}) custom-call(s32[1,128]{1,0:T(1,128)S(1)} %pad_bitcast_fusion.scalar_ref, s32[2,4,6]{2,1,0:T(4,128)S(1)} %get-tuple-element.54.index_ref, ...), custom_call_target="tpu_custom_call" | custom-call | flops 1000 | bytes 1000 | tf_op jit(solution)/shard_map/inner/pallas_call | solution.py:28
  34.9 3.1 %collective-permute-done.15.refs_8_ = bf16[2,1,128,256]{3,2,1,0:T(8,128)(2,1)S(1)} collective-permute-done((bf16[2,1,128,256]{3,2,1,0:T(8,128)(2,1)S(1)}, bf16[2,1,128,256]{3,2,1,0:T(8,128)(2,1)S(1)}, u32[]{:S(2)}, u32[]{:S(2)}) %collective-permute-start.15) | collective-permute-done | bytes 131104 | tf_op jit(solution)/shard_map/ppermute | solution.py:353
  39.5 1.7 %edge.5 = (f32[2,2,128,256]{3,2,1,0:T(8,128)S(1)}, f32[2,2,128,256]{3,2,1,0:T(8,128)S(1)}, bf16[2,1,128,256]{3,2,1,0:T(8,128)(2,1)S(1)}, bf16[2,1,128,256]{3,2,1...) custom-call(s32[1,128]{1,0:T(1,128)S(1)} %pad_bitcast_fusion.scalar_ref, s32[2,4,6]{2,1,0:T(4,128)S(1)} %get-tuple-element.54.index_ref, ...), custom_call_target="tpu_custom_call" | custom-call | flops 1000 | bytes 1000 | tf_op jit(solution)/shard_map/edge/pallas_call | solution.py:28
  41.9 3.2 %collective-permute-start.21 = (bf16[2,1,128,256]{3,2,1,0:T(8,128)(2,1)S(1)}, bf16[2,1,128,256]{3,2,1,0:T(8,128)(2,1)S(1)}, u32[]{:S(2)}, u32[]{:S(2)}) collective-permute-start(bf16[2,1,128,256]{3,2,1,0:T(8,128)(2,1)S(1)} %get-tuple-element.88.refs_5_), channel_id=1, source_target_pairs={{0,14},{2,4},{4,2},{6,8},{8,6},{10,12},{12,10},{14,0},{1,15},{3,5}... | collective-permute-start | bytes 393224 | tf_op jit(solution)/shard_map/ppermute | solution.py:354
  46.9 2.2 %collective-permute-start.24 = (bf16[2,2,128,256]{3,2,1,0:T(8,128)(2,1)S(1)}, bf16[2,2,128,256]{3,2,1,0:T(8,128)(2,1)S(1)}, u32[]{:S(2)}, u32[]{:S(2)}) collective-permute-start(bf16[2,2,128,256]{3,2,1,0:T(8,128)(2,1)S(1)} %get-tuple-element.93), channel_id=1, source_target_pairs={{0,8},{2,10},{4,12},{6,14},{8,0},{10,2},{12,4},{14,6},{1,9},{3,11}... | collective-permute-start | bytes 786440 | tf_op jit(solution)/shard_map/ppermute | solution.py:389
  51.6 1.8 %edge_last.1 = (f32[2,2,128,256]{3,2,1,0:T(8,128)S(1)}, bf16[2,1,128,256]{3,2,1,0:T(8,128)(2,1)S(1)}, bf16[2,1,128,256]{3,2,1,0:T(8,128)(2,1)S(1)}) custom-call(s32[1,128]{1,0:T(1,128)S(1)} %pad_bitcast_fusion.scalar_ref, s32[2,4,6]{2,1,0:T(4,128)S(1)} %get-tuple-element.54.index_ref, bf16[4,2,2,6,128,128]{5,4,3,2,1,0:T(8,128)(2,1)S(1)} %get-tuple-element.65.w_ref, ...), custom_call_target="tpu_custom_call" | custom-call | flops 1000 | bytes 1000 | tf_op jit(solution)/shard_map/edge_last/pallas_call | solution.py:28
  54.6 2.2 %turn_interp.1.interp_ref = bf16[32,128,256]{2,1,0:T(8,128)(2,1)S(1)} custom-call(bf16[32,2,128,128]{3,2,1,0:T(8,128)(2,1)} %interp_ref), custom_call_target="tpu_custom_call" | custom-call | tf_op jit(solution)/shard_map/turn_interp/pallas_call | solution.py:399
  56.8 4.5 %collective-permute-done.24.refs_0_ = bf16[2,2,128,256]{3,2,1,0:T(8,128)(2,1)S(1)} collective-permute-done((bf16[2,2,128,256]{3,2,1,0:T(8,128)(2,1)S(1)}, bf16[2,2,128,256]{3,2,1,0:T(8,128)(2,1)S(1)}, u32[]{:S(2)}, u32[]{:S(2)}) %collective-permute-start.24) | collective-permute-done | bytes 262176 | tf_op jit(solution)/shard_map/ppermute | solution.py:389
  62.4 7.0 %collective-permute-done.26.refs_1_.refs_0_ = bf16[2,2,128,256]{3,2,1,0:T(8,128)(2,1)S(1)} collective-permute-done((bf16[2,2,128,256]{3,2,1,0:T(8,128)(2,1)S(1)}, bf16[2,2,128,256]{3,2,1,0:T(8,128)(2,1)S(1)}, u32[]{:S(2)}, u32[]{:S(2)}) %collective-permute-start.26) | collective-permute-done | bytes 262176 | tf_op jit(solution)/shard_map/ppermute | solution.py:438
  69.5 2.4 %collective-permute-start.30 = (bf16[2,2,128,256]{3,2,1,0:T(8,128)(2,1)S(1)}, bf16[2,2,128,256]{3,2,1,0:T(8,128)(2,1)S(1)}, u32[]{:S(2)}, u32[]{:S(2)}) collective-permute-start(bf16[2,2,128,256]{3,2,1,0:T(8,128)(2,1)S(1)} %pick.3), channel_id=1, source_target_pairs={{0,4},{2,6},{4,0},{6,2},{8,12},{10,14},{12,8},{14,10},{1,5},{3,7},... | collective-permute-start | bytes 786440 | tf_op jit(solution)/shard_map/ppermute | solution.py:441
  72.4 2.6 %collective-permute-start.32 = (bf16[2,1,128,256]{3,2,1,0:T(8,128)(2,1)S(1)}, bf16[2,1,128,256]{3,2,1,0:T(8,128)(2,1)S(1)}, u32[]{:S(2)}, u32[]{:S(2)}) collective-permute-start(bf16[2,1,128,256]{3,2,1,0:T(8,128)(2,1)S(1)} %get-tuple-element.103), channel_id=1, source_target_pairs={{0,6},{2,0},{4,2},{6,4},{8,14},{10,8},{12,10},{14,12},{1,7},{3,1},... | collective-permute-start | bytes 393224 | tf_op jit(solution)/shard_map/ppermute | solution.py:445
  77.5 1.9 %collective-permute-start.34 = (bf16[2,1,128,256]{3,2,1,0:T(8,128)(2,1)S(1)}, bf16[2,1,128,256]{3,2,1,0:T(8,128)(2,1)S(1)}, u32[]{:S(2)}, u32[]{:S(2)}) collective-permute-start(bf16[2,1,128,256]{3,2,1,0:T(8,128)(2,1)S(1)} %get-tuple-element.105), channel_id=1, source_target_pairs={{0,6},{2,0},{4,2},{6,4},{8,14},{10,8},{12,10},{14,12},{1,7},{3,1},... | collective-permute-start | bytes 393224 | tf_op jit(solution)/shard_map/ppermute | solution.py:445
  79.4 5.3 %collective-permute-done.31.refs_1_ = bf16[2,1,128,256]{3,2,1,0:T(8,128)(2,1)S(1)} collective-permute-done((bf16[2,1,128,256]{3,2,1,0:T(8,128)(2,1)S(1)}, bf16[2,1,128,256]{3,2,1,0:T(8,128)(2,1)S(1)}, u32[]{:S(2)}, u32[]{:S(2)}) %collective-permute-start.31) | collective-permute-done | bytes 131104 | tf_op jit(solution)/shard_map/ppermute | solution.py:445
  87.6 2.1 %collective-permute-done.35.refs_1_ = bf16[12,128,256]{2,1,0:T(8,128)(2,1)S(1)} collective-permute-done((bf16[12,128,256]{2,1,0:T(8,128)(2,1)S(1)}, bf16[12,128,256]{2,1,0:T(8,128)(2,1)S(1)}, u32[]{:S(2)}, u32[]{:S(2)}) %collective-permute-start.35) | collective-permute-done | bytes 786464 | tf_op jit(solution)/shard_map/ppermute | solution.py:294
  89.8 1.9 %ocean.1 = bf16[32,128,256]{2,1,0:T(8,128)(2,1)} custom-call(s32[1,128]{1,0:T(1,128)S(1)} %pad_bitcast_fusion.scalar_ref, s32[2,32]{1,0:T(2,128)S(1)} %bitcast.12, s32[2,32]{1,0:T(2,128)S(1)} %bitcast.13, bf16[32,128,256]{2,1,0:T(8,128)(2,1)S(1)} %turn_interp.1.interp_ref, bf16[48,128,256]{2,1,0:T(8,128)(2,1)S(1)} %gather.3.tiles_ref), custom_call_target="tpu_custom_call" | custom-call | tf_op jit(solution)/shard_map/ocean/pallas_call | solution.py:453
  (77 shorter events, 22.7 us)
Async XLA Ops:
  2.2 10.1 %collective-permute-start = (bf16[1,2,128,256]{3,2,1,0:T(8,128)(2,1)S(1)}, bf16[1,2,128,256]{3,2,1,0:T(8,128)(2,1)S(1)}, u32[]{:S(2)}, u32[]{:S(2)}) collective-permute-start(bf16[1,2,128,256]{3,2,1,0:T(8,128)(2,1)S(1)} %get-tuple-element.58), channel_id=1, source_target_pairs={{0,1},{1,0},{2,3},{3,2},{4,5},{5,4},{6,7},{7,6},{8,9},{9,8},{10,11... | collective-permute-start | bytes 393224 | tf_op jit(solution)/shard_map/ppermute | solution.py:294
  2.7 9.6 %collective-permute-start.1 = (bf16[1,2,128,256]{3,2,1,0:T(8,128)(2,1)S(1)}, bf16[1,2,128,256]{3,2,1,0:T(8,128)(2,1)S(1)}, u32[]{:S(2)}, u32[]{:S(2)}) collective-permute-start(bf16[1,2,128,256]{3,2,1,0:T(8,128)(2,1)S(1)} %get-tuple-element.61), channel_id=1, source_target_pairs={{0,1},{1,0},{2,3},{3,2},{4,5},{5,4},{6,7},{7,6},{8,9},{9,8},{10,11... | collective-permute-start | bytes 393224 | tf_op jit(solution)/shard_map/ppermute | solution.py:294
  2.8 11.2 %collective-permute-start.3 = (bf16[2,1,128,256]{3,2,1,0:T(8,128)(2,1)S(1)}, bf16[2,1,128,256]{3,2,1,0:T(8,128)(2,1)S(1)}, u32[]{:S(2)}, u32[]{:S(2)}) collective-permute-start(bf16[2,1,128,256]{3,2,1,0:T(8,128)(2,1)S(1)} %get-tuple-element.59.refs_3_), channel_id=1, source_target_pairs={{0,2},{2,0},{4,6},{6,4},{8,10},{10,8},{12,14},{14,12},{1,3},{3,1},... | collective-permute-start | bytes 393224 | tf_op jit(solution)/shard_map/ppermute | solution.py:353
  5.7 8.3 %collective-permute-start.4 = (bf16[2,1,128,256]{3,2,1,0:T(8,128)(2,1)S(1)}, bf16[2,1,128,256]{3,2,1,0:T(8,128)(2,1)S(1)}, u32[]{:S(2)}, u32[]{:S(2)}) collective-permute-start(bf16[2,1,128,256]{3,2,1,0:T(8,128)(2,1)S(1)} %get-tuple-element.60.refs_4_), channel_id=1, source_target_pairs={{0,14},{2,4},{4,2},{6,8},{8,6},{10,12},{12,10},{14,0},{1,15},{3,5}... | collective-permute-start | bytes 393224 | tf_op jit(solution)/shard_map/ppermute | solution.py:354
  14.6 6.6 %collective-permute-start.2 = (bf16[1,2,128,256]{3,2,1,0:T(8,128)(2,1)S(1)}, bf16[1,2,128,256]{3,2,1,0:T(8,128)(2,1)S(1)}, u32[]{:S(2)}, u32[]{:S(2)}) collective-permute-start(bf16[1,2,128,256]{3,2,1,0:T(8,128)(2,1)S(1)} %get-tuple-element.64), channel_id=1, source_target_pairs={{0,1},{1,0},{2,3},{3,2},{4,5},{5,4},{6,7},{7,6},{8,9},{9,8},{10,11... | collective-permute-start | bytes 393224 | tf_op jit(solution)/shard_map/ppermute | solution.py:294
  17.2 3.9 %collective-permute-start.7 = (bf16[1,2,128,256]{3,2,1,0:T(8,128)(2,1)S(1)}, bf16[1,2,128,256]{3,2,1,0:T(8,128)(2,1)S(1)}, u32[]{:S(2)}, u32[]{:S(2)}) collective-permute-start(bf16[1,2,128,256]{3,2,1,0:T(8,128)(2,1)S(1)} %get-tuple-element.70), channel_id=1, source_target_pairs={{0,1},{1,0},{2,3},{3,2},{4,5},{5,4},{6,7},{7,6},{8,9},{9,8},{10,11... | collective-permute-start | bytes 393224 | tf_op jit(solution)/shard_map/ppermute | solution.py:294
  17.6 8.4 %collective-permute-start.9 = (bf16[2,1,128,256]{3,2,1,0:T(8,128)(2,1)S(1)}, bf16[2,1,128,256]{3,2,1,0:T(8,128)(2,1)S(1)}, u32[]{:S(2)}, u32[]{:S(2)}) collective-permute-start(bf16[2,1,128,256]{3,2,1,0:T(8,128)(2,1)S(1)} %get-tuple-element.68.refs_4_), channel_id=1, source_target_pairs={{0,2},{2,0},{4,6},{6,4},{8,10},{10,8},{12,14},{14,12},{1,3},{3,1},... | collective-permute-start | bytes 393224 | tf_op jit(solution)/shard_map/ppermute | solution.py:353
  17.6 8.4 %collective-permute-start.10 = (bf16[2,1,128,256]{3,2,1,0:T(8,128)(2,1)S(1)}, bf16[2,1,128,256]{3,2,1,0:T(8,128)(2,1)S(1)}, u32[]{:S(2)}, u32[]{:S(2)}) collective-permute-start(bf16[2,1,128,256]{3,2,1,0:T(8,128)(2,1)S(1)} %get-tuple-element.69.refs_5_), channel_id=1, source_target_pairs={{0,14},{2,4},{4,2},{6,8},{8,6},{10,12},{12,10},{14,0},{1,15},{3,5}... | collective-permute-start | bytes 393224 | tf_op jit(solution)/shard_map/ppermute | solution.py:354
  29.2 3.9 %collective-permute-start.13 = (bf16[1,2,128,256]{3,2,1,0:T(8,128)(2,1)S(1)}, bf16[1,2,128,256]{3,2,1,0:T(8,128)(2,1)S(1)}, u32[]{:S(2)}, u32[]{:S(2)}) collective-permute-start(bf16[1,2,128,256]{3,2,1,0:T(8,128)(2,1)S(1)} %get-tuple-element.79), channel_id=1, source_target_pairs={{0,1},{1,0},{2,3},{3,2},{4,5},{5,4},{6,7},{7,6},{8,9},{9,8},{10,11... | collective-permute-start | bytes 393224 | tf_op jit(solution)/shard_map/ppermute | solution.py:294
  29.6 8.4 %collective-permute-start.15 = (bf16[2,1,128,256]{3,2,1,0:T(8,128)(2,1)S(1)}, bf16[2,1,128,256]{3,2,1,0:T(8,128)(2,1)S(1)}, u32[]{:S(2)}, u32[]{:S(2)}) collective-permute-start(bf16[2,1,128,256]{3,2,1,0:T(8,128)(2,1)S(1)} %get-tuple-element.77.refs_5_), channel_id=1, source_target_pairs={{0,2},{2,0},{4,6},{6,4},{8,10},{10,8},{12,14},{14,12},{1,3},{3,1},... | collective-permute-start | bytes 393224 | tf_op jit(solution)/shard_map/ppermute | solution.py:353
  29.9 8.1 %collective-permute-start.16 = (bf16[2,1,128,256]{3,2,1,0:T(8,128)(2,1)S(1)}, bf16[2,1,128,256]{3,2,1,0:T(8,128)(2,1)S(1)}, u32[]{:S(2)}, u32[]{:S(2)}) collective-permute-start(bf16[2,1,128,256]{3,2,1,0:T(8,128)(2,1)S(1)} %get-tuple-element.78.refs_6_), channel_id=1, source_target_pairs={{0,14},{2,4},{4,2},{6,8},{8,6},{10,12},{12,10},{14,0},{1,15},{3,5}... | collective-permute-start | bytes 393224 | tf_op jit(solution)/shard_map/ppermute | solution.py:354
  41.3 3.9 %collective-permute-start.19 = (bf16[1,2,128,256]{3,2,1,0:T(8,128)(2,1)S(1)}, bf16[1,2,128,256]{3,2,1,0:T(8,128)(2,1)S(1)}, u32[]{:S(2)}, u32[]{:S(2)}) collective-permute-start(bf16[1,2,128,256]{3,2,1,0:T(8,128)(2,1)S(1)} %get-tuple-element.89), channel_id=1, source_target_pairs={{0,1},{1,0},{2,3},{3,2},{4,5},{5,4},{6,7},{7,6},{8,9},{9,8},{10,11... | collective-permute-start | bytes 393224 | tf_op jit(solution)/shard_map/ppermute | solution.py:294
  41.7 7.4 %collective-permute-start.20 = (bf16[2,1,128,256]{3,2,1,0:T(8,128)(2,1)S(1)}, bf16[2,1,128,256]{3,2,1,0:T(8,128)(2,1)S(1)}, u32[]{:S(2)}, u32[]{:S(2)}) collective-permute-start(bf16[2,1,128,256]{3,2,1,0:T(8,128)(2,1)S(1)} %get-tuple-element.87.refs_4_), channel_id=1, source_target_pairs={{0,2},{2,0},{4,6},{6,4},{8,10},{10,8},{12,14},{14,12},{1,3},{3,1},... | collective-permute-start | bytes 393224 | tf_op jit(solution)/shard_map/ppermute | solution.py:353
  41.9 8.1 %collective-permute-start.21 = (bf16[2,1,128,256]{3,2,1,0:T(8,128)(2,1)S(1)}, bf16[2,1,128,256]{3,2,1,0:T(8,128)(2,1)S(1)}, u32[]{:S(2)}, u32[]{:S(2)}) collective-permute-start(bf16[2,1,128,256]{3,2,1,0:T(8,128)(2,1)S(1)} %get-tuple-element.88.refs_5_), channel_id=1, source_target_pairs={{0,14},{2,4},{4,2},{6,8},{8,6},{10,12},{12,10},{14,0},{1,15},{3,5}... | collective-permute-start | bytes 393224 | tf_op jit(solution)/shard_map/ppermute | solution.py:354
  46.8 10.0 %collective-permute-start.25 = (bf16[2,2,128,256]{3,2,1,0:T(8,128)(2,1)S(1)}, bf16[2,2,128,256]{3,2,1,0:T(8,128)(2,1)S(1)}, u32[]{:S(2)}, u32[]{:S(2)}) collective-permute-start(bf16[2,2,128,256]{3,2,1,0:T(8,128)(2,1)S(1)} %get-tuple-element.93), channel_id=1, source_target_pairs={{0,2},{2,0},{4,6},{6,4},{8,10},{10,8},{12,14},{14,12},{1,3},{3,1},... | collective-permute-start | bytes 786440 | tf_op jit(solution)/shard_map/ppermute | solution.py:437
  46.9 14.4 %collective-permute-start.24 = (bf16[2,2,128,256]{3,2,1,0:T(8,128)(2,1)S(1)}, bf16[2,2,128,256]{3,2,1,0:T(8,128)(2,1)S(1)}, u32[]{:S(2)}, u32[]{:S(2)}) collective-permute-start(bf16[2,2,128,256]{3,2,1,0:T(8,128)(2,1)S(1)} %get-tuple-element.93), channel_id=1, source_target_pairs={{0,8},{2,10},{4,12},{6,14},{8,0},{10,2},{12,4},{14,6},{1,9},{3,11}... | collective-permute-start | bytes 786440 | tf_op jit(solution)/shard_map/ppermute | solution.py:389
  61.3 8.1 %collective-permute-start.26 = (bf16[2,2,128,256]{3,2,1,0:T(8,128)(2,1)S(1)}, bf16[2,2,128,256]{3,2,1,0:T(8,128)(2,1)S(1)}, u32[]{:S(2)}, u32[]{:S(2)}) collective-permute-start(bf16[2,2,128,256]{3,2,1,0:T(8,128)(2,1)S(1)} %collective-permute-done.24.refs_0_), channel_id=1, source_target_pairs={{0,2},{2,0},{4,6},{6,4},{8,10},{10,8},{12,14},{14,12},{1,3},{3,1},... | collective-permute-start | bytes 786440 | tf_op jit(solution)/shard_map/ppermute | solution.py:438
  62.4 9.6 %collective-permute-start.27 = (bf16[2,1,128,256]{3,2,1,0:T(8,128)(2,1)S(1)}, bf16[2,1,128,256]{3,2,1,0:T(8,128)(2,1)S(1)}, u32[]{:S(2)}, u32[]{:S(2)}) collective-permute-start(bf16[2,1,128,256]{3,2,1,0:T(8,128)(2,1)S(1)} %get-tuple-element.99.first_ref), channel_id=1, source_target_pairs={{0,8},{2,10},{4,12},{6,14},{8,0},{10,2},{12,4},{14,6},{1,9},{3,11}... | collective-permute-start | bytes 393224 | tf_op jit(solution)/shard_map/ppermute | solution.py:439
  69.4 6.9 %collective-permute-start.28 = (bf16[2,1,128,256]{3,2,1,0:T(8,128)(2,1)S(1)}, bf16[2,1,128,256]{3,2,1,0:T(8,128)(2,1)S(1)}, u32[]{:S(2)}, u32[]{:S(2)}) collective-permute-start(bf16[2,1,128,256]{3,2,1,0:T(8,128)(2,1)S(1)} %get-tuple-element.101.first_ref), channel_id=1, source_target_pairs={{0,8},{2,10},{4,12},{6,14},{8,0},{10,2},{12,4},{14,6},{1,9},{3,11}... | collective-permute-start | bytes 393224 | tf_op jit(solution)/shard_map/ppermute | solution.py:440
  69.5 15.2 %collective-permute-start.30 = (bf16[2,2,128,256]{3,2,1,0:T(8,128)(2,1)S(1)}, bf16[2,2,128,256]{3,2,1,0:T(8,128)(2,1)S(1)}, u32[]{:S(2)}, u32[]{:S(2)}) collective-permute-start(bf16[2,2,128,256]{3,2,1,0:T(8,128)(2,1)S(1)} %pick.3), channel_id=1, source_target_pairs={{0,4},{2,6},{4,0},{6,2},{8,12},{10,14},{12,8},{14,10},{1,5},{3,7},... | collective-permute-start | bytes 786440 | tf_op jit(solution)/shard_map/ppermute | solution.py:441
  72.1 12.7 %collective-permute-start.31 = (bf16[2,1,128,256]{3,2,1,0:T(8,128)(2,1)S(1)}, bf16[2,1,128,256]{3,2,1,0:T(8,128)(2,1)S(1)}, u32[]{:S(2)}, u32[]{:S(2)}) collective-permute-start(bf16[2,1,128,256]{3,2,1,0:T(8,128)(2,1)S(1)} %get-tuple-element.102), channel_id=1, source_target_pairs={{0,2},{2,4},{4,6},{6,0},{8,10},{10,12},{12,14},{14,8},{1,3},{3,5},... | collective-permute-start | bytes 393224 | tf_op jit(solution)/shard_map/ppermute | solution.py:445
  72.4 12.3 %collective-permute-start.32 = (bf16[2,1,128,256]{3,2,1,0:T(8,128)(2,1)S(1)}, bf16[2,1,128,256]{3,2,1,0:T(8,128)(2,1)S(1)}, u32[]{:S(2)}, u32[]{:S(2)}) collective-permute-start(bf16[2,1,128,256]{3,2,1,0:T(8,128)(2,1)S(1)} %get-tuple-element.103), channel_id=1, source_target_pairs={{0,6},{2,0},{4,2},{6,4},{8,14},{10,8},{12,10},{14,12},{1,7},{3,1},... | collective-permute-start | bytes 393224 | tf_op jit(solution)/shard_map/ppermute | solution.py:445
  76.4 9.8 %collective-permute-start.33 = (bf16[2,1,128,256]{3,2,1,0:T(8,128)(2,1)S(1)}, bf16[2,1,128,256]{3,2,1,0:T(8,128)(2,1)S(1)}, u32[]{:S(2)}, u32[]{:S(2)}) collective-permute-start(bf16[2,1,128,256]{3,2,1,0:T(8,128)(2,1)S(1)} %get-tuple-element.104), channel_id=1, source_target_pairs={{0,2},{2,4},{4,6},{6,0},{8,10},{10,12},{12,14},{14,8},{1,3},{3,5},... | collective-permute-start | bytes 393224 | tf_op jit(solution)/shard_map/ppermute | solution.py:445
  77.5 9.8 %collective-permute-start.34 = (bf16[2,1,128,256]{3,2,1,0:T(8,128)(2,1)S(1)}, bf16[2,1,128,256]{3,2,1,0:T(8,128)(2,1)S(1)}, u32[]{:S(2)}, u32[]{:S(2)}) collective-permute-start(bf16[2,1,128,256]{3,2,1,0:T(8,128)(2,1)S(1)} %get-tuple-element.105), channel_id=1, source_target_pairs={{0,6},{2,0},{4,2},{6,4},{8,14},{10,8},{12,10},{14,12},{1,7},{3,1},... | collective-permute-start | bytes 393224 | tf_op jit(solution)/shard_map/ppermute | solution.py:445
  (15 other events, 28.6 us)
